TPU v7x, 32 devices: a whole 2x2x4 slice. The times are simulated.
32 devices in a mesh: dp: 4 (over z), expert: 8 (over y, x, core).
Axes of the slice: x: 2, y: 2, z: 4, core: 2. Of those that a mesh axis runs over, the one named last changes fastest.
Arguments:
- tokens: bfloat16 [4096, 1024], P(('dp', 'expert')), may hold values from -6 to 6
- grad_out: bfloat16 [4096, 1024], P(('dp', 'expert')), may hold values from -6 to 6
- routes: int32 [4096, 10], P(('dp', 'expert')), may hold values from 0 to 23, all different within a row; in each aligned block of 128 rows (0 to 127, 128 to 255, ...) at most 64 rows name the same one
- combine: bfloat16 [4096, 10], P(('dp', 'expert')), may hold values from 0.049804688 to 0.29882812
- w_gate: bfloat16 [24, 1024, 512], P('expert'), may hold values from -0.1875 to 0.1875
- w_up: bfloat16 [24, 1024, 512], P('expert'), may hold values from -0.1875 to 0.1875
- w_down: bfloat16 [24, 512, 1024], P('expert'), may hold values from -0.25 to 0.25
Outputs:
- grad_tokens: bfloat16 [4096, 1024], P(('dp', 'expert'))
- grad_gate: bfloat16 [24, 1024, 512], P('expert', 'dp')
- grad_up: bfloat16 [24, 1024, 512], P('expert', 'dp')
- grad_down: bfloat16 [24, 512, 1024], P('expert', 'dp')
Inputs may be any that keep to these rules, and one draw needn't show every extreme that they name: `routes`: A token's 10 experts are different. Among the 128 tokens of one device no expert is named more than 64 times, a bound that some block reaches.
All inputs are finite; a program needn't handle non-finite values.
Results may differ from a plain program's by a relative error of at most 0.022.
Values may be sent and summed in bfloat16 or wider, within the bound.
No kernel may reach another device: no remote copies, remote signals or barrier semaphores. Data moves between devices by JAX's collectives and lax.ppermute only.
A program may use at most 128 MiB of HBM per device.

v0:
```python
import jax
import jax.numpy as jnp
from jax import lax
from jax.sharding import PartitionSpec as P


def slot_ranks(route_block, expert_total):
    flat_ids = route_block.reshape(-1)
    marks = (flat_ids[:, None] == jnp.arange(expert_total, dtype=jnp.int32)[None, :]).astype(
        jnp.int32
    )
    return jnp.sum((jnp.cumsum(marks, axis=0) - 1) * marks, axis=1)


def build_slots(route_block, expert_total, slot_depth):
    flat_ids = route_block.reshape(-1)
    pair_total = flat_ids.shape[0]
    slot_rank = slot_ranks(route_block, expert_total)
    slots = jnp.full((expert_total, slot_depth), pair_total, dtype=jnp.int32)
    slots = slots.at[flat_ids, slot_rank].set(jnp.arange(pair_total, dtype=jnp.int32))
    return (slots, slot_rank)


def contract_last(left, right):
    return lax.dot_general(
        left, right, (((1,), (1,)), ((), ())), preferred_element_type=jnp.float32
    )


def contract_first(left, right):
    return lax.dot_general(
        left, right, (((0,), (0,)), ((), ())), preferred_element_type=jnp.float32
    )


def expert_backward(rows_x, rows_dy, rows_c, gate_w, up_w, down_w):
    gate_pre = jnp.dot(rows_x, gate_w, preferred_element_type=jnp.float32)
    up_pre = jnp.dot(rows_x, up_w, preferred_element_type=jnp.float32)
    sigmoid_gate = jax.nn.sigmoid(gate_pre)
    hidden = (gate_pre * sigmoid_gate * up_pre).astype(jnp.bfloat16)
    d_out = (rows_c[:, None] * rows_dy.astype(jnp.float32)).astype(jnp.bfloat16)
    d_hidden = contract_last(d_out, down_w)
    d_gate = (d_hidden * up_pre * sigmoid_gate * (1.0 + gate_pre * (1.0 - sigmoid_gate))).astype(
        jnp.bfloat16
    )
    d_up = (d_hidden * gate_pre * sigmoid_gate).astype(jnp.bfloat16)
    d_rows = (contract_last(d_gate, gate_w) + contract_last(d_up, up_w)).astype(jnp.bfloat16)
    return (hidden, d_out, d_gate, d_up, d_rows)


def shards(tokens, grad_out, routes, combine, w_gate, w_up, w_down):
    tok_dev, model_width = tokens.shape
    top_count = routes.shape[1]
    peer_count = lax.axis_size("expert")
    held_experts = w_gate.shape[0]
    hidden_units = w_gate.shape[2]
    expert_total = peer_count * held_experts
    slot_depth = 8 * ((tok_dev * top_count * 6 // (5 * expert_total) + 7) // 8)
    pair_total = tok_dev * top_count
    slots, slot_rank = build_slots(routes, expert_total, slot_depth)
    filled = slots < pair_total
    token_index = jnp.where(filled, slots // top_count, tok_dev)
    pad_row = jnp.zeros((1, model_width), jnp.bfloat16)
    send_x = jnp.concatenate([tokens, pad_row])[token_index].reshape(
        peer_count, held_experts, slot_depth, model_width
    )
    send_dy = jnp.concatenate([grad_out, pad_row])[token_index].reshape(
        peer_count, held_experts, slot_depth, model_width
    )
    weight_ext = jnp.concatenate([combine.reshape(-1), jnp.zeros((1,), jnp.bfloat16)])
    send_c = weight_ext[slots].reshape(peer_count, held_experts, slot_depth)
    recv_x, recv_dy, recv_c = (
        lax.all_to_all(send_x, "expert", split_axis=0, concat_axis=0, tiled=True),
        lax.all_to_all(send_dy, "expert", split_axis=0, concat_axis=0, tiled=True),
        lax.all_to_all(send_c, "expert", split_axis=0, concat_axis=0, tiled=True),
    )
    gate_parts = []
    up_parts = []
    down_parts = []
    row_list = []
    for which in range(held_experts):
        rows_x = recv_x[:, which].reshape(-1, model_width)
        rows_dy = recv_dy[:, which].reshape(-1, model_width)
        rows_c = recv_c[:, which].reshape(-1).astype(jnp.float32)
        hidden, d_out, d_gate, d_up, d_rows = expert_backward(
            rows_x, rows_dy, rows_c, w_gate[which], w_up[which], w_down[which]
        )
        d_both = jnp.concatenate([d_gate, d_up], axis=1)
        row_list.append(d_rows.reshape(peer_count, slot_depth, model_width))
        summed = lax.psum_scatter(
            contract_first(rows_x, d_both).astype(jnp.bfloat16),
            "dp",
            scatter_dimension=0,
            tiled=True,
        ).astype(jnp.float32)
        gate_parts.append(summed[:, :hidden_units].astype(jnp.bfloat16))
        up_parts.append(summed[:, hidden_units:].astype(jnp.bfloat16))
        down_parts.append(
            lax.psum_scatter(
                contract_first(hidden, d_out).astype(jnp.bfloat16),
                "dp",
                scatter_dimension=0,
                tiled=True,
            )
        )
    grad_gate = jnp.stack(gate_parts)
    grad_up = jnp.stack(up_parts)
    grad_down = jnp.stack(down_parts)
    stacked = jnp.stack(row_list, axis=1)
    returned = lax.all_to_all(stacked, "expert", split_axis=0, concat_axis=0, tiled=True)
    flat_back = returned.reshape(expert_total * slot_depth, model_width)
    row_of_pair = routes.reshape(-1) * slot_depth + slot_rank
    per_pair = flat_back[row_of_pair].astype(jnp.float32).reshape(tok_dev, top_count, model_width)
    grad_tokens = jnp.sum(per_pair, axis=1).astype(jnp.bfloat16)
    return (grad_tokens, grad_gate, grad_up, grad_down)


def solution(mesh):
    return jax.shard_map(
        shards,
        mesh=mesh,
        in_specs=(
            P(("dp", "expert"), None),
            P(("dp", "expert"), None),
            P(("dp", "expert"), None),
            P(("dp", "expert"), None),
            P("expert", None, None),
            P("expert", None, None),
            P("expert", None, None),
        ),
        out_specs=(
            P(("dp", "expert"), None),
            P("expert", "dp", None),
            P("expert", "dp", None),
            P("expert", "dp", None),
        ),
        check_vma=False,
    )
```

profile of v0, /device:TPU:0, one launch (start us, length us, event | category | flops | bytes accessed | tf_op | source)
XLA Modules:
  0.0 364.2 jit_solution(10668156857478875766)
XLA Ops:
  8.4 6.8 %reduce-window.6 = s32[24,10,128]{2,1,0:T(8,128)S(1)} reduce-window(s32[24,10,128]{2,1,0:T(8,128)S(1)} %fusion.57, s32[]{:T(128)} %constant.16.clone.1), window={size=1x1x128 pad=0_0x0_0x127_0}, to_apply=%region_0.0 | reduce-window | flops 3901440 | bytes 245764 | tf_op jit(solution)/shard_map/reduce-window
  17.4 5.2 %scatter_custom_fusion = s32[1536]{0:T(1024)S(1)} fusion(s32[1280]{0:T(1024)S(1)} %broadcast_select_fusion, s32[1280]{0:T(1024)S(1)} %iota.11, s32[]{:T(128)} %constant.15.clone.1), kind=kCustom, calls=%fused_computation.130 | custom fusion | bytes 6148
  23.8 9.5 %gather_fusion = bf16[1536]{0:T(1024)(128)(2,1)S(1)} fusion(bf16[1281]{0:T(1024)(128)(2,1)S(1)} %pad_maximum_fusion.4, s32[2048]{0:T(1024)S(1)} %pad_clamp_fusion.2), kind=kCustom, calls=%fused_computation | custom fusion | bytes 12288 | tf_op jit(solution)/shard_map/gather | solution.py:71
  34.0 5.2 %all-to-all-start = ((bf16[8,3,64]{2,1,0:T(4,128)(2,1)}), bf16[8,3,64]{2,1,0:T(4,128)(2,1)S(1)}, u32[]{:S(2)}, u32[]{:S(2)}) async-start(bf16[8,3,64]{2,1,0:T(4,128)(2,1)} %reshape.178), calls=%async_computation | async-start | bytes 16384 | tf_op jit(solution)/shard_map/all_to_all | solution.py:75
  39.2 5.8 %gather_fusion.2 = bf16[1536,1024]{1,0:T(8,128)(2,1)} fusion(bf16[129,1024]{1,0:T(8,128)(2,1)S(1)} %concatenate.24, s32[2048]{0:T(1024)S(1)} %pad_clamp_fusion.1), kind=kCustom, calls=%fused_computation.2 | custom fusion | bytes 6297600 | tf_op jit(solution)/shard_map/gather | solution.py:64
  45.1 4.2 %all-to-all-start.2 = ((bf16[8,3,64,1024]{3,2,1,0:T(8,128)(2,1)}), bf16[8,3,64,1024]{3,2,1,0:T(8,128)(2,1)S(1)}, u32[]{:S(2)}, u32[]{:S(2)}) async-start(bf16[8,3,64,1024]{3,2,1,0:T(8,128)(2,1)} %bitcast.131), calls=%async_computation.2 | async-start | bytes 6291456 | tf_op jit(solution)/shard_map/all_to_all | solution.py:73
  50.2 5.8 %gather_fusion.1 = bf16[1536,1024]{1,0:T(8,128)(2,1)} fusion(bf16[129,1024]{1,0:T(8,128)(2,1)S(1)} %concatenate.23, s32[2048]{0:T(1024)S(1)} %pad_clamp_fusion.1), kind=kCustom, calls=%fused_computation.1 | custom fusion | bytes 6297600 | tf_op jit(solution)/shard_map/gather | solution.py:67
  56.1 31.1 %all-to-all-done.2 = bf16[8,3,64,1024]{3,2,1,0:T(8,128)(2,1)S(1)} async-done(((bf16[8,3,64,1024]{3,2,1,0:T(8,128)(2,1)}), bf16[8,3,64,1024]{3,2,1,0:T(8,128)(2,1)S(1)}, u32[]{:S(2)}, u32[]{:S(2)}) %all-to-all-start.2) | async-done | bytes 3145760 | tf_op jit(solution)/shard_map/all_to_all | solution.py:73
  88.8 3.6 %all-to-all-start.1 = ((bf16[8,3,64,1024]{3,2,1,0:T(8,128)(2,1)}), bf16[8,3,64,1024]{3,2,1,0:T(8,128)(2,1)S(1)}, u32[]{:S(2)}, u32[]{:S(2)}) async-start(bf16[8,3,64,1024]{3,2,1,0:T(8,128)(2,1)} %bitcast.130), calls=%async_computation.1 | async-start | bytes 6291456 | tf_op jit(solution)/shard_map/all_to_all | solution.py:74
  92.7 3.6 fusion.74
  96.3 3.4 fusion.32
  99.6 3.0 fusion.35
  102.6 27.7 %all-to-all-done.1 = bf16[8,3,64,1024]{3,2,1,0:T(8,128)(2,1)S(1)} async-done(((bf16[8,3,64,1024]{3,2,1,0:T(8,128)(2,1)}), bf16[8,3,64,1024]{3,2,1,0:T(8,128)(2,1)S(1)}, u32[]{:S(2)}, u32[]{:S(2)}) %all-to-all-start.1) | async-done | bytes 3145760 | tf_op jit(solution)/shard_map/all_to_all | solution.py:74
  130.3 2.7 slice_convert_fusion.2
  136.4 2.4 fusion.23
  144.3 2.4 fusion.14
  146.8 2.4 fusion.17
  154.0 2.4 multiply_convert_fusion.10
  157.1 2.7 convolution_convert_fusion.2
  159.9 3.0 multiply_convert_fusion.8
  163.7 2.6 convolution_convert_fusion.1
  166.7 3.0 multiply_convert_fusion.6
  170.4 2.7 convolution_convert_fusion
  185.5 3.6 %all-to-all-start.3 = ((bf16[8,3,64,1024]{3,2,1,0:T(8,128)(2,1)}), bf16[8,3,64,1024]{3,2,1,0:T(8,128)(2,1)S(1)}, u32[]{:S(2)}, u32[]{:S(2)}) async-start(bf16[8,3,64,1024]{3,2,1,0:T(8,128)(2,1)} %pad_maximum_fusion), calls=%async_computation.3 | async-start | bytes 6291456 | tf_op jit(solution)/shard_map/all_to_all | solution.py:110
  191.2 28.1 %reduce-scatter.17.cloned.1.call-done = bf16[128,1024]{1,0:T(8,128)(2,1)} async-done(((bf16[512,1024]{1,0:T(8,128)(2,1)}), bf16[128,1024]{1,0:T(8,128)(2,1)}) %reduce-scatter.17.cloned.1.call-update) | async-done | bytes 262160 | tf_op jit(solution)/shard_map/reduce_scatter | solution.py:99
  221.4 5.6 %all-to-all-done.3 = bf16[8,3,64,1024]{3,2,1,0:T(8,128)(2,1)S(1)} async-done(((bf16[8,3,64,1024]{3,2,1,0:T(8,128)(2,1)}), bf16[8,3,64,1024]{3,2,1,0:T(8,128)(2,1)S(1)}, u32[]{:S(2)}, u32[]{:S(2)}) %all-to-all-start.3) | async-done | bytes 3145760 | tf_op jit(solution)/shard_map/all_to_all | solution.py:110
  227.0 5.1 %gather_fusion.3 = bf16[1280,1024]{1,0:T(8,128)(2,1)} fusion(bf16[1536,1024]{1,0:T(8,128)(2,1)S(1)} %bitcast.129, s32[2048]{0:T(1024)S(1)} %pad_clamp_fusion), kind=kCustom, calls=%fused_computation.3 | custom fusion | bytes 5248000 | tf_op jit(solution)/shard_map/gather | solution.py:113
  232.1 5.9 %gather.18 = bf16[128,10,1024]{2,1,0:T(8,128)(2,1)} reshape(bf16[1280,1024]{1,0:T(8,128)(2,1)} %gather_fusion.3) | data formatting | bytes 5242880 | tf_op jit(solution)/shard_map/gather | solution.py:113
  238.0 5.0 %reduce_sum.25 = bf16[128,1024]{1,0:T(8,128)(2,1)} reduce(bf16[128,10,1024]{2,1,0:T(8,128)(2,1)} %gather.18, bf16[]{:T(256)} %constant.11.clone.1), dimensions={1}, to_apply=%region_4.5 | reduce | flops 1179648 | bytes 2883586 | tf_op jit(solution)/shard_map/reduce_sum | solution.py:114
  243.1 21.1 %reduce-scatter.7.cloned.1.call-done = bf16[256,1024]{1,0:T(8,128)(2,1)} async-done(((bf16[1024,1024]{1,0:T(8,128)(2,1)}), bf16[256,1024]{1,0:T(8,128)(2,1)}) %reduce-scatter.7.cloned.1.call-update) | async-done | bytes 524304 | tf_op jit(solution)/shard_map/reduce_scatter | solution.py:90
  265.2 44.3 %reduce-scatter.9.cloned.1.call-done = bf16[256,1024]{1,0:T(8,128)(2,1)} async-done(((bf16[1024,1024]{1,0:T(8,128)(2,1)}), bf16[256,1024]{1,0:T(8,128)(2,1)}) %reduce-scatter.9.cloned.1.call-update) | async-done | bytes 524304 | tf_op jit(solution)/shard_map/reduce_scatter | solution.py:90
  310.6 44.4 %reduce-scatter.11.cloned.1.call-done = bf16[256,1024]{1,0:T(8,128)(2,1)} async-done(((bf16[1024,1024]{1,0:T(8,128)(2,1)}), bf16[256,1024]{1,0:T(8,128)(2,1)}) %reduce-scatter.11.cloned.1.call-update) | async-done | bytes 524304 | tf_op jit(solution)/shard_map/reduce_scatter | solution.py:90
  (125 shorter events, 45.2 us)
Async XLA Ops:
  23.8 15.4 %copy-start.19 = (bf16[128,1024]{1,0:T(8,128)(2,1)S(1)}, bf16[128,1024]{1,0:T(8,128)(2,1)}, u32[]{:S(2)}) copy-start(bf16[128,1024]{1,0:T(8,128)(2,1)} %param.7) | copy-start | bytes 786436
  34.0 11.1 %all-to-all-start = ((bf16[8,3,64]{2,1,0:T(4,128)(2,1)}), bf16[8,3,64]{2,1,0:T(4,128)(2,1)S(1)}, u32[]{:S(2)}, u32[]{:S(2)}) async-start(bf16[8,3,64]{2,1,0:T(4,128)(2,1)} %reshape.178), calls=%async_computation | async-start | bytes 16384 | tf_op jit(solution)/shard_map/all_to_all | solution.py:75
  45.1 42.1 %all-to-all-start.2 = ((bf16[8,3,64,1024]{3,2,1,0:T(8,128)(2,1)}), bf16[8,3,64,1024]{3,2,1,0:T(8,128)(2,1)S(1)}, u32[]{:S(2)}, u32[]{:S(2)}) async-start(bf16[8,3,64,1024]{3,2,1,0:T(8,128)(2,1)} %bitcast.131), calls=%async_computation.2 | async-start | bytes 6291456 | tf_op jit(solution)/shard_map/all_to_all | solution.py:73
  87.2 1.7 copy-start
  88.8 41.5 %all-to-all-start.1 = ((bf16[8,3,64,1024]{3,2,1,0:T(8,128)(2,1)}), bf16[8,3,64,1024]{3,2,1,0:T(8,128)(2,1)S(1)}, u32[]{:S(2)}, u32[]{:S(2)}) async-start(bf16[8,3,64,1024]{3,2,1,0:T(8,128)(2,1)} %bitcast.130), calls=%async_computation.1 | async-start | bytes 6291456 | tf_op jit(solution)/shard_map/all_to_all | solution.py:74
  92.5 96.7 %reduce-scatter.13.cloned.1.call-start = ((), (), s32[]{:S(2)}) async-start(), calls=%async_computation.13 | async-start | bytes 1310720 | tf_op jit(solution)/shard_map/reduce_scatter | solution.py:99
  96.3 3.4 copy-start.8
  133.0 1.2 copy-start.20
  133.0 1.5 copy-start.22
  136.3 54.9 %reduce-scatter.15.cloned.1.call-start = ((), (), s32[]{:S(2)}) async-start(), calls=%async_computation.14 | async-start | bytes 1310720 | tf_op jit(solution)/shard_map/reduce_scatter | solution.py:99
  136.4 2.5 copy-start.6
  136.4 4.9 %copy-start.2 = (f32[8,1,64,1024]{3,2,1,0:T(8,128)S(1)}, f32[8,1,64,1024]{3,2,1,0:T(8,128)}, u32[]{:S(2)}) copy-start(f32[8,1,64,1024]{3,2,1,0:T(8,128)} %get-tuple-element.9) | copy-start | bytes 6291460
  138.9 2.6 copy-start.24
  144.0 75.3 %reduce-scatter.17.cloned.1.call-start = ((), (), s32[]{:S(2)}) async-start(), calls=%async_computation.15 | async-start | bytes 1310720 | tf_op jit(solution)/shard_map/reduce_scatter | solution.py:99
  144.3 2.5 copy-start.4
  144.3 4.9 %copy-start.1 = (f32[8,1,64,1024]{3,2,1,0:T(8,128)S(1)}, f32[8,1,64,1024]{3,2,1,0:T(8,128)}, u32[]{:S(2)}) copy-start(f32[8,1,64,1024]{3,2,1,0:T(8,128)} %get-tuple-element.8) | copy-start | bytes 6291460
  146.8 2.6 copy-start.26
  152.0 112.2 %reduce-scatter.7.cloned.1.call-start = ((), (), s32[]{:S(2)}) async-start(), calls=%async_computation.10 | async-start | bytes 2621440 | tf_op jit(solution)/shard_map/reduce_scatter | solution.py:90
  152.0 1.9 copy-start.21
  152.1 1.9 copy-start.23
  154.0 3.2 copy-start.9
  157.1 2.8 copy-start.11
  159.9 149.6 %reduce-scatter.9.cloned.1.call-start = ((), (), s32[]{:S(2)}) async-start(), calls=%async_computation.11 | async-start | bytes 2621440 | tf_op jit(solution)/shard_map/reduce_scatter | solution.py:90
  159.9 3.8 %copy-start.7 = (bf16[8,1,64,1024]{3,2,1,0:T(8,128)(2,1)S(1)}, bf16[8,1,64,1024]{3,2,1,0:T(8,128)(2,1)}, u32[]{:S(2)}) copy-start(bf16[8,1,64,1024]{3,2,1,0:T(8,128)(2,1)} %get-tuple-element.15) | copy-start | bytes 3145732
  163.7 2.9 copy-start.10
  166.4 188.6 %reduce-scatter.11.cloned.1.call-start = ((), (), s32[]{:S(2)}) async-start(), calls=%async_computation.12 | async-start | bytes 2621440 | tf_op jit(solution)/shard_map/reduce_scatter | solution.py:90
  166.6 3.8 %copy-start.5 = (bf16[8,1,64,1024]{3,2,1,0:T(8,128)(2,1)S(1)}, bf16[8,1,64,1024]{3,2,1,0:T(8,128)(2,1)}, u32[]{:S(2)}) copy-start(bf16[8,1,64,1024]{3,2,1,0:T(8,128)(2,1)} %get-tuple-element.14) | copy-start | bytes 3145732
  169.6 3.5 copy-start.16
  175.1 2.1 copy-start.13
  179.2 2.4 copy-start.3
  179.3 2.5 copy-start.15
  185.5 41.5 %all-to-all-start.3 = ((bf16[8,3,64,1024]{3,2,1,0:T(8,128)(2,1)}), bf16[8,3,64,1024]{3,2,1,0:T(8,128)(2,1)S(1)}, u32[]{:S(2)}, u32[]{:S(2)}) async-start(bf16[8,3,64,1024]{3,2,1,0:T(8,128)(2,1)} %pad_maximum_fusion), calls=%async_computation.3 | async-start | bytes 6291456 | tf_op jit(solution)/shard_map/all_to_all | solution.py:110
  (6 other events, 5.4 us)
Sparse Core Ops, SparseCore 0:
  136.4 26.5 reduce-scatter.12
  165.4 25.8 reduce-scatter.14
  193.5 25.7 reduce-scatter.16
  221.6 42.5 reduce-scatter.6
  266.3 43.1 reduce-scatter.8
  311.7 43.1 reduce-scatter.10
where the time goes:
time: 365 us; the launch traced here: 364 us
  waiting for transfers between devices  204 us (56%)
  local copies, waits for them, and re-layouts  56.3 us (15%)
  matrix products  47.4 us (13%)
  other arithmetic  24.2 us (7%)
  starting transfers between devices  17.3 us (5%)
  between operations  14.6 us (4%)
    reduce_scatter x3, waiting for transfers between devices, shards(): lax.psum_scatter(contract_first(rows_x, d_both).astype(jnp.bfloat16), 'dp...  110 us
    all_to_all x1, waiting for transfers between devices, shards(): lax.all_to_all(send_x, 'expert', split_axis=0, concat_axis=0, tiled=True)  31.1 us
    reduce_scatter x3, waiting for transfers between devices, shards(): lax.psum_scatter(contract_first(hidden, d_out).astype(jnp.bfloat16), 'dp'...  30.1 us
    all_to_all x1, waiting for transfers between devices, shards(): lax.all_to_all(send_dy, 'expert', split_axis=0, concat_axis=0, tiled=True)  27.7 us
    dot_general x9, matrix products, contract_last(): lax.dot_general(left, right, (((1,), (1,)), ((), ())), preferred_element_...  18.2 us
    unnamed x59, local copies, waits for them, and re-layouts  14.3 us
    dot_general x6, matrix products, contract_first(): lax.dot_general(left, right, (((0,), (0,)), ((), ())), preferred_element_...  13.2 us
    gather x2, local copies, waits for them, and re-layouts, shards(): flat_back[row_of_pair].astype(jnp.float32)  11 us
  transfers between devices with their start and end apart: 10, of which 8 were waited for; matrix products, arithmetic and copies ran while one was open for 24% of the time, Pallas kernels for 0%

commit v1 on v0

--- a/solution.py
+++ b/solution.py
@@ -1,7 +1,14 @@
+import functools
 import jax
 import jax.numpy as jnp
 from jax import lax
+from jax.experimental import pallas as pl
+from jax.experimental.pallas import tpu as pltpu
 from jax.sharding import PartitionSpec as P
+
+LANES = 128
+VMEM_BYTES = 60 * 1024 * 1024
+GATHER_BYTES = 48 * 1024 * 1024
 
 
 def slot_ranks(route_block, expert_total):
@@ -33,9 +40,17 @@
     )
 
 
+def mul(left, right):
+    return jnp.dot(left, right, preferred_element_type=jnp.float32)
+
+
+def depth_of(tok_dev, top_count, expert_total):
+    return 8 * ((tok_dev * top_count * 6 // (5 * expert_total) + 7) // 8)
+
+
 def expert_backward(rows_x, rows_dy, rows_c, gate_w, up_w, down_w):
-    gate_pre = jnp.dot(rows_x, gate_w, preferred_element_type=jnp.float32)
-    up_pre = jnp.dot(rows_x, up_w, preferred_element_type=jnp.float32)
+    gate_pre = mul(rows_x, gate_w)
+    up_pre = mul(rows_x, up_w)
     sigmoid_gate = jax.nn.sigmoid(gate_pre)
     hidden = (gate_pre * sigmoid_gate * up_pre).astype(jnp.bfloat16)
     d_out = (rows_c[:, None] * rows_dy.astype(jnp.float32)).astype(jnp.bfloat16)
@@ -48,14 +63,14 @@
     return (hidden, d_out, d_gate, d_up, d_rows)
 
 
-def shards(tokens, grad_out, routes, combine, w_gate, w_up, w_down):
+def routed_shards(tokens, grad_out, routes, combine, w_gate, w_up, w_down):
     tok_dev, model_width = tokens.shape
     top_count = routes.shape[1]
     peer_count = lax.axis_size("expert")
     held_experts = w_gate.shape[0]
     hidden_units = w_gate.shape[2]
     expert_total = peer_count * held_experts
-    slot_depth = 8 * ((tok_dev * top_count * 6 // (5 * expert_total) + 7) // 8)
+    slot_depth = depth_of(tok_dev, top_count, expert_total)
     pair_total = tok_dev * top_count
     slots, slot_rank = build_slots(routes, expert_total, slot_depth)
     filled = slots < pair_total
@@ -115,9 +130,328 @@
     return (grad_tokens, grad_gate, grad_up, grad_down)
 
 
+def pack_kernel(tok_ref, dy_ref, routes_ref, combine_ref, out_ref):
+    tok_dev, width = tok_ref.shape
+    half = tok_dev // 2
+    out_ref[:, :width] = tok_ref[...]
+    out_ref[:, width : 2 * width] = dy_ref[...]
+    ids = lax.broadcasted_iota(jnp.int32, (half, tok_dev), 0)
+    weight = jnp.zeros((half, tok_dev), jnp.float32)
+    named = jnp.zeros((half, tok_dev), jnp.float32)
+    for k in range(routes_ref.shape[0]):
+        hit = routes_ref[k : k + 1, :] == ids
+        weight = jnp.where(hit, combine_ref[k : k + 1, :].astype(jnp.float32), weight)
+        named = jnp.where(hit, 1.0, named)
+    earlier = lax.broadcasted_iota(jnp.int32, (tok_dev, tok_dev), 0) < lax.broadcasted_iota(
+        jnp.int32, (tok_dev, tok_dev), 1
+    )
+    rank = mul(named.astype(jnp.bfloat16), earlier.astype(jnp.bfloat16))
+    rank = jnp.where(named > 0.0, rank, -1.0)
+    out_ref[:, 2 * width :] = jnp.concatenate([weight, rank], axis=0).astype(jnp.bfloat16)
+
+
+def pack(tokens, grad_out, routes, combine):
+    tok_dev, width = tokens.shape
+    return pl.pallas_call(
+        pack_kernel,
+        out_shape=jax.ShapeDtypeStruct((tok_dev, 2 * width + tok_dev), jnp.bfloat16),
+        compiler_params=pltpu.CompilerParams(vmem_limit_bytes=VMEM_BYTES),
+        cost_estimate=pl.CostEstimate(flops=10**7, bytes_accessed=2 * 10**6, transcendentals=0),
+    )(tokens, grad_out, routes.T, combine.T)
+
+
+def group_kernel(first, last, own, depth, blocks, *refs):
+    refs = list(refs)
+
+    def take(count):
+        return [refs.pop(0) for _ in range(count)]
+
+    block_hbm = take(blocks)
+    weight_hbm = take(3)
+    acc_hbm = [] if first else take(3)
+    out_hbm = take(3)
+    piece_hbm = take(2) if own else []
+    block_buf, x_rows, d_rows, hid, both, info = take(6)
+    weight_buf = gate_ref, up_ref, down_ref = take(3)
+    acc_buf = take(3)
+    out_buf = take(3) if last else acc_buf
+    if own:
+        back, places, *piece_buf = take(4)
+    block_sem, weight_sem, acc_sem, out_sem, piece_sem = take(5)
+    held, rows, width = x_rows.shape
+    tok_dev = block_buf.shape[1]
+    half = tok_dev // 2
+    units = hid.shape[1]
+    shard = lax.axis_index("dp")
+    base = lax.axis_index("expert") * held
+    x_cut = acc_buf[0].shape[1]
+    h_cut = acc_buf[2].shape[1]
+
+    def weight_in(e, m):
+        return pltpu.make_async_copy(weight_hbm[m].at[e], weight_buf[m].at[e], weight_sem.at[m, e])
+
+    def acc_in(e, m):
+        return pltpu.make_async_copy(acc_hbm[m].at[e], acc_buf[m].at[e], acc_sem.at[m, e])
+
+    def grad_out(e, m):
+        return pltpu.make_async_copy(out_buf[m].at[e], out_hbm[m].at[e], out_sem.at[m, e])
+
+    for b in range(blocks):
+        pltpu.make_async_copy(block_hbm[b], block_buf.at[b], block_sem.at[b]).start()
+
+    slot = lax.broadcasted_iota(jnp.int32, (depth, tok_dev), 0).astype(jnp.float32)
+
+    def select(b, _):
+        pltpu.make_async_copy(block_hbm[0], block_buf.at[b], block_sem.at[b]).wait()
+
+        @pl.when(b == 1)
+        def _():
+            for m in range(3):
+                weight_in(0, m).start()
+
+        info[...] = block_buf[b, :, 2 * width :].astype(jnp.float32)
+        picks, scaled = [], []
+        for i in range(held):
+            weight = info[pl.ds(base + i, 1), :]
+            rank = info[pl.ds(half + base + i, 1), :]
+            hit = slot == rank
+            picks.append(jnp.where(hit, 1.0, 0.0))
+            scaled.append(jnp.where(hit, weight, 0.0))
+        pick = jnp.concatenate(picks, axis=0).astype(jnp.bfloat16)
+        scale = jnp.concatenate(scaled, axis=0).astype(jnp.bfloat16)
+        if own:
+
+            @pl.when(b < own)
+            def _():
+                places[b] = pick
+
+        got_x = mul(pick, block_buf[b, :, :width]).astype(jnp.bfloat16)
+        got_d = mul(scale, block_buf[b, :, width : 2 * width]).astype(jnp.bfloat16)
+        at = pl.ds(pl.multiple_of(b * depth, depth), depth)
+        for i in range(held):
+            x_rows[i, at, :] = got_x[i * depth : (i + 1) * depth]
+            d_rows[i, at, :] = got_d[i * depth : (i + 1) * depth]
+        return 0
+
+    lax.fori_loop(0, blocks, select, 0)
+
+    def expert(e, _):
+        for m in range(3):
+            weight_in(e, m).wait()
+        for m in range(len(acc_hbm)):
+            acc_in(e, m).start()
+
+        @pl.when(e + 1 < held)
+        def _():
+            for m in range(3):
+                weight_in(e + 1, m).start()
+
+        rows_x = x_rows[e]
+        d_out = d_rows[e]
+        gate_pre = mul(rows_x, gate_ref[e])
+        up_pre = mul(rows_x, up_ref[e])
+        d_hidden = contract_last(d_out, down_ref[e])
+        sig = 0.5 * jnp.tanh(0.5 * gate_pre) + 0.5
+        act = gate_pre * sig
+        hid[...] = (act * up_pre).astype(jnp.bfloat16)
+        both[:, :units] = (d_hidden * up_pre * (sig + act * (1.0 - sig))).astype(jnp.bfloat16)
+        both[:, units:] = (d_hidden * act).astype(jnp.bfloat16)
+        x_part = x_rows[e, :, pl.ds(pl.multiple_of(shard * x_cut, LANES), x_cut)]
+        h_part = hid[:, pl.ds(pl.multiple_of(shard * h_cut, LANES), h_cut)]
+        grad_both = contract_first(x_part, both[...])
+        grads = [grad_both[:, :units], grad_both[:, units:], contract_first(h_part, d_out)]
+        for m in range(3):
+            grad = grads[m]
+            if not first:
+                acc_in(e, m).wait()
+                grad = acc_buf[m][e] + grad
+            out_buf[m][e] = grad.astype(out_buf[m].dtype)
+            grad_out(e, m).start()
+        if own:
+            kept = own * depth
+            back[e] = (
+                contract_last(both[:kept, :units], gate_ref[e])
+                + contract_last(both[:kept, units:], up_ref[e])
+            ).astype(jnp.bfloat16)
+        return 0
+
+    lax.fori_loop(0, held, expert, 0)
+
+    if own:
+
+        def collect(p, _):
+            for odd in range(2):
+                at = pl.ds(pl.multiple_of((2 * p + odd) * depth, depth), depth)
+                rows_b = jnp.concatenate([back[i, at, :] for i in range(held)], axis=0)
+                piece_buf[odd][p] = contract_first(places[2 * p + odd], rows_b).astype(
+                    jnp.bfloat16
+                )
+            return 0
+
+        lax.fori_loop(0, own // 2, collect, 0)
+        pieces_out = [
+            pltpu.make_async_copy(piece_buf[m], piece_hbm[m], piece_sem.at[m]) for m in range(2)
+        ]
+        for copy in pieces_out:
+            copy.start()
+        for copy in pieces_out:
+            copy.wait()
+    for e in range(held):
+        for m in range(3):
+            grad_out(e, m).wait()
+
+
+def group(records, weights, accs, shards, depth, last=False, own=0):
+    tok_dev, record = records[0].shape
+    held, width, units = weights[0].shape
+    blocks = len(records)
+    rows = blocks * depth
+    first = accs is None
+    grad_shapes = [
+        (held, width // shards, units),
+        (held, width // shards, units),
+        (held, units // shards, width),
+    ]
+    args = list(records) + list(weights) + ([] if first else list(accs))
+    out_type = jnp.bfloat16 if last else jnp.float32
+    out_shape = [jax.ShapeDtypeStruct(s, out_type) for s in grad_shapes]
+    scratch = [
+        pltpu.VMEM((blocks, tok_dev, record), jnp.bfloat16),
+        pltpu.VMEM((held, rows, width), jnp.bfloat16),
+        pltpu.VMEM((held, rows, width), jnp.bfloat16),
+        pltpu.VMEM((rows, units), jnp.bfloat16),
+        pltpu.VMEM((rows, 2 * units), jnp.bfloat16),
+        pltpu.VMEM((tok_dev, tok_dev), jnp.float32),
+    ]
+    scratch += [pltpu.VMEM(w.shape, jnp.bfloat16) for w in weights]
+    scratch += [pltpu.VMEM(s, jnp.float32) for s in grad_shapes]
+    if last:
+        scratch += [pltpu.VMEM(s, jnp.bfloat16) for s in grad_shapes]
+    if own:
+        piece = (own // 2, tok_dev, width)
+        out_shape += [jax.ShapeDtypeStruct(piece, jnp.bfloat16)] * 2
+        scratch += [
+            pltpu.VMEM((held, own * depth, width), jnp.bfloat16),
+            pltpu.VMEM((own, held * depth, tok_dev), jnp.bfloat16),
+            pltpu.VMEM(piece, jnp.bfloat16),
+            pltpu.VMEM(piece, jnp.bfloat16),
+        ]
+    scratch += [
+        pltpu.SemaphoreType.DMA((blocks,)),
+        pltpu.SemaphoreType.DMA((3, held)),
+        pltpu.SemaphoreType.DMA((3, held)),
+        pltpu.SemaphoreType.DMA((3, held)),
+        pltpu.SemaphoreType.DMA((2,)),
+    ]
+    work = 2 * rows * held * width * units
+    return pl.pallas_call(
+        functools.partial(group_kernel, first, last, own, depth, blocks),
+        in_specs=[pl.BlockSpec(memory_space=pl.ANY)] * len(args),
+        out_specs=[pl.BlockSpec(memory_space=pl.ANY)] * len(out_shape),
+        out_shape=out_shape,
+        scratch_shapes=scratch,
+        compiler_params=pltpu.CompilerParams(vmem_limit_bytes=VMEM_BYTES),
+        cost_estimate=pl.CostEstimate(
+            flops=work // 8,
+            bytes_accessed=tok_dev * record * 2,
+            transcendentals=rows * held * units,
+        ),
+    )(*args)
+
+
+def swap(value, axis, bit):
+    size = lax.axis_size(axis)
+    return lax.ppermute(value, axis, [(i, i ^ bit) for i in range(size)])
+
+
+def beside(value):
+    return swap(value, "expert", 2)
+
+
+def below(value):
+    return swap(value, "expert", 4)
+
+
+def pairs(*blocks):
+    return [piece for block in blocks for piece in (block, swap(block, "expert", 1))]
+
+
+def middle(value):
+    return lax.ppermute(value, "dp", [(1, 2), (2, 1)])
+
+
+def outward(value):
+    return lax.ppermute(value, "dp", [(1, 0), (2, 3)])
+
+
+def gathered_shards(tokens, grad_out, routes, combine, w_gate, w_up, w_down):
+    shards = lax.axis_size("dp")
+    tok_dev = tokens.shape[0]
+    depth = depth_of(tok_dev, routes.shape[1], w_gate.shape[0] * lax.axis_size("expert"))
+    run = functools.partial(
+        group, weights=(w_gate, w_up, w_down), shards=shards, depth=depth
+    )
+    tie = lax.optimization_barrier
+    inner = jnp.logical_and(lax.axis_index("dp") > 0, lax.axis_index("dp") < shards - 1)
+    o0 = pack(tokens, grad_out, routes, combine)
+    x0, y0, o1, near = beside(o0), below(o0), swap(o0, "dp", 1), middle(o0)
+    group0 = pairs(o0)
+    x0, y0, o1, near, group0 = tie((x0, y0, o1, near, group0))
+    x1, d0, near_end, far = beside(o1), below(x0), outward(near), middle(o1)
+    group0 += pairs(x0, y0, o1)
+    y0, near, group0 = tie((y0, near, group0))
+    *accs, even0, odd0 = run(group0, accs=None, own=6)
+    x1, d0, near_end, near, far, even0, odd0, y0 = tie(
+        (x1, d0, near_end, near, far, even0, odd0, y0)
+    )
+    o2 = jnp.where(inner, near, near_end)
+    x2, y2, far_end, y1 = beside(o2), below(o2), outward(far), swap(y0, "dp", 1)
+    crossed0 = swap(odd0, "expert", 1)
+    group1 = pairs(d0, x1, o2)
+    group1, crossed0, d0 = tie((group1, crossed0, d0))
+    pair0 = (even0.astype(jnp.float32) + crossed0.astype(jnp.float32)).astype(jnp.bfloat16)
+    *accs, even1, odd1 = run(group1, accs=accs, own=2)
+    x2, y2, far_end, y1, far, d0, pair0, even1, odd1 = tie(
+        (x2, y2, far_end, y1, far, d0, pair0, even1, odd1)
+    )
+    o3 = jnp.where(inner, far, far_end)
+    x3, y3, d1, d2 = beside(o3), below(o3), swap(d0, "dp", 1), below(x2)
+    crossed1 = swap(odd1, "expert", 1)
+    group2 = pairs(x2, y2, o3, y1)
+    group2, crossed1 = tie((group2, crossed1))
+    pair1 = (even1.astype(jnp.float32) + crossed1.astype(jnp.float32)).astype(jnp.bfloat16)
+    accs = run(group2, accs=accs)
+    x3, y3, d1, d2, accs, pair1 = tie((x3, y3, d1, d2, accs, pair1))
+    d3 = beside(y3)
+    sent = [beside(pair0[1]), below(pair0[2]), swap(pair1[0], "expert", 6)]
+    group3 = pairs(x3, y3, d1, d2)
+    accs = run(group3, accs=accs)
+    d3, accs, sent = tie((d3, accs, sent))
+    total = pair0[0].astype(jnp.float32)
+    for piece in sent:
+        total = total + piece.astype(jnp.float32)
+    accs = run(pairs(d3), accs=accs, last=True)
+    return (total.astype(jnp.bfloat16), *accs)
+
+
 def solution(mesh):
+    shards, peers = mesh.shape["dp"], mesh.shape["expert"]
+
+    def body(tokens, grad_out, routes, combine, w_gate, w_up, w_down):
+        tok_dev, width = tokens.shape
+        gathered = shards * peers * tok_dev * (2 * width + tok_dev) * 2
+        fits = (
+            peers == 8
+            and shards == 4
+            and peers * w_gate.shape[0] <= tok_dev // 2
+            and tok_dev == LANES
+            and gathered <= GATHER_BYTES
+        )
+        plan = gathered_shards if fits else routed_shards
+        return plan(tokens, grad_out, routes, combine, w_gate, w_up, w_down)
+
     return jax.shard_map(
-        shards,
+        body,
         mesh=mesh,
         in_specs=(
             P(("dp", "expert"), None),

time: 365 us -> 156 us (0.43)
  waiting for transfers between devices: 204 us -> 39 us
  Pallas kernels: 0 us -> 73.9 us
  local copies, waits for them, and re-layouts: 56.3 us -> 4.36 us
  matrix products: 47.4 us -> 0 us
  other arithmetic: 24.2 us -> 5.19 us
  starting transfers between devices: 17.3 us -> 31.4 us
  between operations: 14.6 us -> 1.23 us
    reduce_scatter x6 -> x0, waiting for transfers between devices: 140 us -> none  [the longest x3 110 us: shards(): lax.psum_scatter(contract_first(rows_x, d_both).astype(jnp.bfloat16), 'dp...]
    pallas_call x0 -> x6, Pallas kernels: none -> 73.9 us  [the longest x5 71.9 us: group(): pl.pallas_call(functools.partial(group_kernel, first, last, own, depth, b...]
    all_to_all x4 -> x0, waiting for transfers between devices: 64.4 us -> none  [the longest x1 31.1 us: shards(): lax.all_to_all(send_x, 'expert', split_axis=0, concat_axis=0, tiled=True)]
    dot_general x21 -> x0, matrix products: 47.4 us -> none  [the longest x9 18.2 us: contract_last(): lax.dot_general(left, right, (((1,), (1,)), ((), ())), preferred_element_...]
    ppermute x0 -> x38, waiting for transfers between devices: none -> 39 us  [the longest x34 36.5 us: swap(): return lax.ppermute(value, axis, [(i, i ^ bit) for i in range(size)])]
    gather x5 -> x0, local copies, waits for them, and re-layouts: 32.1 us -> none  [the longest x2 11 us: shards(): flat_back[row_of_pair].astype(jnp.float32)]
    ppermute x0 -> x38, starting transfers between devices: none -> 31.4 us  [the longest x34 26.5 us: swap(): return lax.ppermute(value, axis, [(i, i ^ bit) for i in range(size)])]
    all_to_all x4 -> x0, starting transfers between devices: 16.7 us -> none  [the longest x1 5.17 us: shards(): lax.all_to_all(send_c, 'expert', split_axis=0, concat_axis=0, tiled=True)]
  transfers between devices with their start and end apart: 10 -> 38, of which waited for: 8 -> 11; matrix products, arithmetic and copies ran while one was open for 24% -> 3% of each run, Pallas kernels for 0% -> 39%
where the time goes in v1:
time: 156 us; the launch traced here: 155 us
  Pallas kernels  73.9 us (47%)
  waiting for transfers between devices  39 us (25%)
  starting transfers between devices  31.4 us (20%)
  other arithmetic  5.19 us (3%)
  local copies, waits for them, and re-layouts  4.36 us (3%)
    pallas_call x5, Pallas kernels, group(): pl.pallas_call(functools.partial(group_kernel, first, last, own, depth, b...  71.9 us
    ppermute x34, waiting for transfers between devices, swap(): return lax.ppermute(value, axis, [(i, i ^ bit) for i in range(size)])  36.5 us
    ppermute x34, starting transfers between devices, swap(): return lax.ppermute(value, axis, [(i, i ^ bit) for i in range(size)])  26.5 us
    unnamed x52, local copies, waits for them, and re-layouts  3.51 us
  transfers between devices with their start and end apart: 38, of which 11 were waited for; matrix products, arithmetic and copies ran while one was open for 3% of the time, Pallas kernels for 39%

profile of v1, /device:TPU:0, one launch (start us, length us, event | category | flops | bytes accessed | tf_op | source)
XLA Modules:
  0.0 155.1 jit_solution(530428264997166559)
XLA Ops:
  0.6 2.0 %shard_map.102.refs_0_ = bf16[128,2176]{1,0:T(8,128)(2,1)} custom-call(bf16[128,1024]{1,0:T(8,128)(2,1)} %tok_ref.1, bf16[128,1024]{1,0:T(8,128)(2,1)} %dy_ref.1, s32[10,128]{1,0:T(8,128)} %bitcast.10, bf16[10,128]{1,0:T(8,128)(2,1)} %bitcast.11), custom_call_target="tpu_custom_call" | custom-call | flops 10000000 | bytes 2000000 | tf_op jit(solution)/shard_map/pallas_call | solution.py:155
  2.6 2.9 %collective-permute-start = (bf16[128,2176]{1,0:T(8,128)(2,1)}, bf16[128,2176]{1,0:T(8,128)(2,1)S(1)}, u32[]{:S(2)}, u32[]{:S(2)}) collective-permute-start(bf16[128,2176]{1,0:T(8,128)(2,1)} %shard_map.102.refs_0_), channel_id=1, source_target_pairs={{0,2},{1,3},{2,0},{3,1},{4,6},{5,7},{6,4},{7,5},{8,10},{9,11},{10,... | collective-permute-start | bytes 1671176 | tf_op jit(solution)/shard_map/ppermute | solution.py:364
  5.6 1.5 collective-permute-start.1
  7.1 1.6 %collective-permute-start.2 = (bf16[128,2176]{1,0:T(8,128)(2,1)}, bf16[128,2176]{1,0:T(8,128)(2,1)}, u32[]{:S(2)}, u32[]{:S(2)}) collective-permute-start(bf16[128,2176]{1,0:T(8,128)(2,1)} %shard_map.102.refs_0_), channel_id=1, source_target_pairs={{0,8},{8,0},{16,24},{24,16},{1,9},{9,1},{17,25},{25,17},{2,10},{10... | collective-permute-start | bytes 1671176 | tf_op jit(solution)/shard_map/ppermute | solution.py:364
  9.4 9.0 %collective-permute-done.refs_2_ = bf16[128,2176]{1,0:T(8,128)(2,1)S(1)} collective-permute-done((bf16[128,2176]{1,0:T(8,128)(2,1)}, bf16[128,2176]{1,0:T(8,128)(2,1)S(1)}, u32[]{:S(2)}, u32[]{:S(2)}) %collective-permute-start) | collective-permute-done | bytes 557088 | tf_op jit(solution)/shard_map/ppermute | solution.py:364
  18.4 1.6 %collective-permute-done.1.refs_4_ = bf16[128,2176]{1,0:T(8,128)(2,1)} collective-permute-done((bf16[128,2176]{1,0:T(8,128)(2,1)}, bf16[128,2176]{1,0:T(8,128)(2,1)}, u32[]{:S(2)}, u32[]{:S(2)}) %collective-permute-start.1) | collective-permute-done | bytes 557088 | tf_op jit(solution)/shard_map/ppermute | solution.py:364
  20.0 1.2 collective-permute-done.2.refs_6_
  22.1 1.5 collective-permute-start.11
  24.9 1.3 collective-permute-start.7
  26.2 16.5 %shard_map.103 = (f32[3,256,512]{2,1,0:T(8,128)}, f32[3,256,512]{2,1,0:T(8,128)}, f32[3,128,1024]{2,1,0:T(8,128)}, bf16[3,128,1024]{2,1,0:T(8,128)(2,1)}, bf16[3,128,1024]{2,1,0:T(8,128)(2,1)}) custom-call(bf16[128,2176]{1,0:T(8,128)(2,1)} %shard_map.102.refs_0_, bf16[128,2176]{1,0:T(8,128)(2,1)} %copy-done.19, bf16[128,2176]{1,0:T(8,128)(2,1)} %copy-done.18, ...), custom_call_target="tpu_custom_call" | custom-call | flops 201326592 | bytes 557056 | tf_op jit(solution)/shard_map/pallas_call | solution.py:347
  42.8 2.5 %collective-permute-done.7 = bf16[128,2176]{1,0:T(8,128)(2,1)S(1)} collective-permute-done((bf16[128,2176]{1,0:T(8,128)(2,1)S(1)}, bf16[128,2176]{1,0:T(8,128)(2,1)S(1)}, u32[]{:S(2)}, u32[]{:S(2)}) %collective-permute-start.7) | collective-permute-done | bytes 557088 | tf_op jit(solution)/shard_map/ppermute | solution.py:384
  46.5 1.5 collective-permute-start.12
  48.0 0.9 collective-permute-start.13
  48.9 1.5 collective-permute-start.14
  50.4 5.6 %collective-permute-start.15 = (bf16[128,2176]{1,0:T(8,128)(2,1)}, bf16[128,2176]{1,0:T(8,128)(2,1)}, u32[]{:S(2)}, u32[]{:S(2)}) collective-permute-start(bf16[128,2176]{1,0:T(8,128)(2,1)} %collective-permute-done.1.refs_4_), channel_id=1, source_target_pairs={{0,8},{8,0},{16,24},{24,16},{1,9},{9,1},{17,25},{25,17},{2,10},{10... | collective-permute-start | bytes 1671176 | tf_op jit(solution)/shard_map/ppermute | solution.py:364
  56.0 15.3 %shard_map.104 = (f32[3,256,512]{2,1,0:T(8,128)}, f32[3,256,512]{2,1,0:T(8,128)}, f32[3,128,1024]{2,1,0:T(8,128)}, bf16[1,128,1024]{2,1,0:T(8,128)(2,1)}, bf16[1,128,1024]{2,1,0:T(8,128)(2,1)}) custom-call(bf16[128,2176]{1,0:T(8,128)(2,1)} %copy-done.3, bf16[128,2176]{1,0:T(8,128)(2,1)} %copy-done.14, bf16[128,2176]{1,0:T(8,128)(2,1)} %copy-done.7, ...), custom_call_target="tpu_custom_call" | custom-call | flops 150994944 | bytes 557056 | tf_op jit(solution)/shard_map/pallas_call | solution.py:347
  71.7 8.4 %collective-permute-done.15.refs_6_ = bf16[128,2176]{1,0:T(8,128)(2,1)} collective-permute-done((bf16[128,2176]{1,0:T(8,128)(2,1)}, bf16[128,2176]{1,0:T(8,128)(2,1)}, u32[]{:S(2)}, u32[]{:S(2)}) %collective-permute-start.15) | collective-permute-done | bytes 557088 | tf_op jit(solution)/shard_map/ppermute | solution.py:364
  80.1 1.1 broadcast_select_fusion.refs_4_
  82.4 3.7 %collective-permute-done.28 = bf16[1,128,1024]{2,1,0:T(8,128)(2,1)} collective-permute-done((bf16[1,128,1024]{2,1,0:T(8,128)(2,1)S(1)}, bf16[1,128,1024]{2,1,0:T(8,128)(2,1)}, u32[]{:S(2)}, u32[]{:S(2)}) %collective-permute-start.28) | collective-permute-done | bytes 262176 | tf_op jit(solution)/shard_map/ppermute | solution.py:364
  86.7 1.1 collective-permute-start.21
  89.4 1.0 collective-permute-start.23
  90.3 14.4 %shard_map.105 = (f32[3,256,512]{2,1,0:T(8,128)}, f32[3,256,512]{2,1,0:T(8,128)}, f32[3,128,1024]{2,1,0:T(8,128)}) custom-call(bf16[128,2176]{1,0:T(8,128)(2,1)} %copy-done.5, bf16[128,2176]{1,0:T(8,128)(2,1)} %copy-done.9, bf16[128,2176]{1,0:T(8,128)(2,1)} %collective-permute-done.13.refs_2_, bf16[128,2176]{1,0:T(8,128)(2,1)} %copy-done.12, ...), custom_call_target="tpu_custom_call" | custom-call | flops 201326592 | bytes 557056 | tf_op jit(solution)/shard_map/pallas_call | solution.py:347
  104.8 1.7 %add_convert_fusion.1 = bf16[1,128,1024]{2,1,0:T(8,128)(2,1)} fusion(bf16[1,128,1024]{2,1,0:T(8,128)(2,1)} %collective-permute-done.28, bf16[1,128,1024]{2,1,0:T(8,128)(2,1)S(1)} %copy-done.23), kind=kLoop, calls=%fused_computation.7 | loop fusion | flops 524288 | bytes 786432 | tf_op jit(solution)/shard_map/convert_element_type | solution.py:422
  106.5 6.6 %collective-permute-done.23.refs_6_ = bf16[128,2176]{1,0:T(8,128)(2,1)} collective-permute-done((bf16[128,2176]{1,0:T(8,128)(2,1)S(1)}, bf16[128,2176]{1,0:T(8,128)(2,1)}, u32[]{:S(2)}, u32[]{:S(2)}) %collective-permute-start.23) | collective-permute-done | bytes 557088 | tf_op jit(solution)/shard_map/ppermute | solution.py:364
  114.1 1.5 collective-permute-start.29
  115.7 0.8 slice_bitcast_fusion
  117.0 1.1 collective-permute-start.35
  118.1 1.9 %collective-permute-start.36 = (bf16[128,1024]{1,0:T(8,128)(2,1)}, bf16[128,1024]{1,0:T(8,128)(2,1)}, u32[]{:S(2)}, u32[]{:S(2)}) collective-permute-start(bf16[128,1024]{1,0:T(8,128)(2,1)} %bitcast.5), channel_id=1, source_target_pairs={{0,6},{1,7},{2,4},{3,5},{4,2},{5,3},{6,0},{7,1},{8,14},{9,15},{10,... | collective-permute-start | bytes 786440 | tf_op jit(solution)/shard_map/ppermute | solution.py:364
  120.9 14.3 %shard_map.106 = (f32[3,256,512]{2,1,0:T(8,128)}, f32[3,256,512]{2,1,0:T(8,128)}, f32[3,128,1024]{2,1,0:T(8,128)}) custom-call(bf16[128,2176]{1,0:T(8,128)(2,1)} %copy-done.8, bf16[128,2176]{1,0:T(8,128)(2,1)} %copy-done.10, bf16[128,2176]{1,0:T(8,128)(2,1)} %copy-done.6, bf16[128,2176]{1,0:T(8,128)(2,1)} %copy-done.13, ...), custom_call_target="tpu_custom_call" | custom-call | flops 201326592 | bytes 557056 | tf_op jit(solution)/shard_map/pallas_call | solution.py:347
  135.4 5.1 %collective-permute-done.36 = bf16[128,1024]{1,0:T(8,128)(2,1)} collective-permute-done((bf16[128,1024]{1,0:T(8,128)(2,1)}, bf16[128,1024]{1,0:T(8,128)(2,1)}, u32[]{:S(2)}, u32[]{:S(2)}) %collective-permute-start.36) | collective-permute-done | bytes 262176 | tf_op jit(solution)/shard_map/ppermute | solution.py:364
  140.5 2.0 %fusion.2 = bf16[128,1024]{1,0:T(8,128)(2,1)} fusion(bf16[128,1024]{1,0:T(8,128)(2,1)} %collective-permute-done.36, bf16[128,1024]{1,0:T(8,128)(2,1)} %collective-permute-done.35, bf16[128,1024]{1,0:T(8,128)(2,1)} %collective-permute-done.34, bf16[3,128,1024]{2,1,0:T(8,128)(2,1)S(1)} %add_convert_fusion), kind=kLoop, calls=%fused_computation.6 | loop fusion | flops 1048576 | bytes 1310720 | tf_op jit(solution)/shard_map/convert_element_type | solution.py:434
  143.5 11.4 %shard_map.107 = (bf16[3,256,512]{2,1,0:T(8,128)(2,1)}, bf16[3,256,512]{2,1,0:T(8,128)(2,1)}, bf16[3,128,1024]{2,1,0:T(8,128)(2,1)}) custom-call(bf16[128,2176]{1,0:T(8,128)(2,1)} %collective-permute-done.29.refs_0_, bf16[128,2176]{1,0:T(8,128)(2,1)} %copy-done.22, bf16[3,1024,512]{2,1,0:T(8,128)(2,1)} %refs_2_.1, bf16[3,1024,512]{2,1,0:T(8,128)(2,1)} %refs_3_.1, ...), custom_call_target="tpu_custom_call" | custom-call | flops 50331648 | bytes 557056 | tf_op jit(solution)/shard_map/pallas_call | solution.py:347
  (108 shorter events, 11.3 us)
Async XLA Ops:
  2.6 15.8 %collective-permute-start = (bf16[128,2176]{1,0:T(8,128)(2,1)}, bf16[128,2176]{1,0:T(8,128)(2,1)S(1)}, u32[]{:S(2)}, u32[]{:S(2)}) collective-permute-start(bf16[128,2176]{1,0:T(8,128)(2,1)} %shard_map.102.refs_0_), channel_id=1, source_target_pairs={{0,2},{1,3},{2,0},{3,1},{4,6},{5,7},{6,4},{7,5},{8,10},{9,11},{10,... | collective-permute-start | bytes 1671176 | tf_op jit(solution)/shard_map/ppermute | solution.py:364
  5.6 14.4 %collective-permute-start.1 = (bf16[128,2176]{1,0:T(8,128)(2,1)}, bf16[128,2176]{1,0:T(8,128)(2,1)}, u32[]{:S(2)}, u32[]{:S(2)}) collective-permute-start(bf16[128,2176]{1,0:T(8,128)(2,1)} %shard_map.102.refs_0_), channel_id=1, source_target_pairs={{0,4},{1,5},{2,6},{3,7},{4,0},{5,1},{6,2},{7,3},{8,12},{9,13},{10,... | collective-permute-start | bytes 1671176 | tf_op jit(solution)/shard_map/ppermute | solution.py:364
  7.1 14.1 %collective-permute-start.2 = (bf16[128,2176]{1,0:T(8,128)(2,1)}, bf16[128,2176]{1,0:T(8,128)(2,1)}, u32[]{:S(2)}, u32[]{:S(2)}) collective-permute-start(bf16[128,2176]{1,0:T(8,128)(2,1)} %shard_map.102.refs_0_), channel_id=1, source_target_pairs={{0,8},{8,0},{16,24},{24,16},{1,9},{9,1},{17,25},{25,17},{2,10},{10... | collective-permute-start | bytes 1671176 | tf_op jit(solution)/shard_map/ppermute | solution.py:364
  8.7 12.5 %collective-permute-start.3 = (bf16[128,2176]{1,0:T(8,128)(2,1)}, bf16[128,2176]{1,0:T(8,128)(2,1)S(1)}, u32[]{:S(2)}, u32[]{:S(2)}) collective-permute-start(bf16[128,2176]{1,0:T(8,128)(2,1)} %shard_map.102.refs_0_), channel_id=1, source_target_pairs={{8,16},{16,8},{9,17},{17,9},{10,18},{18,10},{11,19},{19,11},{12,20... | collective-permute-start | bytes 1671176 | tf_op jit(solution)/shard_map/ppermute | solution.py:380
  9.4 11.9 %collective-permute-start.4 = (bf16[128,2176]{1,0:T(8,128)(2,1)}, bf16[128,2176]{1,0:T(8,128)(2,1)S(1)}, u32[]{:S(2)}, u32[]{:S(2)}) collective-permute-start(bf16[128,2176]{1,0:T(8,128)(2,1)} %shard_map.102.refs_0_), channel_id=1, source_target_pairs={{0,1},{1,0},{2,3},{3,2},{4,5},{5,4},{6,7},{7,6},{8,9},{9,8},{10,11... | collective-permute-start | bytes 1671176 | tf_op jit(solution)/shard_map/ppermute | solution.py:364
  21.8 4.4 %collective-permute-start.9 = (bf16[128,2176]{1,0:T(8,128)(2,1)}, bf16[128,2176]{1,0:T(8,128)(2,1)}, u32[]{:S(2)}, u32[]{:S(2)}) collective-permute-start(bf16[128,2176]{1,0:T(8,128)(2,1)} %collective-permute-done.1.refs_4_), channel_id=1, source_target_pairs={{0,1},{1,0},{2,3},{3,2},{4,5},{5,4},{6,7},{7,6},{8,9},{9,8},{10,11... | collective-permute-start | bytes 1671176 | tf_op jit(solution)/shard_map/ppermute | solution.py:364
  22.1 20.7 %collective-permute-start.11 = (bf16[128,2176]{1,0:T(8,128)(2,1)}, bf16[128,2176]{1,0:T(8,128)(2,1)}, u32[]{:S(2)}, u32[]{:S(2)}) collective-permute-start(bf16[128,2176]{1,0:T(8,128)(2,1)} %collective-permute-done.2.refs_6_), channel_id=1, source_target_pairs={{8,16},{16,8},{9,17},{17,9},{10,18},{18,10},{11,19},{19,11},{12,20... | collective-permute-start | bytes 1671176 | tf_op jit(solution)/shard_map/ppermute | solution.py:380
  23.5 19.2 %collective-permute-start.5 = (bf16[128,2176]{1,0:T(8,128)(2,1)}, bf16[128,2176]{1,0:T(8,128)(2,1)S(1)}, u32[]{:S(2)}, u32[]{:S(2)}) collective-permute-start(bf16[128,2176]{1,0:T(8,128)(2,1)} %collective-permute-done.2.refs_6_), channel_id=1, source_target_pairs={{0,2},{1,3},{2,0},{3,1},{4,6},{5,7},{6,4},{7,5},{8,10},{9,11},{10,... | collective-permute-start | bytes 1671176 | tf_op jit(solution)/shard_map/ppermute | solution.py:364
  24.0 18.7 %collective-permute-start.6 = (bf16[128,2176]{1,0:T(8,128)(2,1)S(1)}, bf16[128,2176]{1,0:T(8,128)(2,1)S(1)}, u32[]{:S(2)}, u32[]{:S(2)}) collective-permute-start(bf16[128,2176]{1,0:T(8,128)(2,1)S(1)} %collective-permute-done.refs_2_), channel_id=1, source_target_pairs={{0,4},{1,5},{2,6},{3,7},{4,0},{5,1},{6,2},{7,3},{8,12},{9,13},{10,... | collective-permute-start | bytes 1671176 | tf_op jit(solution)/shard_map/ppermute | solution.py:364
  24.9 20.4 %collective-permute-start.7 = (bf16[128,2176]{1,0:T(8,128)(2,1)S(1)}, bf16[128,2176]{1,0:T(8,128)(2,1)S(1)}, u32[]{:S(2)}, u32[]{:S(2)}) collective-permute-start(bf16[128,2176]{1,0:T(8,128)(2,1)S(1)} %collective-permute-done.3), channel_id=1, source_target_pairs={{8,0},{16,24},{9,1},{17,25},{10,2},{18,26},{11,3},{19,27},{12,4},{... | collective-permute-start | bytes 1671176 | tf_op jit(solution)/shard_map/ppermute | solution.py:384
  46.0 4.4 %collective-permute-start.17 = (bf16[128,2176]{1,0:T(8,128)(2,1)S(1)}, bf16[128,2176]{1,0:T(8,128)(2,1)S(1)}, u32[]{:S(2)}, u32[]{:S(2)}) collective-permute-start(bf16[128,2176]{1,0:T(8,128)(2,1)S(1)} %collective-permute-done.5.refs_2_), channel_id=1, source_target_pairs={{0,1},{1,0},{2,3},{3,2},{4,5},{5,4},{6,7},{7,6},{8,9},{9,8},{10,11... | collective-permute-start | bytes 1671176 | tf_op jit(solution)/shard_map/ppermute | solution.py:364
  46.1 9.9 %collective-permute-start.19 = (bf16[3,128,1024]{2,1,0:T(8,128)(2,1)S(1)}, bf16[3,128,1024]{2,1,0:T(8,128)(2,1)S(1)}, u32[]{:S(2)}, u32[]{:S(2)}) collective-permute-start(bf16[3,128,1024]{2,1,0:T(8,128)(2,1)S(1)} %copy-done.24), channel_id=1, source_target_pairs={{0,1},{1,0},{2,3},{3,2},{4,5},{5,4},{6,7},{7,6},{8,9},{9,8},{10,11... | collective-permute-start | bytes 2359304 | tf_op jit(solution)/shard_map/ppermute | solution.py:364
  46.5 25.2 %collective-permute-start.12 = (bf16[128,2176]{1,0:T(8,128)(2,1)S(1)}, bf16[128,2176]{1,0:T(8,128)(2,1)S(1)}, u32[]{:S(2)}, u32[]{:S(2)}) collective-permute-start(bf16[128,2176]{1,0:T(8,128)(2,1)S(1)} %broadcast_select_fusion.1.refs_4_), channel_id=1, source_target_pairs={{0,2},{1,3},{2,0},{3,1},{4,6},{5,7},{6,4},{7,5},{8,10},{9,11},{10,... | collective-permute-start | bytes 1671176 | tf_op jit(solution)/shard_map/ppermute | solution.py:364
  48.0 23.7 %collective-permute-start.13 = (bf16[128,2176]{1,0:T(8,128)(2,1)S(1)}, bf16[128,2176]{1,0:T(8,128)(2,1)}, u32[]{:S(2)}, u32[]{:S(2)}) collective-permute-start(bf16[128,2176]{1,0:T(8,128)(2,1)S(1)} %broadcast_select_fusion.1.refs_4_), channel_id=1, source_target_pairs={{0,4},{1,5},{2,6},{3,7},{4,0},{5,1},{6,2},{7,3},{8,12},{9,13},{10,... | collective-permute-start | bytes 1671176 | tf_op jit(solution)/shard_map/ppermute | solution.py:364
  48.9 22.8 %collective-permute-start.14 = (bf16[128,2176]{1,0:T(8,128)(2,1)}, bf16[128,2176]{1,0:T(8,128)(2,1)}, u32[]{:S(2)}, u32[]{:S(2)}) collective-permute-start(bf16[128,2176]{1,0:T(8,128)(2,1)} %collective-permute-done.11), channel_id=1, source_target_pairs={{8,0},{16,24},{9,1},{17,25},{10,2},{18,26},{11,3},{19,27},{12,4},{... | collective-permute-start | bytes 1671176 | tf_op jit(solution)/shard_map/ppermute | solution.py:384
  50.4 29.7 %collective-permute-start.15 = (bf16[128,2176]{1,0:T(8,128)(2,1)}, bf16[128,2176]{1,0:T(8,128)(2,1)}, u32[]{:S(2)}, u32[]{:S(2)}) collective-permute-start(bf16[128,2176]{1,0:T(8,128)(2,1)} %collective-permute-done.1.refs_4_), channel_id=1, source_target_pairs={{0,8},{8,0},{16,24},{24,16},{1,9},{9,1},{17,25},{25,17},{2,10},{10... | collective-permute-start | bytes 1671176 | tf_op jit(solution)/shard_map/ppermute | solution.py:364
  81.3 5.4 %collective-permute-start.26 = (bf16[128,2176]{1,0:T(8,128)(2,1)S(1)}, bf16[128,2176]{1,0:T(8,128)(2,1)}, u32[]{:S(2)}, u32[]{:S(2)}) collective-permute-start(bf16[128,2176]{1,0:T(8,128)(2,1)S(1)} %broadcast_select_fusion.refs_4_), channel_id=1, source_target_pairs={{0,1},{1,0},{2,3},{3,2},{4,5},{5,4},{6,7},{7,6},{8,9},{9,8},{10,11... | collective-permute-start | bytes 1671176 | tf_op jit(solution)/shard_map/ppermute | solution.py:364
  81.3 6.4 %collective-permute-start.24 = (bf16[128,2176]{1,0:T(8,128)(2,1)S(1)}, bf16[128,2176]{1,0:T(8,128)(2,1)S(1)}, u32[]{:S(2)}, u32[]{:S(2)}) collective-permute-start(bf16[128,2176]{1,0:T(8,128)(2,1)S(1)} %collective-permute-done.12.refs_0_), channel_id=1, source_target_pairs={{0,1},{1,0},{2,3},{3,2},{4,5},{5,4},{6,7},{7,6},{8,9},{9,8},{10,11... | collective-permute-start | bytes 1671176 | tf_op jit(solution)/shard_map/ppermute | solution.py:364
  81.8 6.7 %collective-permute-start.25 = (bf16[128,2176]{1,0:T(8,128)(2,1)}, bf16[128,2176]{1,0:T(8,128)(2,1)S(1)}, u32[]{:S(2)}, u32[]{:S(2)}) collective-permute-start(bf16[128,2176]{1,0:T(8,128)(2,1)} %collective-permute-done.13.refs_2_), channel_id=1, source_target_pairs={{0,1},{1,0},{2,3},{3,2},{4,5},{5,4},{6,7},{7,6},{8,9},{9,8},{10,11... | collective-permute-start | bytes 1671176 | tf_op jit(solution)/shard_map/ppermute | solution.py:364
  81.9 8.4 %collective-permute-start.27 = (bf16[128,2176]{1,0:T(8,128)(2,1)}, bf16[128,2176]{1,0:T(8,128)(2,1)}, u32[]{:S(2)}, u32[]{:S(2)}) collective-permute-start(bf16[128,2176]{1,0:T(8,128)(2,1)} %collective-permute-done.15.refs_6_), channel_id=1, source_target_pairs={{0,1},{1,0},{2,3},{3,2},{4,5},{5,4},{6,7},{7,6},{8,9},{9,8},{10,11... | collective-permute-start | bytes 1671176 | tf_op jit(solution)/shard_map/ppermute | solution.py:364
  82.4 3.8 %collective-permute-start.28 = (bf16[1,128,1024]{2,1,0:T(8,128)(2,1)S(1)}, bf16[1,128,1024]{2,1,0:T(8,128)(2,1)}, u32[]{:S(2)}, u32[]{:S(2)}) collective-permute-start(bf16[1,128,1024]{2,1,0:T(8,128)(2,1)S(1)} %copy-done.25), channel_id=1, source_target_pairs={{0,1},{1,0},{2,3},{3,2},{4,5},{5,4},{6,7},{7,6},{8,9},{9,8},{10,11... | collective-permute-start | bytes 786440 | tf_op jit(solution)/shard_map/ppermute | solution.py:364
  86.2 20.3 %collective-permute-start.20 = (bf16[128,2176]{1,0:T(8,128)(2,1)S(1)}, bf16[128,2176]{1,0:T(8,128)(2,1)S(1)}, u32[]{:S(2)}, u32[]{:S(2)}) collective-permute-start(bf16[128,2176]{1,0:T(8,128)(2,1)S(1)} %broadcast_select_fusion.refs_4_), channel_id=1, source_target_pairs={{0,2},{1,3},{2,0},{3,1},{4,6},{5,7},{6,4},{7,5},{8,10},{9,11},{10,... | collective-permute-start | bytes 1671176 | tf_op jit(solution)/shard_map/ppermute | solution.py:364
  86.7 19.8 %collective-permute-start.21 = (bf16[128,2176]{1,0:T(8,128)(2,1)S(1)}, bf16[128,2176]{1,0:T(8,128)(2,1)S(1)}, u32[]{:S(2)}, u32[]{:S(2)}) collective-permute-start(bf16[128,2176]{1,0:T(8,128)(2,1)S(1)} %broadcast_select_fusion.refs_4_), channel_id=1, source_target_pairs={{0,4},{1,5},{2,6},{3,7},{4,0},{5,1},{6,2},{7,3},{8,12},{9,13},{10,... | collective-permute-start | bytes 1671176 | tf_op jit(solution)/shard_map/ppermute | solution.py:364
  87.7 18.8 %collective-permute-start.22 = (bf16[128,2176]{1,0:T(8,128)(2,1)S(1)}, bf16[128,2176]{1,0:T(8,128)(2,1)}, u32[]{:S(2)}, u32[]{:S(2)}) collective-permute-start(bf16[128,2176]{1,0:T(8,128)(2,1)S(1)} %copy-done.4), channel_id=1, source_target_pairs={{0,8},{8,0},{16,24},{24,16},{1,9},{9,1},{17,25},{25,17},{2,10},{10... | collective-permute-start | bytes 1671176 | tf_op jit(solution)/shard_map/ppermute | solution.py:364
  89.4 23.8 %collective-permute-start.23 = (bf16[128,2176]{1,0:T(8,128)(2,1)S(1)}, bf16[128,2176]{1,0:T(8,128)(2,1)}, u32[]{:S(2)}, u32[]{:S(2)}) collective-permute-start(bf16[128,2176]{1,0:T(8,128)(2,1)S(1)} %collective-permute-done.12.refs_0_), channel_id=1, source_target_pairs={{0,4},{1,5},{2,6},{3,7},{4,0},{5,1},{6,2},{7,3},{8,12},{9,13},{10,... | collective-permute-start | bytes 1671176 | tf_op jit(solution)/shard_map/ppermute | solution.py:364
  113.1 3.9 %collective-permute-start.31 = (bf16[128,2176]{1,0:T(8,128)(2,1)S(1)}, bf16[128,2176]{1,0:T(8,128)(2,1)S(1)}, u32[]{:S(2)}, u32[]{:S(2)}) collective-permute-start(bf16[128,2176]{1,0:T(8,128)(2,1)S(1)} %collective-permute-done.21.refs_2_), channel_id=1, source_target_pairs={{0,1},{1,0},{2,3},{3,2},{4,5},{5,4},{6,7},{7,6},{8,9},{9,8},{10,11... | collective-permute-start | bytes 1671176 | tf_op jit(solution)/shard_map/ppermute | solution.py:364
  113.6 4.5 %collective-permute-start.32 = (bf16[128,2176]{1,0:T(8,128)(2,1)}, bf16[128,2176]{1,0:T(8,128)(2,1)S(1)}, u32[]{:S(2)}, u32[]{:S(2)}) collective-permute-start(bf16[128,2176]{1,0:T(8,128)(2,1)} %collective-permute-done.22.refs_4_), channel_id=1, source_target_pairs={{0,1},{1,0},{2,3},{3,2},{4,5},{5,4},{6,7},{7,6},{8,9},{9,8},{10,11... | collective-permute-start | bytes 1671176 | tf_op jit(solution)/shard_map/ppermute | solution.py:364
  113.6 6.4 %collective-permute-start.33 = (bf16[128,2176]{1,0:T(8,128)(2,1)}, bf16[128,2176]{1,0:T(8,128)(2,1)S(1)}, u32[]{:S(2)}, u32[]{:S(2)}) collective-permute-start(bf16[128,2176]{1,0:T(8,128)(2,1)} %collective-permute-done.23.refs_6_), channel_id=1, source_target_pairs={{0,1},{1,0},{2,3},{3,2},{4,5},{5,4},{6,7},{7,6},{8,9},{9,8},{10,11... | collective-permute-start | bytes 1671176 | tf_op jit(solution)/shard_map/ppermute | solution.py:364
  114.1 26.4 %collective-permute-start.29 = (bf16[128,2176]{1,0:T(8,128)(2,1)S(1)}, bf16[128,2176]{1,0:T(8,128)(2,1)}, u32[]{:S(2)}, u32[]{:S(2)}) collective-permute-start(bf16[128,2176]{1,0:T(8,128)(2,1)S(1)} %collective-permute-done.21.refs_2_), channel_id=1, source_target_pairs={{0,2},{1,3},{2,0},{3,1},{4,6},{5,7},{6,4},{7,5},{8,10},{9,11},{10,... | collective-permute-start | bytes 1671176 | tf_op jit(solution)/shard_map/ppermute | solution.py:364
  116.5 18.8 %collective-permute-start.34 = (bf16[128,1024]{1,0:T(8,128)(2,1)}, bf16[128,1024]{1,0:T(8,128)(2,1)}, u32[]{:S(2)}, u32[]{:S(2)}) collective-permute-start(bf16[128,1024]{1,0:T(8,128)(2,1)} %get-tuple-element.173), channel_id=1, source_target_pairs={{0,2},{1,3},{2,0},{3,1},{4,6},{5,7},{6,4},{7,5},{8,10},{9,11},{10,... | collective-permute-start | bytes 786440 | tf_op jit(solution)/shard_map/ppermute | solution.py:364
  117.0 18.3 %collective-permute-start.35 = (bf16[128,1024]{1,0:T(8,128)(2,1)}, bf16[128,1024]{1,0:T(8,128)(2,1)}, u32[]{:S(2)}, u32[]{:S(2)}) collective-permute-start(bf16[128,1024]{1,0:T(8,128)(2,1)} %get-tuple-element.172), channel_id=1, source_target_pairs={{0,4},{1,5},{2,6},{3,7},{4,0},{5,1},{6,2},{7,3},{8,12},{9,13},{10,... | collective-permute-start | bytes 786440 | tf_op jit(solution)/shard_map/ppermute | solution.py:364
  118.1 22.4 %collective-permute-start.36 = (bf16[128,1024]{1,0:T(8,128)(2,1)}, bf16[128,1024]{1,0:T(8,128)(2,1)}, u32[]{:S(2)}, u32[]{:S(2)}) collective-permute-start(bf16[128,1024]{1,0:T(8,128)(2,1)} %bitcast.5), channel_id=1, source_target_pairs={{0,6},{1,7},{2,4},{3,5},{4,2},{5,3},{6,0},{7,1},{8,14},{9,15},{10,... | collective-permute-start | bytes 786440 | tf_op jit(solution)/shard_map/ppermute | solution.py:364
  (32 other events, 213.6 us)

commit v2 on v1

--- a/solution.py
+++ b/solution.py
@@ -7,7 +7,7 @@
 from jax.sharding import PartitionSpec as P
 
 LANES = 128
-VMEM_BYTES = 60 * 1024 * 1024
+VMEM_BYTES = 26 * 1024 * 1024
 GATHER_BYTES = 48 * 1024 * 1024
 
 
@@ -167,34 +167,26 @@
         return [refs.pop(0) for _ in range(count)]
 
     block_hbm = take(blocks)
-    weight_hbm = take(3)
-    acc_hbm = [] if first else take(3)
-    out_hbm = take(3)
+    gate_ref, up_ref, down_ref = take(3)
+    acc_refs = [] if first else take(3)
+    out_refs = take(3)
     piece_hbm = take(2) if own else []
     block_buf, x_rows, d_rows, hid, both, info = take(6)
-    weight_buf = gate_ref, up_ref, down_ref = take(3)
-    acc_buf = take(3)
-    out_buf = take(3) if last else acc_buf
+    final_buf = take(3) if last else []
     if own:
         back, places, *piece_buf = take(4)
-    block_sem, weight_sem, acc_sem, out_sem, piece_sem = take(5)
+    block_sem, out_sem, piece_sem = take(3)
     held, rows, width = x_rows.shape
     tok_dev = block_buf.shape[1]
     half = tok_dev // 2
     units = hid.shape[1]
     shard = lax.axis_index("dp")
     base = lax.axis_index("expert") * held
-    x_cut = acc_buf[0].shape[1]
-    h_cut = acc_buf[2].shape[1]
-
-    def weight_in(e, m):
-        return pltpu.make_async_copy(weight_hbm[m].at[e], weight_buf[m].at[e], weight_sem.at[m, e])
-
-    def acc_in(e, m):
-        return pltpu.make_async_copy(acc_hbm[m].at[e], acc_buf[m].at[e], acc_sem.at[m, e])
+    x_cut = out_refs[0].shape[1]
+    h_cut = out_refs[2].shape[1]
 
     def grad_out(e, m):
-        return pltpu.make_async_copy(out_buf[m].at[e], out_hbm[m].at[e], out_sem.at[m, e])
+        return pltpu.make_async_copy(final_buf[m].at[e], out_refs[m].at[e], out_sem.at[m, e])
 
     for b in range(blocks):
         pltpu.make_async_copy(block_hbm[b], block_buf.at[b], block_sem.at[b]).start()
@@ -203,12 +195,6 @@
 
     def select(b, _):
         pltpu.make_async_copy(block_hbm[0], block_buf.at[b], block_sem.at[b]).wait()
-
-        @pl.when(b == 1)
-        def _():
-            for m in range(3):
-                weight_in(0, m).start()
-
         info[...] = block_buf[b, :, 2 * width :].astype(jnp.float32)
         picks, scaled = [], []
         for i in range(held):
@@ -236,16 +222,6 @@
     lax.fori_loop(0, blocks, select, 0)
 
     def expert(e, _):
-        for m in range(3):
-            weight_in(e, m).wait()
-        for m in range(len(acc_hbm)):
-            acc_in(e, m).start()
-
-        @pl.when(e + 1 < held)
-        def _():
-            for m in range(3):
-                weight_in(e + 1, m).start()
-
         rows_x = x_rows[e]
         d_out = d_rows[e]
         gate_pre = mul(rows_x, gate_ref[e])
@@ -261,12 +237,12 @@
         grad_both = contract_first(x_part, both[...])
         grads = [grad_both[:, :units], grad_both[:, units:], contract_first(h_part, d_out)]
         for m in range(3):
-            grad = grads[m]
-            if not first:
-                acc_in(e, m).wait()
-                grad = acc_buf[m][e] + grad
-            out_buf[m][e] = grad.astype(out_buf[m].dtype)
-            grad_out(e, m).start()
+            grad = grads[m] if first else acc_refs[m][e] + grads[m]
+            if last:
+                final_buf[m][e] = grad.astype(jnp.bfloat16)
+                grad_out(e, m).start()
+            else:
+                out_refs[m][e] = grad
         if own:
             kept = own * depth
             back[e] = (
@@ -296,9 +272,10 @@
             copy.start()
         for copy in pieces_out:
             copy.wait()
-    for e in range(held):
-        for m in range(3):
-            grad_out(e, m).wait()
+    if last:
+        for e in range(held):
+            for m in range(3):
+                grad_out(e, m).wait()
 
 
 def group(records, weights, accs, shards, depth, last=False, own=0):
@@ -314,7 +291,8 @@
     ]
     args = list(records) + list(weights) + ([] if first else list(accs))
     out_type = jnp.bfloat16 if last else jnp.float32
-    out_shape = [jax.ShapeDtypeStruct(s, out_type) for s in grad_shapes]
+    holder = jax.ShapeDtypeStruct if last else pltpu.VMEM
+    out_shape = [holder(s, out_type) for s in grad_shapes]
     scratch = [
         pltpu.VMEM((blocks, tok_dev, record), jnp.bfloat16),
         pltpu.VMEM((held, rows, width), jnp.bfloat16),
@@ -323,8 +301,6 @@
         pltpu.VMEM((rows, 2 * units), jnp.bfloat16),
         pltpu.VMEM((tok_dev, tok_dev), jnp.float32),
     ]
-    scratch += [pltpu.VMEM(w.shape, jnp.bfloat16) for w in weights]
-    scratch += [pltpu.VMEM(s, jnp.float32) for s in grad_shapes]
     if last:
         scratch += [pltpu.VMEM(s, jnp.bfloat16) for s in grad_shapes]
     if own:
@@ -339,15 +315,16 @@
     scratch += [
         pltpu.SemaphoreType.DMA((blocks,)),
         pltpu.SemaphoreType.DMA((3, held)),
-        pltpu.SemaphoreType.DMA((3, held)),
-        pltpu.SemaphoreType.DMA((3, held)),
         pltpu.SemaphoreType.DMA((2,)),
     ]
+    outside = pl.BlockSpec(memory_space=pltpu.HBM)
+    inside = pl.BlockSpec(memory_space=pltpu.VMEM)
     work = 2 * rows * held * width * units
     return pl.pallas_call(
         functools.partial(group_kernel, first, last, own, depth, blocks),
-        in_specs=[pl.BlockSpec(memory_space=pl.ANY)] * len(args),
-        out_specs=[pl.BlockSpec(memory_space=pl.ANY)] * len(out_shape),
+        in_specs=[outside] * blocks + [inside] * (len(args) - blocks),
+        out_specs=[outside if last else inside] * 3 + [outside] * (len(out_shape) - 3),
+        input_output_aliases={} if first or last else {blocks + 3 + m: m for m in range(3)},
         out_shape=out_shape,
         scratch_shapes=scratch,
         compiler_params=pltpu.CompilerParams(vmem_limit_bytes=VMEM_BYTES),
@@ -359,6 +336,30 @@
     )(*args)
 
 
+def hold_kernel(*refs):
+    sem = refs[-1]
+    count = len(refs) // 2
+    copies = [
+        pltpu.make_async_copy(refs[m], refs[count + m], sem.at[m]) for m in range(count)
+    ]
+    for copy in copies:
+        copy.start()
+    for copy in copies:
+        copy.wait()
+
+
+def hold(*arrays):
+    return pl.pallas_call(
+        hold_kernel,
+        in_specs=[pl.BlockSpec(memory_space=pl.ANY)] * len(arrays),
+        out_specs=[pl.BlockSpec(memory_space=pltpu.VMEM)] * len(arrays),
+        out_shape=[pltpu.VMEM(a.shape, a.dtype) for a in arrays],
+        scratch_shapes=[pltpu.SemaphoreType.DMA((len(arrays),))],
+        compiler_params=pltpu.CompilerParams(vmem_limit_bytes=2 * VMEM_BYTES),
+        cost_estimate=pl.CostEstimate(flops=0, bytes_accessed=2 * 10**6, transcendentals=0),
+    )(*arrays)
+
+
 def swap(value, axis, bit):
     size = lax.axis_size(axis)
     return lax.ppermute(value, axis, [(i, i ^ bit) for i in range(size)])
@@ -388,15 +389,14 @@
     shards = lax.axis_size("dp")
     tok_dev = tokens.shape[0]
     depth = depth_of(tok_dev, routes.shape[1], w_gate.shape[0] * lax.axis_size("expert"))
-    run = functools.partial(
-        group, weights=(w_gate, w_up, w_down), shards=shards, depth=depth
-    )
     tie = lax.optimization_barrier
     inner = jnp.logical_and(lax.axis_index("dp") > 0, lax.axis_index("dp") < shards - 1)
     o0 = pack(tokens, grad_out, routes, combine)
     x0, y0, o1, near = beside(o0), below(o0), swap(o0, "dp", 1), middle(o0)
     group0 = pairs(o0)
-    x0, y0, o1, near, group0 = tie((x0, y0, o1, near, group0))
+    weights = hold(*tie((w_gate, w_up, w_down, o0))[:3])
+    x0, y0, o1, near, group0, weights = tie((x0, y0, o1, near, group0, weights))
+    run = functools.partial(group, weights=weights, shards=shards, depth=depth)
     x1, d0, near_end, far = beside(o1), below(x0), outward(near), middle(o1)
     group0 += pairs(x0, y0, o1)
     y0, near, group0 = tie((y0, near, group0))
@@ -405,32 +405,32 @@
         (x1, d0, near_end, near, far, even0, odd0, y0)
     )
     o2 = jnp.where(inner, near, near_end)
-    x2, y2, far_end, y1 = beside(o2), below(o2), outward(far), swap(y0, "dp", 1)
+    x2, y2, far_end = beside(o2), below(o2), outward(far)
     crossed0 = swap(odd0, "expert", 1)
     group1 = pairs(d0, x1, o2)
     group1, crossed0, d0 = tie((group1, crossed0, d0))
     pair0 = (even0.astype(jnp.float32) + crossed0.astype(jnp.float32)).astype(jnp.bfloat16)
     *accs, even1, odd1 = run(group1, accs=accs, own=2)
-    x2, y2, far_end, y1, far, d0, pair0, even1, odd1 = tie(
-        (x2, y2, far_end, y1, far, d0, pair0, even1, odd1)
+    x2, y2, far_end, y0, far, d0, pair0, even1, odd1 = tie(
+        (x2, y2, far_end, y0, far, d0, pair0, even1, odd1)
     )
     o3 = jnp.where(inner, far, far_end)
-    x3, y3, d1, d2 = beside(o3), below(o3), swap(d0, "dp", 1), below(x2)
+    x3, y3, y1, d2 = beside(o3), below(o3), swap(y0, "dp", 1), below(x2)
     crossed1 = swap(odd1, "expert", 1)
-    group2 = pairs(x2, y2, o3, y1)
+    group2 = pairs(x2, y2, o3)
     group2, crossed1 = tie((group2, crossed1))
     pair1 = (even1.astype(jnp.float32) + crossed1.astype(jnp.float32)).astype(jnp.bfloat16)
     accs = run(group2, accs=accs)
-    x3, y3, d1, d2, accs, pair1 = tie((x3, y3, d1, d2, accs, pair1))
-    d3 = beside(y3)
+    x3, y3, y1, d2, accs, pair1, d0 = tie((x3, y3, y1, d2, accs, pair1, d0))
+    d3, d1 = beside(y3), swap(d0, "dp", 1)
     sent = [beside(pair0[1]), below(pair0[2]), swap(pair1[0], "expert", 6)]
-    group3 = pairs(x3, y3, d1, d2)
+    group3 = pairs(x3, y3, y1, d2)
     accs = run(group3, accs=accs)
-    d3, accs, sent = tie((d3, accs, sent))
+    d3, d1, accs, sent = tie((d3, d1, accs, sent))
     total = pair0[0].astype(jnp.float32)
     for piece in sent:
         total = total + piece.astype(jnp.float32)
-    accs = run(pairs(d3), accs=accs, last=True)
+    accs = run(pairs(d1, d3), accs=accs, last=True)
     return (total.astype(jnp.bfloat16), *accs)
 
 

time: 156 us -> 147 us (0.942)
  Pallas kernels: 73.9 us -> 57.1 us
  local copies, waits for them, and re-layouts: 4.36 us -> 17 us
  other arithmetic: 5.19 us -> 2.45 us
    pallas_call x5, Pallas kernels: 71.9 us -> 53.1 us  [group(): pl.pallas_call(functools.partial(group_kernel, first, last, own, depth, b...]
    unnamed x52 -> x36, local copies, waits for them, and re-layouts: 3.51 us -> 17 us
    ppermute x34, waiting for transfers between devices: 36.5 us -> 30.9 us  [swap(): return lax.ppermute(value, axis, [(i, i ^ bit) for i in range(size)])]
    ppermute x2, waiting for transfers between devices: 2.54 us -> 8.05 us  [outward(): return lax.ppermute(value, 'dp', [(1, 0), (2, 3)])]
    pallas_call x0 -> x1, Pallas kernels: none -> 3.78 us  [hold(): pl.pallas_call(hold_kernel, in_specs=[pl.BlockSpec(memory_space=pl.ANY)]...]
    ppermute x34, starting transfers between devices: 26.5 us -> 24.3 us  [swap(): return lax.ppermute(value, axis, [(i, i ^ bit) for i in range(size)])]
    pallas_call x1, Pallas kernels: 2 us -> 0.19 us  [pack(): pl.pallas_call(pack_kernel, out_shape=jax.ShapeDtypeStruct((tok_dev, 2 *...]
    convert_element_type x1, other arithmetic: 1.72 us -> 0.07 us  [gathered_shards(): (even1.astype(jnp.float32) + crossed1.astype(jnp.float32)).astype(jnp.bfl...]
  transfers between devices with their start and end apart: 38 -> 38, of which waited for: 11 -> 13; matrix products, arithmetic and copies ran while one was open for 3% -> 1% of each run, Pallas kernels for 39% -> 34%
where the time goes in v2:
time: 147 us
  Pallas kernels  57.1 us (39%)
  waiting for transfers between devices  38.9 us (26%)
  starting transfers between devices  30 us (20%)
  local copies, waits for them, and re-layouts  17 us (12%)
  other arithmetic  2.45 us (2%)
    pallas_call x5, Pallas kernels, group(): pl.pallas_call(functools.partial(group_kernel, first, last, own, depth, b...  53.1 us
    ppermute x34, waiting for transfers between devices, swap(): return lax.ppermute(value, axis, [(i, i ^ bit) for i in range(size)])  30.9 us
    ppermute x34, starting transfers between devices, swap(): return lax.ppermute(value, axis, [(i, i ^ bit) for i in range(size)])  24.3 us
    unnamed x36, local copies, waits for them, and re-layouts  17 us
    ppermute x2, waiting for transfers between devices, outward(): return lax.ppermute(value, 'dp', [(1, 0), (2, 3)])  8.05 us
    pallas_call x1, Pallas kernels, hold(): pl.pallas_call(hold_kernel, in_specs=[pl.BlockSpec(memory_space=pl.ANY)]...  3.78 us
    ppermute x2, starting transfers between devices, middle(): return lax.ppermute(value, 'dp', [(1, 2), (2, 1)])  2.99 us
  transfers between devices with their start and end apart: 38, of which 13 were waited for; matrix products, arithmetic and copies ran while one was open for 1% of the time, Pallas kernels for 34%

profile of v2, /device:TPU:0, one launch (start us, length us, event | category | flops | bytes accessed | tf_op | source)
XLA Modules:
  0.0 146.6 jit_solution(7233639162711221650)
XLA Ops:
  4.1 3.0 %collective-permute-start = (bf16[128,2176]{1,0:T(8,128)(2,1)S(1)}, bf16[128,2176]{1,0:T(8,128)(2,1)}, u32[]{:S(2)}, u32[]{:S(2)}) collective-permute-start(bf16[128,2176]{1,0:T(8,128)(2,1)S(1)} %shard_map.102.refs_0_), channel_id=1, source_target_pairs={{0,2},{1,3},{2,0},{3,1},{4,6},{5,7},{6,4},{7,5},{8,10},{9,11},{10,... | collective-permute-start | bytes 1671176 | tf_op jit(solution)/shard_map/ppermute | solution.py:365
  7.1 1.5 %collective-permute-start.1 = (bf16[128,2176]{1,0:T(8,128)(2,1)S(1)}, bf16[128,2176]{1,0:T(8,128)(2,1)}, u32[]{:S(2)}, u32[]{:S(2)}) collective-permute-start(bf16[128,2176]{1,0:T(8,128)(2,1)S(1)} %shard_map.102.refs_0_), channel_id=1, source_target_pairs={{0,4},{1,5},{2,6},{3,7},{4,0},{5,1},{6,2},{7,3},{8,12},{9,13},{10,... | collective-permute-start | bytes 1671176 | tf_op jit(solution)/shard_map/ppermute | solution.py:365
  8.6 1.6 %collective-permute-start.2 = (bf16[128,2176]{1,0:T(8,128)(2,1)S(1)}, bf16[128,2176]{1,0:T(8,128)(2,1)}, u32[]{:S(2)}, u32[]{:S(2)}) collective-permute-start(bf16[128,2176]{1,0:T(8,128)(2,1)S(1)} %shard_map.102.refs_0_), channel_id=1, source_target_pairs={{0,8},{8,0},{16,24},{24,16},{1,9},{9,1},{17,25},{25,17},{2,10},{10... | collective-permute-start | bytes 1671176 | tf_op jit(solution)/shard_map/ppermute | solution.py:365
  10.2 1.5 collective-permute-start.3
  11.7 3.8 %shard_map.103 = (bf16[3,1024,512]{2,1,0:T(8,128)(2,1)S(1)}, bf16[3,1024,512]{2,1,0:T(8,128)(2,1)S(1)}, bf16[3,512,1024]{2,1,0:T(8,128)(2,1)S(1)}) custom-call(bf16[3,1024,512]{2,1,0:T(8,128)(2,1)} %refs_0_, bf16[3,1024,512]{2,1,0:T(8,128)(2,1)} %refs_1_, bf16[3,512,1024]{2,1,0:T(8,128)(2,1)} %refs_2_), custom_call_target="tpu_custom_call" | custom-call | bytes 2000000 | tf_op jit(solution)/shard_map/pallas_call | solution.py:352
  15.5 1.6 %copy-done = bf16[3,1024,512]{2,1,0:T(8,128)(2,1)} copy-done((bf16[3,1024,512]{2,1,0:T(8,128)(2,1)}, bf16[3,1024,512]{2,1,0:T(8,128)(2,1)S(1)}, u32[]{:S(2)}) %copy-start) | copy-done | bytes 3145752
  17.1 1.7 %copy-done.3 = bf16[3,1024,512]{2,1,0:T(8,128)(2,1)} copy-done((bf16[3,1024,512]{2,1,0:T(8,128)(2,1)}, bf16[3,1024,512]{2,1,0:T(8,128)(2,1)S(1)}, u32[]{:S(2)}) %copy-start.3) | copy-done | bytes 3145752
  18.8 1.1 collective-permute-done.refs_2_
  19.8 1.5 collective-permute-done.1.refs_4_
  21.3 1.2 collective-permute-done.2.refs_6_
  23.9 1.5 %collective-permute-start.11 = (bf16[128,2176]{1,0:T(8,128)(2,1)}, bf16[128,2176]{1,0:T(8,128)(2,1)}, u32[]{:S(2)}, u32[]{:S(2)}) collective-permute-start(bf16[128,2176]{1,0:T(8,128)(2,1)} %collective-permute-done.2.refs_6_), channel_id=1, source_target_pairs={{8,16},{16,8},{9,17},{17,9},{10,18},{18,10},{11,19},{19,11},{12,20... | collective-permute-start | bytes 1671176 | tf_op jit(solution)/shard_map/ppermute | solution.py:381
  27.9 1.3 collective-permute-start.7
  29.2 1.9 %copy-done.1 = bf16[3,1024,512]{2,1,0:T(8,128)(2,1)S(1)} copy-done((bf16[3,1024,512]{2,1,0:T(8,128)(2,1)S(1)}, bf16[3,1024,512]{2,1,0:T(8,128)(2,1)}, u32[]{:S(2)}) %copy-start.1) | copy-done | bytes 3145752
  31.1 1.9 %copy-done.4 = bf16[3,1024,512]{2,1,0:T(8,128)(2,1)S(1)} copy-done((bf16[3,1024,512]{2,1,0:T(8,128)(2,1)S(1)}, bf16[3,1024,512]{2,1,0:T(8,128)(2,1)}, u32[]{:S(2)}) %copy-start.4) | copy-done | bytes 3145752
  37.2 14.9 %shard_map.104 = (f32[3,256,512]{2,1,0:T(8,128)S(1)}, f32[3,256,512]{2,1,0:T(8,128)S(1)}, f32[3,128,1024]{2,1,0:T(8,128)S(1)}, bf16[3,128,1024]{2,1,0:T(8,128)(2,1)S(1)}, bf16[3,128,1024]{2,1,0:T(8,128)(2,1)S(1)}) custom-call(bf16[128,2176]{1,0:T(8,128)(2,1)S(1)} %copy-done.7, bf16[128,2176]{1,0:T(8,128)(2,1)S(1)} %copy-done.9, ...), custom_call_target="tpu_custom_call" | custom-call | flops 201326592 | bytes 557056 | tf_op jit(solution)/shard_map/pallas_call | solution.py:323
  52.1 1.1 broadcast_select_fusion.1.refs_4_
  54.4 1.7 %collective-permute-start.12 = (bf16[128,2176]{1,0:T(8,128)(2,1)S(1)}, bf16[128,2176]{1,0:T(8,128)(2,1)S(1)}, u32[]{:S(2)}, u32[]{:S(2)}) collective-permute-start(bf16[128,2176]{1,0:T(8,128)(2,1)S(1)} %broadcast_select_fusion.1.refs_4_), channel_id=1, source_target_pairs={{0,2},{1,3},{2,0},{3,1},{4,6},{5,7},{6,4},{7,5},{8,10},{9,11},{10,... | collective-permute-start | bytes 1671176 | tf_op jit(solution)/shard_map/ppermute | solution.py:365
  56.0 1.5 %collective-permute-start.13 = (bf16[128,2176]{1,0:T(8,128)(2,1)S(1)}, bf16[128,2176]{1,0:T(8,128)(2,1)S(1)}, u32[]{:S(2)}, u32[]{:S(2)}) collective-permute-start(bf16[128,2176]{1,0:T(8,128)(2,1)S(1)} %broadcast_select_fusion.1.refs_4_), channel_id=1, source_target_pairs={{0,4},{1,5},{2,6},{3,7},{4,0},{5,1},{6,2},{7,3},{8,12},{9,13},{10,... | collective-permute-start | bytes 1671176 | tf_op jit(solution)/shard_map/ppermute | solution.py:365
  57.5 1.5 collective-permute-start.14
  59.0 11.8 %shard_map.105 = (f32[3,256,512]{2,1,0:T(8,128)S(1)}, f32[3,256,512]{2,1,0:T(8,128)S(1)}, f32[3,128,1024]{2,1,0:T(8,128)S(1)}, bf16[1,128,1024]{2,1,0:T(8,128)(2,1)S(1)}, bf16[1,128,1024]{2,1,0:T(8,128)(2,1)S(1)}) custom-call(bf16[128,2176]{1,0:T(8,128)(2,1)} %collective-permute-done.6.refs_0_, ...), custom_call_target="tpu_custom_call", output_to_operand_aliasing={{0}: (9, {}), {1}: (10, {}), {2}: (11, {})} | custom-call | flops 150994944 | bytes 557056 | tf_op jit(solution)/shard_map/pallas_call | solution.py:323
  71.2 8.1 %collective-permute-done.14 = bf16[128,2176]{1,0:T(8,128)(2,1)S(1)} collective-permute-done((bf16[128,2176]{1,0:T(8,128)(2,1)}, bf16[128,2176]{1,0:T(8,128)(2,1)S(1)}, u32[]{:S(2)}, u32[]{:S(2)}) %collective-permute-start.14) | collective-permute-done | bytes 557088 | tf_op jit(solution)/shard_map/ppermute | solution.py:385
  80.4 1.5 %collective-permute-start.19 = (bf16[128,2176]{1,0:T(8,128)(2,1)S(1)}, bf16[128,2176]{1,0:T(8,128)(2,1)S(1)}, u32[]{:S(2)}, u32[]{:S(2)}) collective-permute-start(bf16[128,2176]{1,0:T(8,128)(2,1)S(1)} %broadcast_select_fusion.refs_4_), channel_id=1, source_target_pairs={{0,2},{1,3},{2,0},{3,1},{4,6},{5,7},{6,4},{7,5},{8,10},{9,11},{10,... | collective-permute-start | bytes 1671176 | tf_op jit(solution)/shard_map/ppermute | solution.py:365
  82.6 1.5 %collective-permute-start.20 = (bf16[128,2176]{1,0:T(8,128)(2,1)S(1)}, bf16[128,2176]{1,0:T(8,128)(2,1)S(1)}, u32[]{:S(2)}, u32[]{:S(2)}) collective-permute-start(bf16[128,2176]{1,0:T(8,128)(2,1)S(1)} %broadcast_select_fusion.refs_4_), channel_id=1, source_target_pairs={{0,4},{1,5},{2,6},{3,7},{4,0},{5,1},{6,2},{7,3},{8,12},{9,13},{10,... | collective-permute-start | bytes 1671176 | tf_op jit(solution)/shard_map/ppermute | solution.py:365
  85.3 8.7 %shard_map.106 = (f32[3,256,512]{2,1,0:T(8,128)S(1)}, f32[3,256,512]{2,1,0:T(8,128)S(1)}, f32[3,128,1024]{2,1,0:T(8,128)S(1)}) custom-call(bf16[128,2176]{1,0:T(8,128)(2,1)S(1)} %collective-permute-done.12.refs_0_, bf16[128,2176]{1,0:T(8,128)(2,1)S(1)} %collective-permute-done.23.refs_1_, ...), custom_call_target="tpu_custom_call", output_to_operand_aliasing={{0}: (9, {}), {1}: (10, {}), {2}: (11, {})} | custom-call | flops 150994944 | bytes 557056 | tf_op jit(solution)/shard_map/pallas_call | solution.py:323
  95.1 3.0 %collective-permute-done.20.refs_2_ = bf16[128,2176]{1,0:T(8,128)(2,1)S(1)} collective-permute-done((bf16[128,2176]{1,0:T(8,128)(2,1)S(1)}, bf16[128,2176]{1,0:T(8,128)(2,1)S(1)}, u32[]{:S(2)}, u32[]{:S(2)}) %collective-permute-start.20) | collective-permute-done | bytes 557088 | tf_op jit(solution)/shard_map/ppermute | solution.py:365
  98.7 10.5 %collective-permute-done.22.refs_6_ = bf16[128,2176]{1,0:T(8,128)(2,1)S(1)} collective-permute-done((bf16[128,2176]{1,0:T(8,128)(2,1)S(1)}, bf16[128,2176]{1,0:T(8,128)(2,1)S(1)}, u32[]{:S(2)}, u32[]{:S(2)}) %collective-permute-start.22) | collective-permute-done | bytes 557088 | tf_op jit(solution)/shard_map/ppermute | solution.py:365
  110.2 1.5 %collective-permute-start.27 = (bf16[128,2176]{1,0:T(8,128)(2,1)S(1)}, bf16[128,2176]{1,0:T(8,128)(2,1)S(1)}, u32[]{:S(2)}, u32[]{:S(2)}) collective-permute-start(bf16[128,2176]{1,0:T(8,128)(2,1)S(1)} %collective-permute-done.20.refs_2_), channel_id=1, source_target_pairs={{0,2},{1,3},{2,0},{3,1},{4,6},{5,7},{6,4},{7,5},{8,10},{9,11},{10,... | collective-permute-start | bytes 1671176 | tf_op jit(solution)/shard_map/ppermute | solution.py:365
  113.4 1.5 %collective-permute-start.34 = (bf16[128,1024]{1,0:T(8,128)(2,1)S(1)}, bf16[128,1024]{1,0:T(8,128)(2,1)S(1)}, u32[]{:S(2)}, u32[]{:S(2)}) collective-permute-start(bf16[128,1024]{1,0:T(8,128)(2,1)S(1)} %get-tuple-element.190), channel_id=1, source_target_pairs={{0,4},{1,5},{2,6},{3,7},{4,0},{5,1},{6,2},{7,3},{8,12},{9,13},{10,... | collective-permute-start | bytes 786440 | tf_op jit(solution)/shard_map/ppermute | solution.py:365
  116.0 11.0 %shard_map.107 = (f32[3,256,512]{2,1,0:T(8,128)S(1)}, f32[3,256,512]{2,1,0:T(8,128)S(1)}, f32[3,128,1024]{2,1,0:T(8,128)S(1)}) custom-call(bf16[128,2176]{1,0:T(8,128)(2,1)S(1)} %collective-permute-done.19.refs_0_, bf16[128,2176]{1,0:T(8,128)(2,1)S(1)} %collective-permute-done.29.refs_1_, ...), custom_call_target="tpu_custom_call", output_to_operand_aliasing={{0}: (11, {}), {1}: (12, {}), {2}: (13, {})} | custom-call | flops 201326592 | bytes 557056 | tf_op jit(solution)/shard_map/pallas_call | solution.py:323
  127.0 4.3 %collective-permute-done.33 = bf16[128,1024]{1,0:T(8,128)(2,1)S(1)} collective-permute-done((bf16[128,1024]{1,0:T(8,128)(2,1)S(1)}, bf16[128,1024]{1,0:T(8,128)(2,1)S(1)}, u32[]{:S(2)}, u32[]{:S(2)}) %collective-permute-start.33) | collective-permute-done | bytes 262176 | tf_op jit(solution)/shard_map/ppermute | solution.py:365
  131.3 5.6 %collective-permute-done.35 = bf16[128,1024]{1,0:T(8,128)(2,1)S(1)} collective-permute-done((bf16[128,1024]{1,0:T(8,128)(2,1)S(1)}, bf16[128,1024]{1,0:T(8,128)(2,1)S(1)}, u32[]{:S(2)}, u32[]{:S(2)}) %collective-permute-start.35) | collective-permute-done | bytes 262176 | tf_op jit(solution)/shard_map/ppermute | solution.py:365
  139.7 6.7 %shard_map.108 = (bf16[3,256,512]{2,1,0:T(8,128)(2,1)}, bf16[3,256,512]{2,1,0:T(8,128)(2,1)}, bf16[3,128,1024]{2,1,0:T(8,128)(2,1)}) custom-call(bf16[128,2176]{1,0:T(8,128)(2,1)S(1)} %collective-permute-done.28.refs_0_, bf16[128,2176]{1,0:T(8,128)(2,1)S(1)} %collective-permute-done.36.refs_1_, bf16[128,2176]{1,0:T(8,128)(2,1)S(1)} %collective-permute-done.27.refs_2_, ...), custom_call_target="tpu_custom_call" | custom-call | flops 100663296 | bytes 557056 | tf_op jit(solution)/shard_map/pallas_call | solution.py:323
  (93 shorter events, 24.2 us)
Async XLA Ops:
  4.1 15.7 %collective-permute-start = (bf16[128,2176]{1,0:T(8,128)(2,1)S(1)}, bf16[128,2176]{1,0:T(8,128)(2,1)}, u32[]{:S(2)}, u32[]{:S(2)}) collective-permute-start(bf16[128,2176]{1,0:T(8,128)(2,1)S(1)} %shard_map.102.refs_0_), channel_id=1, source_target_pairs={{0,2},{1,3},{2,0},{3,1},{4,6},{5,7},{6,4},{7,5},{8,10},{9,11},{10,... | collective-permute-start | bytes 1671176 | tf_op jit(solution)/shard_map/ppermute | solution.py:365
  7.1 14.2 %collective-permute-start.1 = (bf16[128,2176]{1,0:T(8,128)(2,1)S(1)}, bf16[128,2176]{1,0:T(8,128)(2,1)}, u32[]{:S(2)}, u32[]{:S(2)}) collective-permute-start(bf16[128,2176]{1,0:T(8,128)(2,1)S(1)} %shard_map.102.refs_0_), channel_id=1, source_target_pairs={{0,4},{1,5},{2,6},{3,7},{4,0},{5,1},{6,2},{7,3},{8,12},{9,13},{10,... | collective-permute-start | bytes 1671176 | tf_op jit(solution)/shard_map/ppermute | solution.py:365
  8.6 13.9 %collective-permute-start.2 = (bf16[128,2176]{1,0:T(8,128)(2,1)S(1)}, bf16[128,2176]{1,0:T(8,128)(2,1)}, u32[]{:S(2)}, u32[]{:S(2)}) collective-permute-start(bf16[128,2176]{1,0:T(8,128)(2,1)S(1)} %shard_map.102.refs_0_), channel_id=1, source_target_pairs={{0,8},{8,0},{16,24},{24,16},{1,9},{9,1},{17,25},{25,17},{2,10},{10... | collective-permute-start | bytes 1671176 | tf_op jit(solution)/shard_map/ppermute | solution.py:365
  10.2 12.3 %collective-permute-start.3 = (bf16[128,2176]{1,0:T(8,128)(2,1)S(1)}, bf16[128,2176]{1,0:T(8,128)(2,1)}, u32[]{:S(2)}, u32[]{:S(2)}) collective-permute-start(bf16[128,2176]{1,0:T(8,128)(2,1)S(1)} %shard_map.102.refs_0_), channel_id=1, source_target_pairs={{8,16},{16,8},{9,17},{17,9},{10,18},{18,10},{11,19},{19,11},{12,20... | collective-permute-start | bytes 1671176 | tf_op jit(solution)/shard_map/ppermute | solution.py:381
  11.7 10.9 %collective-permute-start.4 = (bf16[128,2176]{1,0:T(8,128)(2,1)S(1)}, bf16[128,2176]{1,0:T(8,128)(2,1)S(1)}, u32[]{:S(2)}, u32[]{:S(2)}) collective-permute-start(bf16[128,2176]{1,0:T(8,128)(2,1)S(1)} %shard_map.102.refs_0_), channel_id=1, source_target_pairs={{0,1},{1,0},{2,3},{3,2},{4,5},{5,4},{6,7},{7,6},{8,9},{9,8},{10,11... | collective-permute-start | bytes 1671176 | tf_op jit(solution)/shard_map/ppermute | solution.py:365
  23.4 3.8 %collective-permute-start.8 = (bf16[128,2176]{1,0:T(8,128)(2,1)}, bf16[128,2176]{1,0:T(8,128)(2,1)S(1)}, u32[]{:S(2)}, u32[]{:S(2)}) collective-permute-start(bf16[128,2176]{1,0:T(8,128)(2,1)} %collective-permute-done.refs_2_), channel_id=1, source_target_pairs={{0,1},{1,0},{2,3},{3,2},{4,5},{5,4},{6,7},{7,6},{8,9},{9,8},{10,11... | collective-permute-start | bytes 1671176 | tf_op jit(solution)/shard_map/ppermute | solution.py:365
  23.9 5.4 %collective-permute-start.9 = (bf16[128,2176]{1,0:T(8,128)(2,1)}, bf16[128,2176]{1,0:T(8,128)(2,1)}, u32[]{:S(2)}, u32[]{:S(2)}) collective-permute-start(bf16[128,2176]{1,0:T(8,128)(2,1)} %collective-permute-done.1.refs_4_), channel_id=1, source_target_pairs={{0,1},{1,0},{2,3},{3,2},{4,5},{5,4},{6,7},{7,6},{8,9},{9,8},{10,11... | collective-permute-start | bytes 1671176 | tf_op jit(solution)/shard_map/ppermute | solution.py:365
  23.9 28.2 %collective-permute-start.11 = (bf16[128,2176]{1,0:T(8,128)(2,1)}, bf16[128,2176]{1,0:T(8,128)(2,1)}, u32[]{:S(2)}, u32[]{:S(2)}) collective-permute-start(bf16[128,2176]{1,0:T(8,128)(2,1)} %collective-permute-done.2.refs_6_), channel_id=1, source_target_pairs={{8,16},{16,8},{9,17},{17,9},{10,18},{18,10},{11,19},{19,11},{12,20... | collective-permute-start | bytes 1671176 | tf_op jit(solution)/shard_map/ppermute | solution.py:381
  25.4 26.7 %collective-permute-start.5 = (bf16[128,2176]{1,0:T(8,128)(2,1)}, bf16[128,2176]{1,0:T(8,128)(2,1)}, u32[]{:S(2)}, u32[]{:S(2)}) collective-permute-start(bf16[128,2176]{1,0:T(8,128)(2,1)} %collective-permute-done.2.refs_6_), channel_id=1, source_target_pairs={{0,2},{1,3},{2,0},{3,1},{4,6},{5,7},{6,4},{7,5},{8,10},{9,11},{10,... | collective-permute-start | bytes 1671176 | tf_op jit(solution)/shard_map/ppermute | solution.py:365
  26.8 25.4 %collective-permute-start.6 = (bf16[128,2176]{1,0:T(8,128)(2,1)}, bf16[128,2176]{1,0:T(8,128)(2,1)}, u32[]{:S(2)}, u32[]{:S(2)}) collective-permute-start(bf16[128,2176]{1,0:T(8,128)(2,1)} %collective-permute-done.refs_2_), channel_id=1, source_target_pairs={{0,4},{1,5},{2,6},{3,7},{4,0},{5,1},{6,2},{7,3},{8,12},{9,13},{10,... | collective-permute-start | bytes 1671176 | tf_op jit(solution)/shard_map/ppermute | solution.py:365
  27.9 24.2 %collective-permute-start.7 = (bf16[128,2176]{1,0:T(8,128)(2,1)}, bf16[128,2176]{1,0:T(8,128)(2,1)}, u32[]{:S(2)}, u32[]{:S(2)}) collective-permute-start(bf16[128,2176]{1,0:T(8,128)(2,1)} %collective-permute-done.3), channel_id=1, source_target_pairs={{8,0},{16,24},{9,1},{17,25},{10,2},{18,26},{11,3},{19,27},{12,4},{... | collective-permute-start | bytes 1671176 | tf_op jit(solution)/shard_map/ppermute | solution.py:385
  53.5 4.0 %collective-permute-start.15 = (bf16[128,2176]{1,0:T(8,128)(2,1)}, bf16[128,2176]{1,0:T(8,128)(2,1)S(1)}, u32[]{:S(2)}, u32[]{:S(2)}) collective-permute-start(bf16[128,2176]{1,0:T(8,128)(2,1)} %collective-permute-done.6.refs_0_), channel_id=1, source_target_pairs={{0,1},{1,0},{2,3},{3,2},{4,5},{5,4},{6,7},{7,6},{8,9},{9,8},{10,11... | collective-permute-start | bytes 1671176 | tf_op jit(solution)/shard_map/ppermute | solution.py:365
  53.8 5.2 %collective-permute-start.18 = (bf16[3,128,1024]{2,1,0:T(8,128)(2,1)S(1)}, bf16[3,128,1024]{2,1,0:T(8,128)(2,1)S(1)}, u32[]{:S(2)}, u32[]{:S(2)}) collective-permute-start(bf16[3,128,1024]{2,1,0:T(8,128)(2,1)S(1)} %get-tuple-element.130), channel_id=1, source_target_pairs={{0,1},{1,0},{2,3},{3,2},{4,5},{5,4},{6,7},{7,6},{8,9},{9,8},{10,11... | collective-permute-start | bytes 2359304 | tf_op jit(solution)/shard_map/ppermute | solution.py:365
  54.0 5.0 %collective-permute-start.16 = (bf16[128,2176]{1,0:T(8,128)(2,1)}, bf16[128,2176]{1,0:T(8,128)(2,1)S(1)}, u32[]{:S(2)}, u32[]{:S(2)}) collective-permute-start(bf16[128,2176]{1,0:T(8,128)(2,1)} %collective-permute-done.5.refs_2_), channel_id=1, source_target_pairs={{0,1},{1,0},{2,3},{3,2},{4,5},{5,4},{6,7},{7,6},{8,9},{9,8},{10,11... | collective-permute-start | bytes 1671176 | tf_op jit(solution)/shard_map/ppermute | solution.py:365
  54.4 16.9 %collective-permute-start.12 = (bf16[128,2176]{1,0:T(8,128)(2,1)S(1)}, bf16[128,2176]{1,0:T(8,128)(2,1)S(1)}, u32[]{:S(2)}, u32[]{:S(2)}) collective-permute-start(bf16[128,2176]{1,0:T(8,128)(2,1)S(1)} %broadcast_select_fusion.1.refs_4_), channel_id=1, source_target_pairs={{0,2},{1,3},{2,0},{3,1},{4,6},{5,7},{6,4},{7,5},{8,10},{9,11},{10,... | collective-permute-start | bytes 1671176 | tf_op jit(solution)/shard_map/ppermute | solution.py:365
  56.0 15.2 %collective-permute-start.13 = (bf16[128,2176]{1,0:T(8,128)(2,1)S(1)}, bf16[128,2176]{1,0:T(8,128)(2,1)S(1)}, u32[]{:S(2)}, u32[]{:S(2)}) collective-permute-start(bf16[128,2176]{1,0:T(8,128)(2,1)S(1)} %broadcast_select_fusion.1.refs_4_), channel_id=1, source_target_pairs={{0,4},{1,5},{2,6},{3,7},{4,0},{5,1},{6,2},{7,3},{8,12},{9,13},{10,... | collective-permute-start | bytes 1671176 | tf_op jit(solution)/shard_map/ppermute | solution.py:365
  57.5 21.8 %collective-permute-start.14 = (bf16[128,2176]{1,0:T(8,128)(2,1)}, bf16[128,2176]{1,0:T(8,128)(2,1)S(1)}, u32[]{:S(2)}, u32[]{:S(2)}) collective-permute-start(bf16[128,2176]{1,0:T(8,128)(2,1)} %collective-permute-done.11), channel_id=1, source_target_pairs={{8,0},{16,24},{9,1},{17,25},{10,2},{18,26},{11,3},{19,27},{12,4},{... | collective-permute-start | bytes 1671176 | tf_op jit(solution)/shard_map/ppermute | solution.py:385
  79.4 4.7 %collective-permute-start.25 = (bf16[128,2176]{1,0:T(8,128)(2,1)S(1)}, bf16[128,2176]{1,0:T(8,128)(2,1)S(1)}, u32[]{:S(2)}, u32[]{:S(2)}) collective-permute-start(bf16[128,2176]{1,0:T(8,128)(2,1)S(1)} %broadcast_select_fusion.refs_4_), channel_id=1, source_target_pairs={{0,1},{1,0},{2,3},{3,2},{4,5},{5,4},{6,7},{7,6},{8,9},{9,8},{10,11... | collective-permute-start | bytes 1671176 | tf_op jit(solution)/shard_map/ppermute | solution.py:365
  79.4 5.4 %collective-permute-start.23 = (bf16[128,2176]{1,0:T(8,128)(2,1)S(1)}, bf16[128,2176]{1,0:T(8,128)(2,1)S(1)}, u32[]{:S(2)}, u32[]{:S(2)}) collective-permute-start(bf16[128,2176]{1,0:T(8,128)(2,1)S(1)} %collective-permute-done.12.refs_0_), channel_id=1, source_target_pairs={{0,1},{1,0},{2,3},{3,2},{4,5},{5,4},{6,7},{7,6},{8,9},{9,8},{10,11... | collective-permute-start | bytes 1671176 | tf_op jit(solution)/shard_map/ppermute | solution.py:365
  80.0 5.3 %collective-permute-start.24 = (bf16[128,2176]{1,0:T(8,128)(2,1)S(1)}, bf16[128,2176]{1,0:T(8,128)(2,1)S(1)}, u32[]{:S(2)}, u32[]{:S(2)}) collective-permute-start(bf16[128,2176]{1,0:T(8,128)(2,1)S(1)} %collective-permute-done.13.refs_2_), channel_id=1, source_target_pairs={{0,1},{1,0},{2,3},{3,2},{4,5},{5,4},{6,7},{7,6},{8,9},{9,8},{10,11... | collective-permute-start | bytes 1671176 | tf_op jit(solution)/shard_map/ppermute | solution.py:365
  80.4 14.6 %collective-permute-start.19 = (bf16[128,2176]{1,0:T(8,128)(2,1)S(1)}, bf16[128,2176]{1,0:T(8,128)(2,1)S(1)}, u32[]{:S(2)}, u32[]{:S(2)}) collective-permute-start(bf16[128,2176]{1,0:T(8,128)(2,1)S(1)} %broadcast_select_fusion.refs_4_), channel_id=1, source_target_pairs={{0,2},{1,3},{2,0},{3,1},{4,6},{5,7},{6,4},{7,5},{8,10},{9,11},{10,... | collective-permute-start | bytes 1671176 | tf_op jit(solution)/shard_map/ppermute | solution.py:365
  82.6 15.5 %collective-permute-start.20 = (bf16[128,2176]{1,0:T(8,128)(2,1)S(1)}, bf16[128,2176]{1,0:T(8,128)(2,1)S(1)}, u32[]{:S(2)}, u32[]{:S(2)}) collective-permute-start(bf16[128,2176]{1,0:T(8,128)(2,1)S(1)} %broadcast_select_fusion.refs_4_), channel_id=1, source_target_pairs={{0,4},{1,5},{2,6},{3,7},{4,0},{5,1},{6,2},{7,3},{8,12},{9,13},{10,... | collective-permute-start | bytes 1671176 | tf_op jit(solution)/shard_map/ppermute | solution.py:365
  84.1 14.6 %collective-permute-start.21 = (bf16[128,2176]{1,0:T(8,128)(2,1)}, bf16[128,2176]{1,0:T(8,128)(2,1)S(1)}, u32[]{:S(2)}, u32[]{:S(2)}) collective-permute-start(bf16[128,2176]{1,0:T(8,128)(2,1)} %collective-permute-done.1.refs_4_), channel_id=1, source_target_pairs={{0,8},{8,0},{16,24},{24,16},{1,9},{9,1},{17,25},{25,17},{2,10},{10... | collective-permute-start | bytes 1671176 | tf_op jit(solution)/shard_map/ppermute | solution.py:365
  84.8 24.4 %collective-permute-start.22 = (bf16[128,2176]{1,0:T(8,128)(2,1)S(1)}, bf16[128,2176]{1,0:T(8,128)(2,1)S(1)}, u32[]{:S(2)}, u32[]{:S(2)}) collective-permute-start(bf16[128,2176]{1,0:T(8,128)(2,1)S(1)} %collective-permute-done.12.refs_0_), channel_id=1, source_target_pairs={{0,4},{1,5},{2,6},{3,7},{4,0},{5,1},{6,2},{7,3},{8,12},{9,13},{10,... | collective-permute-start | bytes 1671176 | tf_op jit(solution)/shard_map/ppermute | solution.py:365
  109.2 3.2 %collective-permute-start.30 = (bf16[128,2176]{1,0:T(8,128)(2,1)S(1)}, bf16[128,2176]{1,0:T(8,128)(2,1)S(1)}, u32[]{:S(2)}, u32[]{:S(2)}) collective-permute-start(bf16[128,2176]{1,0:T(8,128)(2,1)S(1)} %collective-permute-done.20.refs_2_), channel_id=1, source_target_pairs={{0,1},{1,0},{2,3},{3,2},{4,5},{5,4},{6,7},{7,6},{8,9},{9,8},{10,11... | collective-permute-start | bytes 1671176 | tf_op jit(solution)/shard_map/ppermute | solution.py:365
  109.7 3.7 %collective-permute-start.31 = (bf16[128,2176]{1,0:T(8,128)(2,1)S(1)}, bf16[128,2176]{1,0:T(8,128)(2,1)S(1)}, u32[]{:S(2)}, u32[]{:S(2)}) collective-permute-start(bf16[128,2176]{1,0:T(8,128)(2,1)S(1)} %collective-permute-done.21.refs_4_), channel_id=1, source_target_pairs={{0,1},{1,0},{2,3},{3,2},{4,5},{5,4},{6,7},{7,6},{8,9},{9,8},{10,11... | collective-permute-start | bytes 1671176 | tf_op jit(solution)/shard_map/ppermute | solution.py:365
  109.7 5.3 %collective-permute-start.32 = (bf16[128,2176]{1,0:T(8,128)(2,1)S(1)}, bf16[128,2176]{1,0:T(8,128)(2,1)S(1)}, u32[]{:S(2)}, u32[]{:S(2)}) collective-permute-start(bf16[128,2176]{1,0:T(8,128)(2,1)S(1)} %collective-permute-done.22.refs_6_), channel_id=1, source_target_pairs={{0,1},{1,0},{2,3},{3,2},{4,5},{5,4},{6,7},{7,6},{8,9},{9,8},{10,11... | collective-permute-start | bytes 1671176 | tf_op jit(solution)/shard_map/ppermute | solution.py:365
  110.2 26.7 %collective-permute-start.27 = (bf16[128,2176]{1,0:T(8,128)(2,1)S(1)}, bf16[128,2176]{1,0:T(8,128)(2,1)S(1)}, u32[]{:S(2)}, u32[]{:S(2)}) collective-permute-start(bf16[128,2176]{1,0:T(8,128)(2,1)S(1)} %collective-permute-done.20.refs_2_), channel_id=1, source_target_pairs={{0,2},{1,3},{2,0},{3,1},{4,6},{5,7},{6,4},{7,5},{8,10},{9,11},{10,... | collective-permute-start | bytes 1671176 | tf_op jit(solution)/shard_map/ppermute | solution.py:365
  111.7 25.3 %collective-permute-start.28 = (bf16[128,2176]{1,0:T(8,128)(2,1)}, bf16[128,2176]{1,0:T(8,128)(2,1)S(1)}, u32[]{:S(2)}, u32[]{:S(2)}) collective-permute-start(bf16[128,2176]{1,0:T(8,128)(2,1)} %collective-permute-done.6.refs_0_), channel_id=1, source_target_pairs={{0,8},{8,0},{16,24},{24,16},{1,9},{9,1},{17,25},{25,17},{2,10},{10... | collective-permute-start | bytes 1671176 | tf_op jit(solution)/shard_map/ppermute | solution.py:365
  112.4 18.9 %collective-permute-start.33 = (bf16[128,1024]{1,0:T(8,128)(2,1)S(1)}, bf16[128,1024]{1,0:T(8,128)(2,1)S(1)}, u32[]{:S(2)}, u32[]{:S(2)}) collective-permute-start(bf16[128,1024]{1,0:T(8,128)(2,1)S(1)} %get-tuple-element.191), channel_id=1, source_target_pairs={{0,2},{1,3},{2,0},{3,1},{4,6},{5,7},{6,4},{7,5},{8,10},{9,11},{10,... | collective-permute-start | bytes 786440 | tf_op jit(solution)/shard_map/ppermute | solution.py:365
  113.4 17.9 %collective-permute-start.34 = (bf16[128,1024]{1,0:T(8,128)(2,1)S(1)}, bf16[128,1024]{1,0:T(8,128)(2,1)S(1)}, u32[]{:S(2)}, u32[]{:S(2)}) collective-permute-start(bf16[128,1024]{1,0:T(8,128)(2,1)S(1)} %get-tuple-element.190), channel_id=1, source_target_pairs={{0,4},{1,5},{2,6},{3,7},{4,0},{5,1},{6,2},{7,3},{8,12},{9,13},{10,... | collective-permute-start | bytes 786440 | tf_op jit(solution)/shard_map/ppermute | solution.py:365
  114.9 22.0 %collective-permute-start.35 = (bf16[128,1024]{1,0:T(8,128)(2,1)S(1)}, bf16[128,1024]{1,0:T(8,128)(2,1)S(1)}, u32[]{:S(2)}, u32[]{:S(2)}) collective-permute-start(bf16[128,1024]{1,0:T(8,128)(2,1)S(1)} %bitcast.12), channel_id=1, source_target_pairs={{0,6},{1,7},{2,4},{3,5},{4,2},{5,3},{6,0},{7,1},{8,14},{9,15},{10,... | collective-permute-start | bytes 786440 | tf_op jit(solution)/shard_map/ppermute | solution.py:365
  (24 other events, 87.1 us)

commit v3 on v2

--- a/solution.py
+++ b/solution.py
@@ -155,7 +155,7 @@
     return pl.pallas_call(
         pack_kernel,
         out_shape=jax.ShapeDtypeStruct((tok_dev, 2 * width + tok_dev), jnp.bfloat16),
-        compiler_params=pltpu.CompilerParams(vmem_limit_bytes=VMEM_BYTES),
+        compiler_params=pltpu.CompilerParams(vmem_limit_bytes=2 * VMEM_BYTES),
         cost_estimate=pl.CostEstimate(flops=10**7, bytes_accessed=2 * 10**6, transcendentals=0),
     )(tokens, grad_out, routes.T, combine.T)
 
@@ -360,6 +360,35 @@
     )(*arrays)
 
 
+def choose_kernel(inner_ref, outer_ref, out_ref, sem):
+    place = lax.axis_index("dp")
+    inner = jnp.logical_and(place > 0, place < lax.axis_size("dp") - 1)
+
+    @pl.when(inner)
+    def _():
+        copy = pltpu.make_async_copy(inner_ref, out_ref, sem)
+        copy.start()
+        copy.wait()
+
+    @pl.when(jnp.logical_not(inner))
+    def _():
+        copy = pltpu.make_async_copy(outer_ref, out_ref, sem)
+        copy.start()
+        copy.wait()
+
+
+def choose(inner, outer):
+    return pl.pallas_call(
+        choose_kernel,
+        in_specs=[pl.BlockSpec(memory_space=pltpu.HBM)] * 2,
+        out_specs=pl.BlockSpec(memory_space=pltpu.HBM),
+        out_shape=pltpu.HBM(inner.shape, inner.dtype),
+        scratch_shapes=[pltpu.SemaphoreType.DMA],
+        compiler_params=pltpu.CompilerParams(vmem_limit_bytes=VMEM_BYTES),
+        cost_estimate=pl.CostEstimate(flops=0, bytes_accessed=10**6, transcendentals=0),
+    )(inner, outer)
+
+
 def swap(value, axis, bit):
     size = lax.axis_size(axis)
     return lax.ppermute(value, axis, [(i, i ^ bit) for i in range(size)])
@@ -390,7 +419,6 @@
     tok_dev = tokens.shape[0]
     depth = depth_of(tok_dev, routes.shape[1], w_gate.shape[0] * lax.axis_size("expert"))
     tie = lax.optimization_barrier
-    inner = jnp.logical_and(lax.axis_index("dp") > 0, lax.axis_index("dp") < shards - 1)
     o0 = pack(tokens, grad_out, routes, combine)
     x0, y0, o1, near = beside(o0), below(o0), swap(o0, "dp", 1), middle(o0)
     group0 = pairs(o0)
@@ -404,7 +432,7 @@
     x1, d0, near_end, near, far, even0, odd0, y0 = tie(
         (x1, d0, near_end, near, far, even0, odd0, y0)
     )
-    o2 = jnp.where(inner, near, near_end)
+    o2 = choose(near, near_end)
     x2, y2, far_end = beside(o2), below(o2), outward(far)
     crossed0 = swap(odd0, "expert", 1)
     group1 = pairs(d0, x1, o2)
@@ -414,23 +442,23 @@
     x2, y2, far_end, y0, far, d0, pair0, even1, odd1 = tie(
         (x2, y2, far_end, y0, far, d0, pair0, even1, odd1)
     )
-    o3 = jnp.where(inner, far, far_end)
-    x3, y3, y1, d2 = beside(o3), below(o3), swap(y0, "dp", 1), below(x2)
+    o3 = choose(far, far_end)
+    x3, y3, y1 = beside(o3), below(o3), swap(y0, "dp", 1)
+    sent = [beside(pair0[1]), below(pair0[2])]
     crossed1 = swap(odd1, "expert", 1)
     group2 = pairs(x2, y2, o3)
     group2, crossed1 = tie((group2, crossed1))
     pair1 = (even1.astype(jnp.float32) + crossed1.astype(jnp.float32)).astype(jnp.bfloat16)
     accs = run(group2, accs=accs)
-    x3, y3, y1, d2, accs, pair1, d0 = tie((x3, y3, y1, d2, accs, pair1, d0))
-    d3, d1 = beside(y3), swap(d0, "dp", 1)
-    sent = [beside(pair0[1]), below(pair0[2]), swap(pair1[0], "expert", 6)]
-    group3 = pairs(x3, y3, y1, d2)
-    accs = run(group3, accs=accs)
-    d3, d1, accs, sent = tie((d3, d1, accs, sent))
+    x3, y3, y1, accs, pair1, d0, x2, sent = tie((x3, y3, y1, accs, pair1, d0, x2, sent))
+    d3, d2, d1 = beside(y3), below(x2), swap(d0, "dp", 1)
+    sent.append(swap(pair1[0], "expert", 6))
+    accs = run(pairs(x3, y3, y1), accs=accs)
+    d3, d2, d1, accs, sent = tie((d3, d2, d1, accs, sent))
     total = pair0[0].astype(jnp.float32)
     for piece in sent:
         total = total + piece.astype(jnp.float32)
-    accs = run(pairs(d1, d3), accs=accs, last=True)
+    accs = run(pairs(d1, d2, d3), accs=accs, last=True)
     return (total.astype(jnp.bfloat16), *accs)
 
 

time: 147 us -> 129 us (0.88)
  local copies, waits for them, and re-layouts: 17 us -> 5.41 us
  waiting for transfers between devices: 38.9 us -> 34 us
  starting transfers between devices: 30 us -> 27.8 us
  Pallas kernels: 57.1 us -> 58.6 us
    unnamed x36 -> x12, local copies, waits for them, and re-layouts: 17 us -> 5.38 us
    ppermute x34, waiting for transfers between devices: 30.9 us -> 27.3 us  [swap(): return lax.ppermute(value, axis, [(i, i ^ bit) for i in range(size)])]
    pallas_call x0 -> x2, Pallas kernels: none -> 1.62 us  [choose(): pl.pallas_call(choose_kernel, in_specs=[pl.BlockSpec(memory_space=pltpu.H...]
    ppermute x2, starting transfers between devices: 2.99 us -> 1.37 us  [middle(): return lax.ppermute(value, 'dp', [(1, 2), (2, 1)])]
  transfers between devices with their start and end apart: 38 -> 38, of which waited for: 13 -> 15; matrix products, arithmetic and copies ran while one was open for 1% -> 1% of each run, Pallas kernels for 34% -> 37%
where the time goes in v3:
time: 129 us; the launch traced here: 128 us
  Pallas kernels  58.6 us (45%)
  waiting for transfers between devices  34 us (26%)
  starting transfers between devices  27.8 us (22%)
  local copies, waits for them, and re-layouts  5.41 us (4%)
    pallas_call x5, Pallas kernels, group(): pl.pallas_call(functools.partial(group_kernel, first, last, own, depth, b...  53 us
    ppermute x34, waiting for transfers between devices, swap(): return lax.ppermute(value, axis, [(i, i ^ bit) for i in range(size)])  27.3 us
    ppermute x34, starting transfers between devices, swap(): return lax.ppermute(value, axis, [(i, i ^ bit) for i in range(size)])  23.7 us
    ppermute x2, waiting for transfers between devices, outward(): return lax.ppermute(value, 'dp', [(1, 0), (2, 3)])  6.68 us
    unnamed x12, local copies, waits for them, and re-layouts  5.38 us
    pallas_call x1, Pallas kernels, hold(): pl.pallas_call(hold_kernel, in_specs=[pl.BlockSpec(memory_space=pl.ANY)]...  3.79 us
    ppermute x2, starting transfers between devices, outward(): return lax.ppermute(value, 'dp', [(1, 0), (2, 3)])  2.74 us
  transfers between devices with their start and end apart: 38, of which 15 were waited for; matrix products, arithmetic and copies ran while one was open for 1% of the time, Pallas kernels for 37%

profile of v3, /device:TPU:0, one launch (start us, length us, event | category | flops | bytes accessed | tf_op | source)
XLA Modules:
  0.0 128.1 jit_solution(2584532648945794916)
XLA Ops:
  0.6 0.9 copy-done.2
  1.6 0.9 copy-done.3
  4.1 2.9 %collective-permute-start = (bf16[128,2176]{1,0:T(8,128)(2,1)S(1)}, bf16[128,2176]{1,0:T(8,128)(2,1)S(1)}, u32[]{:S(2)}, u32[]{:S(2)}) collective-permute-start(bf16[128,2176]{1,0:T(8,128)(2,1)S(1)} %shard_map.102.refs_0_), channel_id=1, source_target_pairs={{0,2},{1,3},{2,0},{3,1},{4,6},{5,7},{6,4},{7,5},{8,10},{9,11},{10,... | collective-permute-start | bytes 1671176 | tf_op jit(solution)/shard_map/ppermute | solution.py:394
  7.1 1.5 %collective-permute-start.1 = (bf16[128,2176]{1,0:T(8,128)(2,1)S(1)}, bf16[128,2176]{1,0:T(8,128)(2,1)S(1)}, u32[]{:S(2)}, u32[]{:S(2)}) collective-permute-start(bf16[128,2176]{1,0:T(8,128)(2,1)S(1)} %shard_map.102.refs_0_), channel_id=1, source_target_pairs={{0,4},{1,5},{2,6},{3,7},{4,0},{5,1},{6,2},{7,3},{8,12},{9,13},{10,... | collective-permute-start | bytes 1671176 | tf_op jit(solution)/shard_map/ppermute | solution.py:394
  8.6 1.6 %collective-permute-start.2 = (bf16[128,2176]{1,0:T(8,128)(2,1)S(1)}, bf16[128,2176]{1,0:T(8,128)(2,1)S(1)}, u32[]{:S(2)}, u32[]{:S(2)}) collective-permute-start(bf16[128,2176]{1,0:T(8,128)(2,1)S(1)} %shard_map.102.refs_0_), channel_id=1, source_target_pairs={{0,8},{8,0},{16,24},{24,16},{1,9},{9,1},{17,25},{25,17},{2,10},{10... | collective-permute-start | bytes 1671176 | tf_op jit(solution)/shard_map/ppermute | solution.py:394
  10.9 3.8 %shard_map.103 = (bf16[3,1024,512]{2,1,0:T(8,128)(2,1)S(1)}, bf16[3,1024,512]{2,1,0:T(8,128)(2,1)S(1)}, bf16[3,512,1024]{2,1,0:T(8,128)(2,1)S(1)}) custom-call(bf16[3,1024,512]{2,1,0:T(8,128)(2,1)} %refs_0_, bf16[3,1024,512]{2,1,0:T(8,128)(2,1)} %refs_1_, bf16[3,512,1024]{2,1,0:T(8,128)(2,1)} %refs_2_), custom_call_target="tpu_custom_call" | custom-call | bytes 2000000 | tf_op jit(solution)/shard_map/pallas_call | solution.py:352
  14.7 5.0 %collective-permute-done.refs_2_ = bf16[128,2176]{1,0:T(8,128)(2,1)S(1)} collective-permute-done((bf16[128,2176]{1,0:T(8,128)(2,1)S(1)}, bf16[128,2176]{1,0:T(8,128)(2,1)S(1)}, u32[]{:S(2)}, u32[]{:S(2)}) %collective-permute-start) | collective-permute-done | bytes 557088 | tf_op jit(solution)/shard_map/ppermute | solution.py:394
  19.7 1.5 %collective-permute-done.1.refs_4_ = bf16[128,2176]{1,0:T(8,128)(2,1)S(1)} collective-permute-done((bf16[128,2176]{1,0:T(8,128)(2,1)S(1)}, bf16[128,2176]{1,0:T(8,128)(2,1)S(1)}, u32[]{:S(2)}, u32[]{:S(2)}) %collective-permute-start.1) | collective-permute-done | bytes 557088 | tf_op jit(solution)/shard_map/ppermute | solution.py:394
  21.1 1.2 collective-permute-done.2.refs_6_
  25.1 1.3 collective-permute-start.7
  26.4 15.0 %shard_map.104 = (f32[3,256,512]{2,1,0:T(8,128)S(1)}, f32[3,256,512]{2,1,0:T(8,128)S(1)}, f32[3,128,1024]{2,1,0:T(8,128)S(1)}, bf16[3,128,1024]{2,1,0:T(8,128)(2,1)S(1)}, bf16[3,128,1024]{2,1,0:T(8,128)(2,1)S(1)}) custom-call(bf16[128,2176]{1,0:T(8,128)(2,1)S(1)} %shard_map.102.refs_0_, bf16[128,2176]{1,0:T(8,128)(2,1)} %collective-permute-done.4.refs_1_, ...), custom_call_target="tpu_custom_call" | custom-call | flops 201326592 | bytes 557056 | tf_op jit(solution)/shard_map/pallas_call | solution.py:323
  41.5 4.5 %collective-permute-done.7.outer_ref = bf16[128,2176]{1,0:T(8,128)(2,1)S(1)} collective-permute-done((bf16[128,2176]{1,0:T(8,128)(2,1)S(1)}, bf16[128,2176]{1,0:T(8,128)(2,1)S(1)}, u32[]{:S(2)}, u32[]{:S(2)}) %collective-permute-start.7) | collective-permute-done | bytes 557088 | tf_op jit(solution)/shard_map/ppermute | solution.py:414
  47.9 1.5 %collective-permute-start.12 = (bf16[128,2176]{1,0:T(8,128)(2,1)}, bf16[128,2176]{1,0:T(8,128)(2,1)S(1)}, u32[]{:S(2)}, u32[]{:S(2)}) collective-permute-start(bf16[128,2176]{1,0:T(8,128)(2,1)} %shard_map.105.refs_4_), channel_id=1, source_target_pairs={{0,2},{1,3},{2,0},{3,1},{4,6},{5,7},{6,4},{7,5},{8,10},{9,11},{10,... | collective-permute-start | bytes 1671176 | tf_op jit(solution)/shard_map/ppermute | solution.py:394
  49.4 1.5 %collective-permute-start.13 = (bf16[128,2176]{1,0:T(8,128)(2,1)}, bf16[128,2176]{1,0:T(8,128)(2,1)S(1)}, u32[]{:S(2)}, u32[]{:S(2)}) collective-permute-start(bf16[128,2176]{1,0:T(8,128)(2,1)} %shard_map.105.refs_4_), channel_id=1, source_target_pairs={{0,4},{1,5},{2,6},{3,7},{4,0},{5,1},{6,2},{7,3},{8,12},{9,13},{10,... | collective-permute-start | bytes 1671176 | tf_op jit(solution)/shard_map/ppermute | solution.py:394
  50.9 1.5 %collective-permute-start.14 = (bf16[128,2176]{1,0:T(8,128)(2,1)S(1)}, bf16[128,2176]{1,0:T(8,128)(2,1)S(1)}, u32[]{:S(2)}, u32[]{:S(2)}) collective-permute-start(bf16[128,2176]{1,0:T(8,128)(2,1)S(1)} %collective-permute-done.11.inner_ref), channel_id=1, source_target_pairs={{8,0},{16,24},{9,1},{17,25},{10,2},{18,26},{11,3},{19,27},{12,4},{... | collective-permute-start | bytes 1671176 | tf_op jit(solution)/shard_map/ppermute | solution.py:414
  52.4 1.0 copy-done.1
  53.4 11.3 %shard_map.106 = (f32[3,256,512]{2,1,0:T(8,128)S(1)}, f32[3,256,512]{2,1,0:T(8,128)S(1)}, f32[3,128,1024]{2,1,0:T(8,128)S(1)}, bf16[1,128,1024]{2,1,0:T(8,128)(2,1)S(1)}, bf16[1,128,1024]{2,1,0:T(8,128)(2,1)S(1)}) custom-call(bf16[128,2176]{1,0:T(8,128)(2,1)S(1)} %collective-permute-done.6.refs_0_, ...), custom_call_target="tpu_custom_call", output_to_operand_aliasing={{0}: (9, {}), {1}: (10, {}), {2}: (11, {})} | custom-call | flops 150994944 | bytes 557056 | tf_op jit(solution)/shard_map/pallas_call | solution.py:323
  65.0 2.2 %collective-permute-done.14.outer_ref = bf16[128,2176]{1,0:T(8,128)(2,1)S(1)} collective-permute-done((bf16[128,2176]{1,0:T(8,128)(2,1)S(1)}, bf16[128,2176]{1,0:T(8,128)(2,1)S(1)}, u32[]{:S(2)}, u32[]{:S(2)}) %collective-permute-start.14) | collective-permute-done | bytes 557088 | tf_op jit(solution)/shard_map/ppermute | solution.py:414
  69.2 1.5 %collective-permute-start.19 = (bf16[128,2176]{1,0:T(8,128)(2,1)}, bf16[128,2176]{1,0:T(8,128)(2,1)S(1)}, u32[]{:S(2)}, u32[]{:S(2)}) collective-permute-start(bf16[128,2176]{1,0:T(8,128)(2,1)} %shard_map.107.refs_4_), channel_id=1, source_target_pairs={{0,2},{1,3},{2,0},{3,1},{4,6},{5,7},{6,4},{7,5},{8,10},{9,11},{10,... | collective-permute-start | bytes 1671176 | tf_op jit(solution)/shard_map/ppermute | solution.py:394
  70.7 1.4 %collective-permute-done.25 = bf16[1,128,1024]{2,1,0:T(8,128)(2,1)S(1)} collective-permute-done((bf16[1,128,1024]{2,1,0:T(8,128)(2,1)S(1)}, bf16[1,128,1024]{2,1,0:T(8,128)(2,1)S(1)}, u32[]{:S(2)}, u32[]{:S(2)}) %collective-permute-start.25) | collective-permute-done | bytes 262176 | tf_op jit(solution)/shard_map/ppermute | solution.py:394
  73.4 1.6 %collective-permute-start.26 = (bf16[128,1024]{1,0:T(8,128)(2,1)S(1)}, bf16[128,1024]{1,0:T(8,128)(2,1)S(1)}, u32[]{:S(2)}, u32[]{:S(2)}) collective-permute-start(bf16[128,1024]{1,0:T(8,128)(2,1)S(1)} %get-tuple-element.197), channel_id=1, source_target_pairs={{0,2},{1,3},{2,0},{3,1},{4,6},{5,7},{6,4},{7,5},{8,10},{9,11},{10,... | collective-permute-start | bytes 786440 | tf_op jit(solution)/shard_map/ppermute | solution.py:394
  75.0 1.0 collective-permute-start.27
  76.0 1.1 copy-done
  77.1 8.7 %shard_map.108 = (f32[3,256,512]{2,1,0:T(8,128)S(1)}, f32[3,256,512]{2,1,0:T(8,128)S(1)}, f32[3,128,1024]{2,1,0:T(8,128)S(1)}) custom-call(bf16[128,2176]{1,0:T(8,128)(2,1)S(1)} %collective-permute-done.12.refs_0_, bf16[128,2176]{1,0:T(8,128)(2,1)S(1)} %collective-permute-done.22.refs_1_, ...), custom_call_target="tpu_custom_call", output_to_operand_aliasing={{0}: (9, {}), {1}: (10, {}), {2}: (11, {})} | custom-call | flops 150994944 | bytes 557056 | tf_op jit(solution)/shard_map/pallas_call | solution.py:323
  85.9 3.7 %collective-permute-done.26 = bf16[128,1024]{1,0:T(8,128)(2,1)S(1)} collective-permute-done((bf16[128,1024]{1,0:T(8,128)(2,1)S(1)}, bf16[128,1024]{1,0:T(8,128)(2,1)S(1)}, u32[]{:S(2)}, u32[]{:S(2)}) %collective-permute-start.26) | collective-permute-done | bytes 262176 | tf_op jit(solution)/shard_map/ppermute | solution.py:394
  89.6 3.0 %collective-permute-done.27 = bf16[128,1024]{1,0:T(8,128)(2,1)S(1)} collective-permute-done((bf16[128,1024]{1,0:T(8,128)(2,1)S(1)}, bf16[128,1024]{1,0:T(8,128)(2,1)S(1)}, u32[]{:S(2)}, u32[]{:S(2)}) %collective-permute-start.27) | collective-permute-done | bytes 262176 | tf_op jit(solution)/shard_map/ppermute | solution.py:394
  93.2 1.5 %collective-permute-start.28 = (bf16[128,2176]{1,0:T(8,128)(2,1)S(1)}, bf16[128,2176]{1,0:T(8,128)(2,1)S(1)}, u32[]{:S(2)}, u32[]{:S(2)}) collective-permute-start(bf16[128,2176]{1,0:T(8,128)(2,1)S(1)} %collective-permute-done.20.refs_2_), channel_id=1, source_target_pairs={{0,2},{1,3},{2,0},{3,1},{4,6},{5,7},{6,4},{7,5},{8,10},{9,11},{10,... | collective-permute-start | bytes 1671176 | tf_op jit(solution)/shard_map/ppermute | solution.py:394
  96.1 1.4 %collective-permute-start.34 = (bf16[128,1024]{1,0:T(8,128)(2,1)S(1)}, bf16[128,1024]{1,0:T(8,128)(2,1)S(1)}, u32[]{:S(2)}, u32[]{:S(2)}) collective-permute-start(bf16[128,1024]{1,0:T(8,128)(2,1)S(1)} %bitcast.12), channel_id=1, source_target_pairs={{0,6},{1,7},{2,4},{3,5},{4,2},{5,3},{6,0},{7,1},{8,14},{9,15},{10,... | collective-permute-start | bytes 786440 | tf_op jit(solution)/shard_map/ppermute | solution.py:394
  97.4 8.7 %shard_map.109 = (f32[3,256,512]{2,1,0:T(8,128)S(1)}, f32[3,256,512]{2,1,0:T(8,128)S(1)}, f32[3,128,1024]{2,1,0:T(8,128)S(1)}) custom-call(bf16[128,2176]{1,0:T(8,128)(2,1)S(1)} %collective-permute-done.19.refs_0_, bf16[128,2176]{1,0:T(8,128)(2,1)S(1)} %collective-permute-done.31.refs_1_, ...), custom_call_target="tpu_custom_call", output_to_operand_aliasing={{0}: (9, {}), {1}: (10, {}), {2}: (11, {})} | custom-call | flops 150994944 | bytes 557056 | tf_op jit(solution)/shard_map/pallas_call | solution.py:323
  106.1 8.1 %collective-permute-done.34 = bf16[128,1024]{1,0:T(8,128)(2,1)S(1)} collective-permute-done((bf16[128,1024]{1,0:T(8,128)(2,1)S(1)}, bf16[128,1024]{1,0:T(8,128)(2,1)S(1)}, u32[]{:S(2)}, u32[]{:S(2)}) %collective-permute-start.34) | collective-permute-done | bytes 262176 | tf_op jit(solution)/shard_map/ppermute | solution.py:394
  115.6 0.9 fusion.2
  118.6 9.4 %shard_map.110 = (bf16[3,256,512]{2,1,0:T(8,128)(2,1)}, bf16[3,256,512]{2,1,0:T(8,128)(2,1)}, bf16[3,128,1024]{2,1,0:T(8,128)(2,1)}) custom-call(bf16[128,2176]{1,0:T(8,128)(2,1)S(1)} %collective-permute-done.30.refs_0_, bf16[128,2176]{1,0:T(8,128)(2,1)S(1)} %collective-permute-done.35.refs_1_, bf16[128,2176]{1,0:T(8,128)(2,1)S(1)} %collective-permute-done.29.refs_2_, ...), custom_call_target="tpu_custom_call" | custom-call | flops 150994944 | bytes 557056 | tf_op jit(solution)/shard_map/pallas_call | solution.py:323
  (69 shorter events, 16.1 us)
Async XLA Ops:
  4.1 15.6 %collective-permute-start = (bf16[128,2176]{1,0:T(8,128)(2,1)S(1)}, bf16[128,2176]{1,0:T(8,128)(2,1)S(1)}, u32[]{:S(2)}, u32[]{:S(2)}) collective-permute-start(bf16[128,2176]{1,0:T(8,128)(2,1)S(1)} %shard_map.102.refs_0_), channel_id=1, source_target_pairs={{0,2},{1,3},{2,0},{3,1},{4,6},{5,7},{6,4},{7,5},{8,10},{9,11},{10,... | collective-permute-start | bytes 1671176 | tf_op jit(solution)/shard_map/ppermute | solution.py:394
  7.1 14.1 %collective-permute-start.1 = (bf16[128,2176]{1,0:T(8,128)(2,1)S(1)}, bf16[128,2176]{1,0:T(8,128)(2,1)S(1)}, u32[]{:S(2)}, u32[]{:S(2)}) collective-permute-start(bf16[128,2176]{1,0:T(8,128)(2,1)S(1)} %shard_map.102.refs_0_), channel_id=1, source_target_pairs={{0,4},{1,5},{2,6},{3,7},{4,0},{5,1},{6,2},{7,3},{8,12},{9,13},{10,... | collective-permute-start | bytes 1671176 | tf_op jit(solution)/shard_map/ppermute | solution.py:394
  8.6 13.8 %collective-permute-start.2 = (bf16[128,2176]{1,0:T(8,128)(2,1)S(1)}, bf16[128,2176]{1,0:T(8,128)(2,1)S(1)}, u32[]{:S(2)}, u32[]{:S(2)}) collective-permute-start(bf16[128,2176]{1,0:T(8,128)(2,1)S(1)} %shard_map.102.refs_0_), channel_id=1, source_target_pairs={{0,8},{8,0},{16,24},{24,16},{1,9},{9,1},{17,25},{25,17},{2,10},{10... | collective-permute-start | bytes 1671176 | tf_op jit(solution)/shard_map/ppermute | solution.py:394
  10.1 12.2 %collective-permute-start.3 = (bf16[128,2176]{1,0:T(8,128)(2,1)S(1)}, bf16[128,2176]{1,0:T(8,128)(2,1)S(1)}, u32[]{:S(2)}, u32[]{:S(2)}) collective-permute-start(bf16[128,2176]{1,0:T(8,128)(2,1)S(1)} %shard_map.102.refs_0_), channel_id=1, source_target_pairs={{8,16},{16,8},{9,17},{17,9},{10,18},{18,10},{11,19},{19,11},{12,20... | collective-permute-start | bytes 1671176 | tf_op jit(solution)/shard_map/ppermute | solution.py:410
  10.8 11.5 %collective-permute-start.4 = (bf16[128,2176]{1,0:T(8,128)(2,1)S(1)}, bf16[128,2176]{1,0:T(8,128)(2,1)}, u32[]{:S(2)}, u32[]{:S(2)}) collective-permute-start(bf16[128,2176]{1,0:T(8,128)(2,1)S(1)} %shard_map.102.refs_0_), channel_id=1, source_target_pairs={{0,1},{1,0},{2,3},{3,2},{4,5},{5,4},{6,7},{7,6},{8,9},{9,8},{10,11... | collective-permute-start | bytes 1671176 | tf_op jit(solution)/shard_map/ppermute | solution.py:394
  22.9 3.5 %collective-permute-start.9 = (bf16[128,2176]{1,0:T(8,128)(2,1)S(1)}, bf16[128,2176]{1,0:T(8,128)(2,1)S(1)}, u32[]{:S(2)}, u32[]{:S(2)}) collective-permute-start(bf16[128,2176]{1,0:T(8,128)(2,1)S(1)} %collective-permute-done.1.refs_4_), channel_id=1, source_target_pairs={{0,1},{1,0},{2,3},{3,2},{4,5},{5,4},{6,7},{7,6},{8,9},{9,8},{10,11... | collective-permute-start | bytes 1671176 | tf_op jit(solution)/shard_map/ppermute | solution.py:394
  23.0 18.5 %collective-permute-start.11 = (bf16[128,2176]{1,0:T(8,128)(2,1)S(1)}, bf16[128,2176]{1,0:T(8,128)(2,1)S(1)}, u32[]{:S(2)}, u32[]{:S(2)}) collective-permute-start(bf16[128,2176]{1,0:T(8,128)(2,1)S(1)} %collective-permute-done.2.refs_6_), channel_id=1, source_target_pairs={{8,16},{16,8},{9,17},{17,9},{10,18},{18,10},{11,19},{19,11},{12,20... | collective-permute-start | bytes 1671176 | tf_op jit(solution)/shard_map/ppermute | solution.py:410
  23.7 17.8 %collective-permute-start.5 = (bf16[128,2176]{1,0:T(8,128)(2,1)S(1)}, bf16[128,2176]{1,0:T(8,128)(2,1)S(1)}, u32[]{:S(2)}, u32[]{:S(2)}) collective-permute-start(bf16[128,2176]{1,0:T(8,128)(2,1)S(1)} %collective-permute-done.2.refs_6_), channel_id=1, source_target_pairs={{0,2},{1,3},{2,0},{3,1},{4,6},{5,7},{6,4},{7,5},{8,10},{9,11},{10,... | collective-permute-start | bytes 1671176 | tf_op jit(solution)/shard_map/ppermute | solution.py:394
  24.3 17.1 %collective-permute-start.6 = (bf16[128,2176]{1,0:T(8,128)(2,1)S(1)}, bf16[128,2176]{1,0:T(8,128)(2,1)S(1)}, u32[]{:S(2)}, u32[]{:S(2)}) collective-permute-start(bf16[128,2176]{1,0:T(8,128)(2,1)S(1)} %collective-permute-done.refs_2_), channel_id=1, source_target_pairs={{0,4},{1,5},{2,6},{3,7},{4,0},{5,1},{6,2},{7,3},{8,12},{9,13},{10,... | collective-permute-start | bytes 1671176 | tf_op jit(solution)/shard_map/ppermute | solution.py:394
  25.1 20.8 %collective-permute-start.7 = (bf16[128,2176]{1,0:T(8,128)(2,1)S(1)}, bf16[128,2176]{1,0:T(8,128)(2,1)S(1)}, u32[]{:S(2)}, u32[]{:S(2)}) collective-permute-start(bf16[128,2176]{1,0:T(8,128)(2,1)S(1)} %collective-permute-done.3.inner_ref), channel_id=1, source_target_pairs={{8,0},{16,24},{9,1},{17,25},{10,2},{18,26},{11,3},{19,27},{12,4},{... | collective-permute-start | bytes 1671176 | tf_op jit(solution)/shard_map/ppermute | solution.py:414
  46.9 4.0 %collective-permute-start.15 = (bf16[128,2176]{1,0:T(8,128)(2,1)S(1)}, bf16[128,2176]{1,0:T(8,128)(2,1)S(1)}, u32[]{:S(2)}, u32[]{:S(2)}) collective-permute-start(bf16[128,2176]{1,0:T(8,128)(2,1)S(1)} %collective-permute-done.6.refs_0_), channel_id=1, source_target_pairs={{0,1},{1,0},{2,3},{3,2},{4,5},{5,4},{6,7},{7,6},{8,9},{9,8},{10,11... | collective-permute-start | bytes 1671176 | tf_op jit(solution)/shard_map/ppermute | solution.py:394
  47.4 5.0 %collective-permute-start.18 = (bf16[3,128,1024]{2,1,0:T(8,128)(2,1)S(1)}, bf16[3,128,1024]{2,1,0:T(8,128)(2,1)S(1)}, u32[]{:S(2)}, u32[]{:S(2)}) collective-permute-start(bf16[3,128,1024]{2,1,0:T(8,128)(2,1)S(1)} %get-tuple-element.133), channel_id=1, source_target_pairs={{0,1},{1,0},{2,3},{3,2},{4,5},{5,4},{6,7},{7,6},{8,9},{9,8},{10,11... | collective-permute-start | bytes 2359304 | tf_op jit(solution)/shard_map/ppermute | solution.py:394
  47.4 4.9 %collective-permute-start.16 = (bf16[128,2176]{1,0:T(8,128)(2,1)S(1)}, bf16[128,2176]{1,0:T(8,128)(2,1)S(1)}, u32[]{:S(2)}, u32[]{:S(2)}) collective-permute-start(bf16[128,2176]{1,0:T(8,128)(2,1)S(1)} %collective-permute-done.5.refs_2_), channel_id=1, source_target_pairs={{0,1},{1,0},{2,3},{3,2},{4,5},{5,4},{6,7},{7,6},{8,9},{9,8},{10,11... | collective-permute-start | bytes 1671176 | tf_op jit(solution)/shard_map/ppermute | solution.py:394
  47.9 17.2 %collective-permute-start.12 = (bf16[128,2176]{1,0:T(8,128)(2,1)}, bf16[128,2176]{1,0:T(8,128)(2,1)S(1)}, u32[]{:S(2)}, u32[]{:S(2)}) collective-permute-start(bf16[128,2176]{1,0:T(8,128)(2,1)} %shard_map.105.refs_4_), channel_id=1, source_target_pairs={{0,2},{1,3},{2,0},{3,1},{4,6},{5,7},{6,4},{7,5},{8,10},{9,11},{10,... | collective-permute-start | bytes 1671176 | tf_op jit(solution)/shard_map/ppermute | solution.py:394
  49.4 15.7 %collective-permute-start.13 = (bf16[128,2176]{1,0:T(8,128)(2,1)}, bf16[128,2176]{1,0:T(8,128)(2,1)S(1)}, u32[]{:S(2)}, u32[]{:S(2)}) collective-permute-start(bf16[128,2176]{1,0:T(8,128)(2,1)} %shard_map.105.refs_4_), channel_id=1, source_target_pairs={{0,4},{1,5},{2,6},{3,7},{4,0},{5,1},{6,2},{7,3},{8,12},{9,13},{10,... | collective-permute-start | bytes 1671176 | tf_op jit(solution)/shard_map/ppermute | solution.py:394
  50.9 16.4 %collective-permute-start.14 = (bf16[128,2176]{1,0:T(8,128)(2,1)S(1)}, bf16[128,2176]{1,0:T(8,128)(2,1)S(1)}, u32[]{:S(2)}, u32[]{:S(2)}) collective-permute-start(bf16[128,2176]{1,0:T(8,128)(2,1)S(1)} %collective-permute-done.11.inner_ref), channel_id=1, source_target_pairs={{8,0},{16,24},{9,1},{17,25},{10,2},{18,26},{11,3},{19,27},{12,4},{... | collective-permute-start | bytes 1671176 | tf_op jit(solution)/shard_map/ppermute | solution.py:414
  68.1 4.8 %collective-permute-start.24 = (bf16[128,2176]{1,0:T(8,128)(2,1)}, bf16[128,2176]{1,0:T(8,128)(2,1)S(1)}, u32[]{:S(2)}, u32[]{:S(2)}) collective-permute-start(bf16[128,2176]{1,0:T(8,128)(2,1)} %shard_map.107.refs_4_), channel_id=1, source_target_pairs={{0,1},{1,0},{2,3},{3,2},{4,5},{5,4},{6,7},{7,6},{8,9},{9,8},{10,11... | collective-permute-start | bytes 1671176 | tf_op jit(solution)/shard_map/ppermute | solution.py:394
  68.2 5.2 %collective-permute-start.22 = (bf16[128,2176]{1,0:T(8,128)(2,1)S(1)}, bf16[128,2176]{1,0:T(8,128)(2,1)S(1)}, u32[]{:S(2)}, u32[]{:S(2)}) collective-permute-start(bf16[128,2176]{1,0:T(8,128)(2,1)S(1)} %collective-permute-done.12.refs_0_), channel_id=1, source_target_pairs={{0,1},{1,0},{2,3},{3,2},{4,5},{5,4},{6,7},{7,6},{8,9},{9,8},{10,11... | collective-permute-start | bytes 1671176 | tf_op jit(solution)/shard_map/ppermute | solution.py:394
  68.7 6.3 %collective-permute-start.23 = (bf16[128,2176]{1,0:T(8,128)(2,1)S(1)}, bf16[128,2176]{1,0:T(8,128)(2,1)S(1)}, u32[]{:S(2)}, u32[]{:S(2)}) collective-permute-start(bf16[128,2176]{1,0:T(8,128)(2,1)S(1)} %collective-permute-done.13.refs_2_), channel_id=1, source_target_pairs={{0,1},{1,0},{2,3},{3,2},{4,5},{5,4},{6,7},{7,6},{8,9},{9,8},{10,11... | collective-permute-start | bytes 1671176 | tf_op jit(solution)/shard_map/ppermute | solution.py:394
  68.7 3.3 %collective-permute-start.25 = (bf16[1,128,1024]{2,1,0:T(8,128)(2,1)S(1)}, bf16[1,128,1024]{2,1,0:T(8,128)(2,1)S(1)}, u32[]{:S(2)}, u32[]{:S(2)}) collective-permute-start(bf16[1,128,1024]{2,1,0:T(8,128)(2,1)S(1)} %get-tuple-element.154), channel_id=1, source_target_pairs={{0,1},{1,0},{2,3},{3,2},{4,5},{5,4},{6,7},{7,6},{8,9},{9,8},{10,11... | collective-permute-start | bytes 786440 | tf_op jit(solution)/shard_map/ppermute | solution.py:394
  69.2 23.4 %collective-permute-start.19 = (bf16[128,2176]{1,0:T(8,128)(2,1)}, bf16[128,2176]{1,0:T(8,128)(2,1)S(1)}, u32[]{:S(2)}, u32[]{:S(2)}) collective-permute-start(bf16[128,2176]{1,0:T(8,128)(2,1)} %shard_map.107.refs_4_), channel_id=1, source_target_pairs={{0,2},{1,3},{2,0},{3,1},{4,6},{5,7},{6,4},{7,5},{8,10},{9,11},{10,... | collective-permute-start | bytes 1671176 | tf_op jit(solution)/shard_map/ppermute | solution.py:394
  72.1 20.5 %collective-permute-start.20 = (bf16[128,2176]{1,0:T(8,128)(2,1)}, bf16[128,2176]{1,0:T(8,128)(2,1)S(1)}, u32[]{:S(2)}, u32[]{:S(2)}) collective-permute-start(bf16[128,2176]{1,0:T(8,128)(2,1)} %shard_map.107.refs_4_), channel_id=1, source_target_pairs={{0,4},{1,5},{2,6},{3,7},{4,0},{5,1},{6,2},{7,3},{8,12},{9,13},{10,... | collective-permute-start | bytes 1671176 | tf_op jit(solution)/shard_map/ppermute | solution.py:394
  72.9 19.7 %collective-permute-start.21 = (bf16[128,2176]{1,0:T(8,128)(2,1)S(1)}, bf16[128,2176]{1,0:T(8,128)(2,1)S(1)}, u32[]{:S(2)}, u32[]{:S(2)}) collective-permute-start(bf16[128,2176]{1,0:T(8,128)(2,1)S(1)} %collective-permute-done.1.refs_4_), channel_id=1, source_target_pairs={{0,8},{8,0},{16,24},{24,16},{1,9},{9,1},{17,25},{25,17},{2,10},{10... | collective-permute-start | bytes 1671176 | tf_op jit(solution)/shard_map/ppermute | solution.py:394
  73.4 16.2 %collective-permute-start.26 = (bf16[128,1024]{1,0:T(8,128)(2,1)S(1)}, bf16[128,1024]{1,0:T(8,128)(2,1)S(1)}, u32[]{:S(2)}, u32[]{:S(2)}) collective-permute-start(bf16[128,1024]{1,0:T(8,128)(2,1)S(1)} %get-tuple-element.197), channel_id=1, source_target_pairs={{0,2},{1,3},{2,0},{3,1},{4,6},{5,7},{6,4},{7,5},{8,10},{9,11},{10,... | collective-permute-start | bytes 786440 | tf_op jit(solution)/shard_map/ppermute | solution.py:394
  75.0 17.6 %collective-permute-start.27 = (bf16[128,1024]{1,0:T(8,128)(2,1)S(1)}, bf16[128,1024]{1,0:T(8,128)(2,1)S(1)}, u32[]{:S(2)}, u32[]{:S(2)}) collective-permute-start(bf16[128,1024]{1,0:T(8,128)(2,1)S(1)} %get-tuple-element.196), channel_id=1, source_target_pairs={{0,4},{1,5},{2,6},{3,7},{4,0},{5,1},{6,2},{7,3},{8,12},{9,13},{10,... | collective-permute-start | bytes 786440 | tf_op jit(solution)/shard_map/ppermute | solution.py:394
  92.7 3.4 %collective-permute-start.32 = (bf16[128,2176]{1,0:T(8,128)(2,1)S(1)}, bf16[128,2176]{1,0:T(8,128)(2,1)S(1)}, u32[]{:S(2)}, u32[]{:S(2)}) collective-permute-start(bf16[128,2176]{1,0:T(8,128)(2,1)S(1)} %collective-permute-done.20.refs_2_), channel_id=1, source_target_pairs={{0,1},{1,0},{2,3},{3,2},{4,5},{5,4},{6,7},{7,6},{8,9},{9,8},{10,11... | collective-permute-start | bytes 1671176 | tf_op jit(solution)/shard_map/ppermute | solution.py:394
  93.2 4.3 %collective-permute-start.33 = (bf16[128,2176]{1,0:T(8,128)(2,1)S(1)}, bf16[128,2176]{1,0:T(8,128)(2,1)S(1)}, u32[]{:S(2)}, u32[]{:S(2)}) collective-permute-start(bf16[128,2176]{1,0:T(8,128)(2,1)S(1)} %collective-permute-done.21.refs_4_), channel_id=1, source_target_pairs={{0,1},{1,0},{2,3},{3,2},{4,5},{5,4},{6,7},{7,6},{8,9},{9,8},{10,11... | collective-permute-start | bytes 1671176 | tf_op jit(solution)/shard_map/ppermute | solution.py:394
  93.2 21.0 %collective-permute-start.28 = (bf16[128,2176]{1,0:T(8,128)(2,1)S(1)}, bf16[128,2176]{1,0:T(8,128)(2,1)S(1)}, u32[]{:S(2)}, u32[]{:S(2)}) collective-permute-start(bf16[128,2176]{1,0:T(8,128)(2,1)S(1)} %collective-permute-done.20.refs_2_), channel_id=1, source_target_pairs={{0,2},{1,3},{2,0},{3,1},{4,6},{5,7},{6,4},{7,5},{8,10},{9,11},{10,... | collective-permute-start | bytes 1671176 | tf_op jit(solution)/shard_map/ppermute | solution.py:394
  94.7 20.3 %collective-permute-start.29 = (bf16[128,2176]{1,0:T(8,128)(2,1)S(1)}, bf16[128,2176]{1,0:T(8,128)(2,1)S(1)}, u32[]{:S(2)}, u32[]{:S(2)}) collective-permute-start(bf16[128,2176]{1,0:T(8,128)(2,1)S(1)} %collective-permute-done.12.refs_0_), channel_id=1, source_target_pairs={{0,4},{1,5},{2,6},{3,7},{4,0},{5,1},{6,2},{7,3},{8,12},{9,13},{10,... | collective-permute-start | bytes 1671176 | tf_op jit(solution)/shard_map/ppermute | solution.py:394
  95.6 19.5 %collective-permute-start.30 = (bf16[128,2176]{1,0:T(8,128)(2,1)S(1)}, bf16[128,2176]{1,0:T(8,128)(2,1)S(1)}, u32[]{:S(2)}, u32[]{:S(2)}) collective-permute-start(bf16[128,2176]{1,0:T(8,128)(2,1)S(1)} %collective-permute-done.6.refs_0_), channel_id=1, source_target_pairs={{0,8},{8,0},{16,24},{24,16},{1,9},{9,1},{17,25},{25,17},{2,10},{10... | collective-permute-start | bytes 1671176 | tf_op jit(solution)/shard_map/ppermute | solution.py:394
  96.1 18.1 %collective-permute-start.34 = (bf16[128,1024]{1,0:T(8,128)(2,1)S(1)}, bf16[128,1024]{1,0:T(8,128)(2,1)S(1)}, u32[]{:S(2)}, u32[]{:S(2)}) collective-permute-start(bf16[128,1024]{1,0:T(8,128)(2,1)S(1)} %bitcast.12), channel_id=1, source_target_pairs={{0,6},{1,7},{2,4},{3,5},{4,2},{5,3},{6,0},{7,1},{8,14},{9,15},{10,... | collective-permute-start | bytes 786440 | tf_op jit(solution)/shard_map/ppermute | solution.py:394
  115.6 3.0 %collective-permute-start.37 = (bf16[128,2176]{1,0:T(8,128)(2,1)S(1)}, bf16[128,2176]{1,0:T(8,128)(2,1)S(1)}, u32[]{:S(2)}, u32[]{:S(2)}) collective-permute-start(bf16[128,2176]{1,0:T(8,128)(2,1)S(1)} %collective-permute-done.28.refs_4_), channel_id=1, source_target_pairs={{0,1},{1,0},{2,3},{3,2},{4,5},{5,4},{6,7},{7,6},{8,9},{9,8},{10,11... | collective-permute-start | bytes 1671176 | tf_op jit(solution)/shard_map/ppermute | solution.py:394
  (12 other events, 20.4 us)

commit v4 on v3

--- a/solution.py
+++ b/solution.py
@@ -155,7 +155,7 @@
     return pl.pallas_call(
         pack_kernel,
         out_shape=jax.ShapeDtypeStruct((tok_dev, 2 * width + tok_dev), jnp.bfloat16),
-        compiler_params=pltpu.CompilerParams(vmem_limit_bytes=2 * VMEM_BYTES),
+        compiler_params=pltpu.CompilerParams(vmem_limit_bytes=60 * 1024 * 1024),
         cost_estimate=pl.CostEstimate(flops=10**7, bytes_accessed=2 * 10**6, transcendentals=0),
     )(tokens, grad_out, routes.T, combine.T)
 
@@ -255,6 +255,11 @@
 
     if own:
 
+        def piece_out(odd, p):
+            return pltpu.make_async_copy(
+                piece_buf[odd].at[p], piece_hbm[odd].at[p], piece_sem.at[odd, p]
+            )
+
         def collect(p, _):
             for odd in range(2):
                 at = pl.ds(pl.multiple_of((2 * p + odd) * depth, depth), depth)
@@ -262,16 +267,13 @@
                 piece_buf[odd][p] = contract_first(places[2 * p + odd], rows_b).astype(
                     jnp.bfloat16
                 )
+                piece_out(odd, p).start()
             return 0
 
         lax.fori_loop(0, own // 2, collect, 0)
-        pieces_out = [
-            pltpu.make_async_copy(piece_buf[m], piece_hbm[m], piece_sem.at[m]) for m in range(2)
-        ]
-        for copy in pieces_out:
-            copy.start()
-        for copy in pieces_out:
-            copy.wait()
+        for p in range(own // 2):
+            for odd in range(2):
+                piece_out(odd, p).wait()
     if last:
         for e in range(held):
             for m in range(3):
@@ -315,7 +317,7 @@
     scratch += [
         pltpu.SemaphoreType.DMA((blocks,)),
         pltpu.SemaphoreType.DMA((3, held)),
-        pltpu.SemaphoreType.DMA((2,)),
+        pltpu.SemaphoreType.DMA((2, max(own // 2, 1))),
     ]
     outside = pl.BlockSpec(memory_space=pltpu.HBM)
     inside = pl.BlockSpec(memory_space=pltpu.VMEM)
@@ -436,29 +438,30 @@
     x2, y2, far_end = beside(o2), below(o2), outward(far)
     crossed0 = swap(odd0, "expert", 1)
     group1 = pairs(d0, x1, o2)
-    group1, crossed0, d0 = tie((group1, crossed0, d0))
     pair0 = (even0.astype(jnp.float32) + crossed0.astype(jnp.float32)).astype(jnp.bfloat16)
+    group1, pair0, d0 = tie((group1, pair0, d0))
+    sent = [beside(pair0[1]), below(pair0[2])]
     *accs, even1, odd1 = run(group1, accs=accs, own=2)
-    x2, y2, far_end, y0, far, d0, pair0, even1, odd1 = tie(
-        (x2, y2, far_end, y0, far, d0, pair0, even1, odd1)
+    x2, y2, far_end, y0, far, d0, even1, odd1, sent = tie(
+        (x2, y2, far_end, y0, far, d0, even1, odd1, sent)
     )
     o3 = choose(far, far_end)
     x3, y3, y1 = beside(o3), below(o3), swap(y0, "dp", 1)
-    sent = [beside(pair0[1]), below(pair0[2])]
     crossed1 = swap(odd1, "expert", 1)
     group2 = pairs(x2, y2, o3)
     group2, crossed1 = tie((group2, crossed1))
     pair1 = (even1.astype(jnp.float32) + crossed1.astype(jnp.float32)).astype(jnp.bfloat16)
     accs = run(group2, accs=accs)
-    x3, y3, y1, accs, pair1, d0, x2, sent = tie((x3, y3, y1, accs, pair1, d0, x2, sent))
+    x3, y3, y1, accs, pair1, d0, x2 = tie((x3, y3, y1, accs, pair1, d0, x2))
     d3, d2, d1 = beside(y3), below(x2), swap(d0, "dp", 1)
+    accs = run(pairs(x3, y3, y1), accs=accs)
+    d3, d2, d1, accs, pair1 = tie((d3, d2, d1, accs, pair1))
     sent.append(swap(pair1[0], "expert", 6))
-    accs = run(pairs(x3, y3, y1), accs=accs)
-    d3, d2, d1, accs, sent = tie((d3, d2, d1, accs, sent))
+    accs = run(pairs(d1, d2, d3), accs=accs, last=True)
+    sent, accs = tie((sent, accs))
     total = pair0[0].astype(jnp.float32)
     for piece in sent:
         total = total + piece.astype(jnp.float32)
-    accs = run(pairs(d1, d2, d3), accs=accs, last=True)
     return (total.astype(jnp.bfloat16), *accs)
 
 

time: 129 us -> 121 us (0.938)
  waiting for transfers between devices: 34 us -> 24.2 us
  local copies, waits for them, and re-layouts: 5.41 us -> 1.1 us
  starting transfers between devices: 27.8 us -> 31.7 us
  Pallas kernels: 58.6 us -> 61.2 us
    ppermute x34, waiting for transfers between devices: 27.3 us -> 18.2 us  [swap(): return lax.ppermute(value, axis, [(i, i ^ bit) for i in range(size)])]
    unnamed x12 -> x6, local copies, waits for them, and re-layouts: 5.38 us -> 1.06 us
    ppermute x34, starting transfers between devices: 23.7 us -> 27.5 us  [swap(): return lax.ppermute(value, axis, [(i, i ^ bit) for i in range(size)])]
    pallas_call x1, Pallas kernels: 0.19 us -> 2 us  [pack(): pl.pallas_call(pack_kernel, out_shape=jax.ShapeDtypeStruct((tok_dev, 2 *...]
  transfers between devices with their start and end apart: 38 -> 38, of which waited for: 15 -> 15; matrix products, arithmetic and copies ran while one was open for 1% -> 0% of each run, Pallas kernels for 37% -> 49%
where the time goes in v4:
time: 121 us; the launch traced here: 120 us
  Pallas kernels  61.2 us (51%)
  starting transfers between devices  31.7 us (26%)
  waiting for transfers between devices  24.2 us (20%)
  other arithmetic  1.25 us (1%)
    pallas_call x5, Pallas kernels, group(): pl.pallas_call(functools.partial(group_kernel, first, last, own, depth, b...  53.8 us
    ppermute x34, starting transfers between devices, swap(): return lax.ppermute(value, axis, [(i, i ^ bit) for i in range(size)])  27.5 us
    ppermute x34, waiting for transfers between devices, swap(): return lax.ppermute(value, axis, [(i, i ^ bit) for i in range(size)])  18.2 us
    ppermute x2, waiting for transfers between devices, outward(): return lax.ppermute(value, 'dp', [(1, 0), (2, 3)])  5.94 us
    pallas_call x1, Pallas kernels, hold(): pl.pallas_call(hold_kernel, in_specs=[pl.BlockSpec(memory_space=pl.ANY)]...  3.79 us
    ppermute x2, starting transfers between devices, outward(): return lax.ppermute(value, 'dp', [(1, 0), (2, 3)])  2.74 us
  transfers between devices with their start and end apart: 38, of which 15 were waited for; matrix products, arithmetic and copies ran while one was open for 0% of the time, Pallas kernels for 49%

profile of v4, /device:TPU:0, one launch (start us, length us, event | category | flops | bytes accessed | tf_op | source)
XLA Modules:
  0.0 120.3 jit_solution(1392514317898666250)
XLA Ops:
  0.6 2.0 %shard_map.102.refs_0_ = bf16[128,2176]{1,0:T(8,128)(2,1)} custom-call(bf16[128,1024]{1,0:T(8,128)(2,1)} %tok_ref.1, bf16[128,1024]{1,0:T(8,128)(2,1)} %dy_ref.1, s32[10,128]{1,0:T(8,128)} %bitcast.11, bf16[10,128]{1,0:T(8,128)(2,1)} %bitcast.12), custom_call_target="tpu_custom_call" | custom-call | flops 10000000 | bytes 2000000 | tf_op jit(solution)/shard_map/pallas_call | solution.py:155
  2.6 2.9 %collective-permute-start = (bf16[128,2176]{1,0:T(8,128)(2,1)}, bf16[128,2176]{1,0:T(8,128)(2,1)S(1)}, u32[]{:S(2)}, u32[]{:S(2)}) collective-permute-start(bf16[128,2176]{1,0:T(8,128)(2,1)} %shard_map.102.refs_0_), channel_id=1, source_target_pairs={{0,2},{1,3},{2,0},{3,1},{4,6},{5,7},{6,4},{7,5},{8,10},{9,11},{10,... | collective-permute-start | bytes 1671176 | tf_op jit(solution)/shard_map/ppermute | solution.py:396
  5.6 1.5 %collective-permute-start.1 = (bf16[128,2176]{1,0:T(8,128)(2,1)}, bf16[128,2176]{1,0:T(8,128)(2,1)S(1)}, u32[]{:S(2)}, u32[]{:S(2)}) collective-permute-start(bf16[128,2176]{1,0:T(8,128)(2,1)} %shard_map.102.refs_0_), channel_id=1, source_target_pairs={{0,4},{1,5},{2,6},{3,7},{4,0},{5,1},{6,2},{7,3},{8,12},{9,13},{10,... | collective-permute-start | bytes 1671176 | tf_op jit(solution)/shard_map/ppermute | solution.py:396
  7.1 1.6 %collective-permute-start.2 = (bf16[128,2176]{1,0:T(8,128)(2,1)}, bf16[128,2176]{1,0:T(8,128)(2,1)S(1)}, u32[]{:S(2)}, u32[]{:S(2)}) collective-permute-start(bf16[128,2176]{1,0:T(8,128)(2,1)} %shard_map.102.refs_0_), channel_id=1, source_target_pairs={{0,8},{8,0},{16,24},{24,16},{1,9},{9,1},{17,25},{25,17},{2,10},{10... | collective-permute-start | bytes 1671176 | tf_op jit(solution)/shard_map/ppermute | solution.py:396
  9.4 3.8 %shard_map.103 = (bf16[3,1024,512]{2,1,0:T(8,128)(2,1)S(1)}, bf16[3,1024,512]{2,1,0:T(8,128)(2,1)S(1)}, bf16[3,512,1024]{2,1,0:T(8,128)(2,1)S(1)}) custom-call(bf16[3,1024,512]{2,1,0:T(8,128)(2,1)} %refs_0_, bf16[3,1024,512]{2,1,0:T(8,128)(2,1)} %refs_1_, bf16[3,512,1024]{2,1,0:T(8,128)(2,1)} %refs_2_), custom_call_target="tpu_custom_call" | custom-call | bytes 2000000 | tf_op jit(solution)/shard_map/pallas_call | solution.py:354
  13.2 5.2 %collective-permute-done.refs_2_ = bf16[128,2176]{1,0:T(8,128)(2,1)S(1)} collective-permute-done((bf16[128,2176]{1,0:T(8,128)(2,1)}, bf16[128,2176]{1,0:T(8,128)(2,1)S(1)}, u32[]{:S(2)}, u32[]{:S(2)}) %collective-permute-start) | collective-permute-done | bytes 557088 | tf_op jit(solution)/shard_map/ppermute | solution.py:396
  18.5 1.4 %collective-permute-done.1.refs_4_ = bf16[128,2176]{1,0:T(8,128)(2,1)S(1)} collective-permute-done((bf16[128,2176]{1,0:T(8,128)(2,1)}, bf16[128,2176]{1,0:T(8,128)(2,1)S(1)}, u32[]{:S(2)}, u32[]{:S(2)}) %collective-permute-start.1) | collective-permute-done | bytes 557088 | tf_op jit(solution)/shard_map/ppermute | solution.py:396
  19.9 1.2 %collective-permute-done.2.refs_6_ = bf16[128,2176]{1,0:T(8,128)(2,1)S(1)} collective-permute-done((bf16[128,2176]{1,0:T(8,128)(2,1)}, bf16[128,2176]{1,0:T(8,128)(2,1)S(1)}, u32[]{:S(2)}, u32[]{:S(2)}) %collective-permute-start.2) | collective-permute-done | bytes 557088 | tf_op jit(solution)/shard_map/ppermute | solution.py:396
  23.9 1.3 %collective-permute-start.7 = (bf16[128,2176]{1,0:T(8,128)(2,1)S(1)}, bf16[128,2176]{1,0:T(8,128)(2,1)S(1)}, u32[]{:S(2)}, u32[]{:S(2)}) collective-permute-start(bf16[128,2176]{1,0:T(8,128)(2,1)S(1)} %collective-permute-done.3.inner_ref), channel_id=1, source_target_pairs={{8,0},{16,24},{9,1},{17,25},{10,2},{18,26},{11,3},{19,27},{12,4},{... | collective-permute-start | bytes 1671176 | tf_op jit(solution)/shard_map/ppermute | solution.py:416
  25.2 15.6 %shard_map.104 = (f32[3,256,512]{2,1,0:T(8,128)S(1)}, f32[3,256,512]{2,1,0:T(8,128)S(1)}, f32[3,128,1024]{2,1,0:T(8,128)S(1)}, bf16[3,128,1024]{2,1,0:T(8,128)(2,1)S(1)}, bf16[3,128,1024]{2,1,0:T(8,128)(2,1)S(1)}) custom-call(bf16[128,2176]{1,0:T(8,128)(2,1)S(1)} %copy-done.2, bf16[128,2176]{1,0:T(8,128)(2,1)} %collective-permute-done.4.refs_1_, ...), custom_call_target="tpu_custom_call" | custom-call | flops 201326592 | bytes 557056 | tf_op jit(solution)/shard_map/pallas_call | solution.py:325
  40.8 3.9 %collective-permute-done.7.outer_ref = bf16[128,2176]{1,0:T(8,128)(2,1)S(1)} collective-permute-done((bf16[128,2176]{1,0:T(8,128)(2,1)S(1)}, bf16[128,2176]{1,0:T(8,128)(2,1)S(1)}, u32[]{:S(2)}, u32[]{:S(2)}) %collective-permute-start.7) | collective-permute-done | bytes 557088 | tf_op jit(solution)/shard_map/ppermute | solution.py:416
  46.6 1.5 %collective-permute-start.16 = (bf16[128,2176]{1,0:T(8,128)(2,1)}, bf16[128,2176]{1,0:T(8,128)(2,1)S(1)}, u32[]{:S(2)}, u32[]{:S(2)}) collective-permute-start(bf16[128,2176]{1,0:T(8,128)(2,1)} %shard_map.105.refs_4_), channel_id=1, source_target_pairs={{0,2},{1,3},{2,0},{3,1},{4,6},{5,7},{6,4},{7,5},{8,10},{9,11},{10,... | collective-permute-start | bytes 1671176 | tf_op jit(solution)/shard_map/ppermute | solution.py:396
  48.1 1.5 %collective-permute-start.17 = (bf16[128,2176]{1,0:T(8,128)(2,1)}, bf16[128,2176]{1,0:T(8,128)(2,1)S(1)}, u32[]{:S(2)}, u32[]{:S(2)}) collective-permute-start(bf16[128,2176]{1,0:T(8,128)(2,1)} %shard_map.105.refs_4_), channel_id=1, source_target_pairs={{0,4},{1,5},{2,6},{3,7},{4,0},{5,1},{6,2},{7,3},{8,12},{9,13},{10,... | collective-permute-start | bytes 1671176 | tf_op jit(solution)/shard_map/ppermute | solution.py:396
  49.6 1.5 %collective-permute-start.18 = (bf16[128,2176]{1,0:T(8,128)(2,1)S(1)}, bf16[128,2176]{1,0:T(8,128)(2,1)S(1)}, u32[]{:S(2)}, u32[]{:S(2)}) collective-permute-start(bf16[128,2176]{1,0:T(8,128)(2,1)S(1)} %collective-permute-done.11.inner_ref), channel_id=1, source_target_pairs={{8,0},{16,24},{9,1},{17,25},{10,2},{18,26},{11,3},{19,27},{12,4},{... | collective-permute-start | bytes 1671176 | tf_op jit(solution)/shard_map/ppermute | solution.py:416
  51.5 1.4 %collective-permute-start.19 = (bf16[128,1024]{1,0:T(8,128)(2,1)S(1)}, bf16[128,1024]{1,0:T(8,128)(2,1)S(1)}, u32[]{:S(2)}, u32[]{:S(2)}) collective-permute-start(bf16[128,1024]{1,0:T(8,128)(2,1)S(1)} %get-tuple-element.203), channel_id=1, source_target_pairs={{0,2},{1,3},{2,0},{3,1},{4,6},{5,7},{6,4},{7,5},{8,10},{9,11},{10,... | collective-permute-start | bytes 786440 | tf_op jit(solution)/shard_map/ppermute | solution.py:396
  53.4 11.4 %shard_map.106 = (f32[3,256,512]{2,1,0:T(8,128)S(1)}, f32[3,256,512]{2,1,0:T(8,128)S(1)}, f32[3,128,1024]{2,1,0:T(8,128)S(1)}, bf16[1,128,1024]{2,1,0:T(8,128)(2,1)S(1)}, bf16[1,128,1024]{2,1,0:T(8,128)(2,1)S(1)}) custom-call(bf16[128,2176]{1,0:T(8,128)(2,1)S(1)} %collective-permute-done.6.refs_0_, ...), custom_call_target="tpu_custom_call", output_to_operand_aliasing={{0}: (9, {}), {1}: (10, {}), {2}: (11, {})} | custom-call | flops 150994944 | bytes 557056 | tf_op jit(solution)/shard_map/pallas_call | solution.py:325
  64.9 2.1 %collective-permute-done.18.outer_ref = bf16[128,2176]{1,0:T(8,128)(2,1)S(1)} collective-permute-done((bf16[128,2176]{1,0:T(8,128)(2,1)S(1)}, bf16[128,2176]{1,0:T(8,128)(2,1)S(1)}, u32[]{:S(2)}, u32[]{:S(2)}) %collective-permute-start.18) | collective-permute-done | bytes 557088 | tf_op jit(solution)/shard_map/ppermute | solution.py:416
  67.1 1.6 %collective-permute-done.20 = bf16[128,1024]{1,0:T(8,128)(2,1)S(1)} collective-permute-done((bf16[128,1024]{1,0:T(8,128)(2,1)S(1)}, bf16[128,1024]{1,0:T(8,128)(2,1)S(1)}, u32[]{:S(2)}, u32[]{:S(2)}) %collective-permute-start.20) | collective-permute-done | bytes 262176 | tf_op jit(solution)/shard_map/ppermute | solution.py:396
  70.5 1.5 %collective-permute-start.21 = (bf16[128,2176]{1,0:T(8,128)(2,1)}, bf16[128,2176]{1,0:T(8,128)(2,1)S(1)}, u32[]{:S(2)}, u32[]{:S(2)}) collective-permute-start(bf16[128,2176]{1,0:T(8,128)(2,1)} %shard_map.107.refs_4_), channel_id=1, source_target_pairs={{0,2},{1,3},{2,0},{3,1},{4,6},{5,7},{6,4},{7,5},{8,10},{9,11},{10,... | collective-permute-start | bytes 1671176 | tf_op jit(solution)/shard_map/ppermute | solution.py:396
  72.0 1.5 %collective-permute-start.22 = (bf16[128,2176]{1,0:T(8,128)(2,1)}, bf16[128,2176]{1,0:T(8,128)(2,1)S(1)}, u32[]{:S(2)}, u32[]{:S(2)}) collective-permute-start(bf16[128,2176]{1,0:T(8,128)(2,1)} %shard_map.107.refs_4_), channel_id=1, source_target_pairs={{0,4},{1,5},{2,6},{3,7},{4,0},{5,1},{6,2},{7,3},{8,12},{9,13},{10,... | collective-permute-start | bytes 1671176 | tf_op jit(solution)/shard_map/ppermute | solution.py:396
  73.6 3.4 %collective-permute-start.23 = (bf16[128,2176]{1,0:T(8,128)(2,1)S(1)}, bf16[128,2176]{1,0:T(8,128)(2,1)S(1)}, u32[]{:S(2)}, u32[]{:S(2)}) collective-permute-start(bf16[128,2176]{1,0:T(8,128)(2,1)S(1)} %collective-permute-done.1.refs_4_), channel_id=1, source_target_pairs={{0,8},{8,0},{16,24},{24,16},{1,9},{9,1},{17,25},{25,17},{2,10},{10... | collective-permute-start | bytes 1671176 | tf_op jit(solution)/shard_map/ppermute | solution.py:396
  76.9 1.1 copy-done.1
  78.0 8.7 %shard_map.108 = (f32[3,256,512]{2,1,0:T(8,128)S(1)}, f32[3,256,512]{2,1,0:T(8,128)S(1)}, f32[3,128,1024]{2,1,0:T(8,128)S(1)}) custom-call(bf16[128,2176]{1,0:T(8,128)(2,1)S(1)} %collective-permute-done.16.refs_0_, bf16[128,2176]{1,0:T(8,128)(2,1)S(1)} %collective-permute-done.24.refs_1_, ...), custom_call_target="tpu_custom_call", output_to_operand_aliasing={{0}: (9, {}), {1}: (10, {}), {2}: (11, {})} | custom-call | flops 150994944 | bytes 557056 | tf_op jit(solution)/shard_map/pallas_call | solution.py:325
  86.8 2.6 %collective-permute-done.23.refs_4_ = bf16[128,2176]{1,0:T(8,128)(2,1)S(1)} collective-permute-done((bf16[128,2176]{1,0:T(8,128)(2,1)S(1)}, bf16[128,2176]{1,0:T(8,128)(2,1)S(1)}, u32[]{:S(2)}, u32[]{:S(2)}) %collective-permute-start.23) | collective-permute-done | bytes 557088 | tf_op jit(solution)/shard_map/ppermute | solution.py:396
  89.9 1.5 %collective-permute-start.28 = (bf16[128,2176]{1,0:T(8,128)(2,1)S(1)}, bf16[128,2176]{1,0:T(8,128)(2,1)S(1)}, u32[]{:S(2)}, u32[]{:S(2)}) collective-permute-start(bf16[128,2176]{1,0:T(8,128)(2,1)S(1)} %collective-permute-done.22.refs_2_), channel_id=1, source_target_pairs={{0,2},{1,3},{2,0},{3,1},{4,6},{5,7},{6,4},{7,5},{8,10},{9,11},{10,... | collective-permute-start | bytes 1671176 | tf_op jit(solution)/shard_map/ppermute | solution.py:396
  91.9 1.7 %collective-permute-start.30 = (bf16[128,2176]{1,0:T(8,128)(2,1)S(1)}, bf16[128,2176]{1,0:T(8,128)(2,1)S(1)}, u32[]{:S(2)}, u32[]{:S(2)}) collective-permute-start(bf16[128,2176]{1,0:T(8,128)(2,1)S(1)} %collective-permute-done.6.refs_0_), channel_id=1, source_target_pairs={{0,8},{8,0},{16,24},{24,16},{1,9},{9,1},{17,25},{25,17},{2,10},{10... | collective-permute-start | bytes 1671176 | tf_op jit(solution)/shard_map/ppermute | solution.py:396
  93.7 8.7 %shard_map.109 = (f32[3,256,512]{2,1,0:T(8,128)S(1)}, f32[3,256,512]{2,1,0:T(8,128)S(1)}, f32[3,128,1024]{2,1,0:T(8,128)S(1)}) custom-call(bf16[128,2176]{1,0:T(8,128)(2,1)S(1)} %collective-permute-done.21.refs_0_, bf16[128,2176]{1,0:T(8,128)(2,1)S(1)} %collective-permute-done.31.refs_1_, ...), custom_call_target="tpu_custom_call", output_to_operand_aliasing={{0}: (9, {}), {1}: (10, {}), {2}: (11, {})} | custom-call | flops 150994944 | bytes 557056 | tf_op jit(solution)/shard_map/pallas_call | solution.py:325
  102.4 2.6 %collective-permute-done.28.refs_4_ = bf16[128,2176]{1,0:T(8,128)(2,1)S(1)} collective-permute-done((bf16[128,2176]{1,0:T(8,128)(2,1)S(1)}, bf16[128,2176]{1,0:T(8,128)(2,1)S(1)}, u32[]{:S(2)}, u32[]{:S(2)}) %collective-permute-start.28) | collective-permute-done | bytes 557088 | tf_op jit(solution)/shard_map/ppermute | solution.py:396
  105.0 1.2 collective-permute-done.29.refs_2_
  106.9 1.5 %collective-permute-start.34 = (bf16[128,1024]{1,0:T(8,128)(2,1)S(1)}, bf16[128,1024]{1,0:T(8,128)(2,1)S(1)}, u32[]{:S(2)}, u32[]{:S(2)}) collective-permute-start(bf16[128,1024]{1,0:T(8,128)(2,1)S(1)} %bitcast.10), channel_id=1, source_target_pairs={{0,6},{1,7},{2,4},{3,5},{4,2},{5,3},{6,0},{7,1},{8,14},{9,15},{10,... | collective-permute-start | bytes 786440 | tf_op jit(solution)/shard_map/ppermute | solution.py:396
  110.0 9.4 %shard_map.110 = (bf16[3,256,512]{2,1,0:T(8,128)(2,1)}, bf16[3,256,512]{2,1,0:T(8,128)(2,1)}, bf16[3,128,1024]{2,1,0:T(8,128)(2,1)}) custom-call(bf16[128,2176]{1,0:T(8,128)(2,1)S(1)} %collective-permute-done.30.refs_0_, bf16[128,2176]{1,0:T(8,128)(2,1)S(1)} %collective-permute-done.35.refs_1_, bf16[128,2176]{1,0:T(8,128)(2,1)S(1)} %collective-permute-done.29.refs_2_, ...), custom_call_target="tpu_custom_call" | custom-call | flops 150994944 | bytes 557056 | tf_op jit(solution)/shard_map/pallas_call | solution.py:325
  119.4 0.9 fusion.2
  (63 shorter events, 11.8 us)
Async XLA Ops:
  2.6 15.8 %collective-permute-start = (bf16[128,2176]{1,0:T(8,128)(2,1)}, bf16[128,2176]{1,0:T(8,128)(2,1)S(1)}, u32[]{:S(2)}, u32[]{:S(2)}) collective-permute-start(bf16[128,2176]{1,0:T(8,128)(2,1)} %shard_map.102.refs_0_), channel_id=1, source_target_pairs={{0,2},{1,3},{2,0},{3,1},{4,6},{5,7},{6,4},{7,5},{8,10},{9,11},{10,... | collective-permute-start | bytes 1671176 | tf_op jit(solution)/shard_map/ppermute | solution.py:396
  5.6 14.3 %collective-permute-start.1 = (bf16[128,2176]{1,0:T(8,128)(2,1)}, bf16[128,2176]{1,0:T(8,128)(2,1)S(1)}, u32[]{:S(2)}, u32[]{:S(2)}) collective-permute-start(bf16[128,2176]{1,0:T(8,128)(2,1)} %shard_map.102.refs_0_), channel_id=1, source_target_pairs={{0,4},{1,5},{2,6},{3,7},{4,0},{5,1},{6,2},{7,3},{8,12},{9,13},{10,... | collective-permute-start | bytes 1671176 | tf_op jit(solution)/shard_map/ppermute | solution.py:396
  7.1 14.0 %collective-permute-start.2 = (bf16[128,2176]{1,0:T(8,128)(2,1)}, bf16[128,2176]{1,0:T(8,128)(2,1)S(1)}, u32[]{:S(2)}, u32[]{:S(2)}) collective-permute-start(bf16[128,2176]{1,0:T(8,128)(2,1)} %shard_map.102.refs_0_), channel_id=1, source_target_pairs={{0,8},{8,0},{16,24},{24,16},{1,9},{9,1},{17,25},{25,17},{2,10},{10... | collective-permute-start | bytes 1671176 | tf_op jit(solution)/shard_map/ppermute | solution.py:396
  8.7 12.4 %collective-permute-start.3 = (bf16[128,2176]{1,0:T(8,128)(2,1)}, bf16[128,2176]{1,0:T(8,128)(2,1)S(1)}, u32[]{:S(2)}, u32[]{:S(2)}) collective-permute-start(bf16[128,2176]{1,0:T(8,128)(2,1)} %shard_map.102.refs_0_), channel_id=1, source_target_pairs={{8,16},{16,8},{9,17},{17,9},{10,18},{18,10},{11,19},{19,11},{12,20... | collective-permute-start | bytes 1671176 | tf_op jit(solution)/shard_map/ppermute | solution.py:412
  9.4 11.8 %collective-permute-start.4 = (bf16[128,2176]{1,0:T(8,128)(2,1)}, bf16[128,2176]{1,0:T(8,128)(2,1)}, u32[]{:S(2)}, u32[]{:S(2)}) collective-permute-start(bf16[128,2176]{1,0:T(8,128)(2,1)} %shard_map.102.refs_0_), channel_id=1, source_target_pairs={{0,1},{1,0},{2,3},{3,2},{4,5},{5,4},{6,7},{7,6},{8,9},{9,8},{10,11... | collective-permute-start | bytes 1671176 | tf_op jit(solution)/shard_map/ppermute | solution.py:396
  21.6 3.5 %collective-permute-start.9 = (bf16[128,2176]{1,0:T(8,128)(2,1)S(1)}, bf16[128,2176]{1,0:T(8,128)(2,1)S(1)}, u32[]{:S(2)}, u32[]{:S(2)}) collective-permute-start(bf16[128,2176]{1,0:T(8,128)(2,1)S(1)} %collective-permute-done.1.refs_4_), channel_id=1, source_target_pairs={{0,1},{1,0},{2,3},{3,2},{4,5},{5,4},{6,7},{7,6},{8,9},{9,8},{10,11... | collective-permute-start | bytes 1671176 | tf_op jit(solution)/shard_map/ppermute | solution.py:396
  21.7 19.1 %collective-permute-start.11 = (bf16[128,2176]{1,0:T(8,128)(2,1)S(1)}, bf16[128,2176]{1,0:T(8,128)(2,1)S(1)}, u32[]{:S(2)}, u32[]{:S(2)}) collective-permute-start(bf16[128,2176]{1,0:T(8,128)(2,1)S(1)} %collective-permute-done.2.refs_6_), channel_id=1, source_target_pairs={{8,16},{16,8},{9,17},{17,9},{10,18},{18,10},{11,19},{19,11},{12,20... | collective-permute-start | bytes 1671176 | tf_op jit(solution)/shard_map/ppermute | solution.py:412
  22.4 18.4 %collective-permute-start.5 = (bf16[128,2176]{1,0:T(8,128)(2,1)S(1)}, bf16[128,2176]{1,0:T(8,128)(2,1)S(1)}, u32[]{:S(2)}, u32[]{:S(2)}) collective-permute-start(bf16[128,2176]{1,0:T(8,128)(2,1)S(1)} %collective-permute-done.2.refs_6_), channel_id=1, source_target_pairs={{0,2},{1,3},{2,0},{3,1},{4,6},{5,7},{6,4},{7,5},{8,10},{9,11},{10,... | collective-permute-start | bytes 1671176 | tf_op jit(solution)/shard_map/ppermute | solution.py:396
  23.1 17.7 %collective-permute-start.6 = (bf16[128,2176]{1,0:T(8,128)(2,1)S(1)}, bf16[128,2176]{1,0:T(8,128)(2,1)S(1)}, u32[]{:S(2)}, u32[]{:S(2)}) collective-permute-start(bf16[128,2176]{1,0:T(8,128)(2,1)S(1)} %collective-permute-done.refs_2_), channel_id=1, source_target_pairs={{0,4},{1,5},{2,6},{3,7},{4,0},{5,1},{6,2},{7,3},{8,12},{9,13},{10,... | collective-permute-start | bytes 1671176 | tf_op jit(solution)/shard_map/ppermute | solution.py:396
  23.9 20.8 %collective-permute-start.7 = (bf16[128,2176]{1,0:T(8,128)(2,1)S(1)}, bf16[128,2176]{1,0:T(8,128)(2,1)S(1)}, u32[]{:S(2)}, u32[]{:S(2)}) collective-permute-start(bf16[128,2176]{1,0:T(8,128)(2,1)S(1)} %collective-permute-done.3.inner_ref), channel_id=1, source_target_pairs={{8,0},{16,24},{9,1},{17,25},{10,2},{18,26},{11,3},{19,27},{12,4},{... | collective-permute-start | bytes 1671176 | tf_op jit(solution)/shard_map/ppermute | solution.py:416
  44.7 4.9 %collective-permute-start.15 = (bf16[3,128,1024]{2,1,0:T(8,128)(2,1)S(1)}, bf16[3,128,1024]{2,1,0:T(8,128)(2,1)S(1)}, u32[]{:S(2)}, u32[]{:S(2)}) collective-permute-start(bf16[3,128,1024]{2,1,0:T(8,128)(2,1)S(1)} %get-tuple-element.135), channel_id=1, source_target_pairs={{0,1},{1,0},{2,3},{3,2},{4,5},{5,4},{6,7},{7,6},{8,9},{9,8},{10,11... | collective-permute-start | bytes 2359304 | tf_op jit(solution)/shard_map/ppermute | solution.py:396
  46.1 5.3 %collective-permute-start.12 = (bf16[128,2176]{1,0:T(8,128)(2,1)S(1)}, bf16[128,2176]{1,0:T(8,128)(2,1)S(1)}, u32[]{:S(2)}, u32[]{:S(2)}) collective-permute-start(bf16[128,2176]{1,0:T(8,128)(2,1)S(1)} %collective-permute-done.6.refs_0_), channel_id=1, source_target_pairs={{0,1},{1,0},{2,3},{3,2},{4,5},{5,4},{6,7},{7,6},{8,9},{9,8},{10,11... | collective-permute-start | bytes 1671176 | tf_op jit(solution)/shard_map/ppermute | solution.py:396
  46.2 5.2 %collective-permute-start.13 = (bf16[128,2176]{1,0:T(8,128)(2,1)S(1)}, bf16[128,2176]{1,0:T(8,128)(2,1)S(1)}, u32[]{:S(2)}, u32[]{:S(2)}) collective-permute-start(bf16[128,2176]{1,0:T(8,128)(2,1)S(1)} %collective-permute-done.5.refs_2_), channel_id=1, source_target_pairs={{0,1},{1,0},{2,3},{3,2},{4,5},{5,4},{6,7},{7,6},{8,9},{9,8},{10,11... | collective-permute-start | bytes 1671176 | tf_op jit(solution)/shard_map/ppermute | solution.py:396
  46.6 18.3 %collective-permute-start.16 = (bf16[128,2176]{1,0:T(8,128)(2,1)}, bf16[128,2176]{1,0:T(8,128)(2,1)S(1)}, u32[]{:S(2)}, u32[]{:S(2)}) collective-permute-start(bf16[128,2176]{1,0:T(8,128)(2,1)} %shard_map.105.refs_4_), channel_id=1, source_target_pairs={{0,2},{1,3},{2,0},{3,1},{4,6},{5,7},{6,4},{7,5},{8,10},{9,11},{10,... | collective-permute-start | bytes 1671176 | tf_op jit(solution)/shard_map/ppermute | solution.py:396
  48.1 16.8 %collective-permute-start.17 = (bf16[128,2176]{1,0:T(8,128)(2,1)}, bf16[128,2176]{1,0:T(8,128)(2,1)S(1)}, u32[]{:S(2)}, u32[]{:S(2)}) collective-permute-start(bf16[128,2176]{1,0:T(8,128)(2,1)} %shard_map.105.refs_4_), channel_id=1, source_target_pairs={{0,4},{1,5},{2,6},{3,7},{4,0},{5,1},{6,2},{7,3},{8,12},{9,13},{10,... | collective-permute-start | bytes 1671176 | tf_op jit(solution)/shard_map/ppermute | solution.py:396
  49.6 17.3 %collective-permute-start.18 = (bf16[128,2176]{1,0:T(8,128)(2,1)S(1)}, bf16[128,2176]{1,0:T(8,128)(2,1)S(1)}, u32[]{:S(2)}, u32[]{:S(2)}) collective-permute-start(bf16[128,2176]{1,0:T(8,128)(2,1)S(1)} %collective-permute-done.11.inner_ref), channel_id=1, source_target_pairs={{8,0},{16,24},{9,1},{17,25},{10,2},{18,26},{11,3},{19,27},{12,4},{... | collective-permute-start | bytes 1671176 | tf_op jit(solution)/shard_map/ppermute | solution.py:416
  51.5 15.6 %collective-permute-start.19 = (bf16[128,1024]{1,0:T(8,128)(2,1)S(1)}, bf16[128,1024]{1,0:T(8,128)(2,1)S(1)}, u32[]{:S(2)}, u32[]{:S(2)}) collective-permute-start(bf16[128,1024]{1,0:T(8,128)(2,1)S(1)} %get-tuple-element.203), channel_id=1, source_target_pairs={{0,2},{1,3},{2,0},{3,1},{4,6},{5,7},{6,4},{7,5},{8,10},{9,11},{10,... | collective-permute-start | bytes 786440 | tf_op jit(solution)/shard_map/ppermute | solution.py:396
  52.9 15.7 %collective-permute-start.20 = (bf16[128,1024]{1,0:T(8,128)(2,1)S(1)}, bf16[128,1024]{1,0:T(8,128)(2,1)S(1)}, u32[]{:S(2)}, u32[]{:S(2)}) collective-permute-start(bf16[128,1024]{1,0:T(8,128)(2,1)S(1)} %get-tuple-element.202), channel_id=1, source_target_pairs={{0,4},{1,5},{2,6},{3,7},{4,0},{5,1},{6,2},{7,3},{8,12},{9,13},{10,... | collective-permute-start | bytes 786440 | tf_op jit(solution)/shard_map/ppermute | solution.py:396
  69.5 4.1 %collective-permute-start.26 = (bf16[128,2176]{1,0:T(8,128)(2,1)}, bf16[128,2176]{1,0:T(8,128)(2,1)S(1)}, u32[]{:S(2)}, u32[]{:S(2)}) collective-permute-start(bf16[128,2176]{1,0:T(8,128)(2,1)} %shard_map.107.refs_4_), channel_id=1, source_target_pairs={{0,1},{1,0},{2,3},{3,2},{4,5},{5,4},{6,7},{7,6},{8,9},{9,8},{10,11... | collective-permute-start | bytes 1671176 | tf_op jit(solution)/shard_map/ppermute | solution.py:396
  70.0 6.9 %collective-permute-start.24 = (bf16[128,2176]{1,0:T(8,128)(2,1)S(1)}, bf16[128,2176]{1,0:T(8,128)(2,1)S(1)}, u32[]{:S(2)}, u32[]{:S(2)}) collective-permute-start(bf16[128,2176]{1,0:T(8,128)(2,1)S(1)} %collective-permute-done.16.refs_0_), channel_id=1, source_target_pairs={{0,1},{1,0},{2,3},{3,2},{4,5},{5,4},{6,7},{7,6},{8,9},{9,8},{10,11... | collective-permute-start | bytes 1671176 | tf_op jit(solution)/shard_map/ppermute | solution.py:396
  70.1 6.8 %collective-permute-start.25 = (bf16[128,2176]{1,0:T(8,128)(2,1)S(1)}, bf16[128,2176]{1,0:T(8,128)(2,1)S(1)}, u32[]{:S(2)}, u32[]{:S(2)}) collective-permute-start(bf16[128,2176]{1,0:T(8,128)(2,1)S(1)} %collective-permute-done.17.refs_2_), channel_id=1, source_target_pairs={{0,1},{1,0},{2,3},{3,2},{4,5},{5,4},{6,7},{7,6},{8,9},{9,8},{10,11... | collective-permute-start | bytes 1671176 | tf_op jit(solution)/shard_map/ppermute | solution.py:396
  70.5 16.2 %collective-permute-start.21 = (bf16[128,2176]{1,0:T(8,128)(2,1)}, bf16[128,2176]{1,0:T(8,128)(2,1)S(1)}, u32[]{:S(2)}, u32[]{:S(2)}) collective-permute-start(bf16[128,2176]{1,0:T(8,128)(2,1)} %shard_map.107.refs_4_), channel_id=1, source_target_pairs={{0,2},{1,3},{2,0},{3,1},{4,6},{5,7},{6,4},{7,5},{8,10},{9,11},{10,... | collective-permute-start | bytes 1671176 | tf_op jit(solution)/shard_map/ppermute | solution.py:396
  72.0 14.7 %collective-permute-start.22 = (bf16[128,2176]{1,0:T(8,128)(2,1)}, bf16[128,2176]{1,0:T(8,128)(2,1)S(1)}, u32[]{:S(2)}, u32[]{:S(2)}) collective-permute-start(bf16[128,2176]{1,0:T(8,128)(2,1)} %shard_map.107.refs_4_), channel_id=1, source_target_pairs={{0,4},{1,5},{2,6},{3,7},{4,0},{5,1},{6,2},{7,3},{8,12},{9,13},{10,... | collective-permute-start | bytes 1671176 | tf_op jit(solution)/shard_map/ppermute | solution.py:396
  73.6 15.8 %collective-permute-start.23 = (bf16[128,2176]{1,0:T(8,128)(2,1)S(1)}, bf16[128,2176]{1,0:T(8,128)(2,1)S(1)}, u32[]{:S(2)}, u32[]{:S(2)}) collective-permute-start(bf16[128,2176]{1,0:T(8,128)(2,1)S(1)} %collective-permute-done.1.refs_4_), channel_id=1, source_target_pairs={{0,8},{8,0},{16,24},{24,16},{1,9},{9,1},{17,25},{25,17},{2,10},{10... | collective-permute-start | bytes 1671176 | tf_op jit(solution)/shard_map/ppermute | solution.py:396
  89.4 4.3 %collective-permute-start.32 = (bf16[128,2176]{1,0:T(8,128)(2,1)S(1)}, bf16[128,2176]{1,0:T(8,128)(2,1)S(1)}, u32[]{:S(2)}, u32[]{:S(2)}) collective-permute-start(bf16[128,2176]{1,0:T(8,128)(2,1)S(1)} %collective-permute-done.22.refs_2_), channel_id=1, source_target_pairs={{0,1},{1,0},{2,3},{3,2},{4,5},{5,4},{6,7},{7,6},{8,9},{9,8},{10,11... | collective-permute-start | bytes 1671176 | tf_op jit(solution)/shard_map/ppermute | solution.py:396
  89.9 3.8 %collective-permute-start.33 = (bf16[128,2176]{1,0:T(8,128)(2,1)S(1)}, bf16[128,2176]{1,0:T(8,128)(2,1)S(1)}, u32[]{:S(2)}, u32[]{:S(2)}) collective-permute-start(bf16[128,2176]{1,0:T(8,128)(2,1)S(1)} %collective-permute-done.23.refs_4_), channel_id=1, source_target_pairs={{0,1},{1,0},{2,3},{3,2},{4,5},{5,4},{6,7},{7,6},{8,9},{9,8},{10,11... | collective-permute-start | bytes 1671176 | tf_op jit(solution)/shard_map/ppermute | solution.py:396
  89.9 15.0 %collective-permute-start.28 = (bf16[128,2176]{1,0:T(8,128)(2,1)S(1)}, bf16[128,2176]{1,0:T(8,128)(2,1)S(1)}, u32[]{:S(2)}, u32[]{:S(2)}) collective-permute-start(bf16[128,2176]{1,0:T(8,128)(2,1)S(1)} %collective-permute-done.22.refs_2_), channel_id=1, source_target_pairs={{0,2},{1,3},{2,0},{3,1},{4,6},{5,7},{6,4},{7,5},{8,10},{9,11},{10,... | collective-permute-start | bytes 1671176 | tf_op jit(solution)/shard_map/ppermute | solution.py:396
  91.4 14.8 %collective-permute-start.29 = (bf16[128,2176]{1,0:T(8,128)(2,1)S(1)}, bf16[128,2176]{1,0:T(8,128)(2,1)S(1)}, u32[]{:S(2)}, u32[]{:S(2)}) collective-permute-start(bf16[128,2176]{1,0:T(8,128)(2,1)S(1)} %collective-permute-done.16.refs_0_), channel_id=1, source_target_pairs={{0,4},{1,5},{2,6},{3,7},{4,0},{5,1},{6,2},{7,3},{8,12},{9,13},{10,... | collective-permute-start | bytes 1671176 | tf_op jit(solution)/shard_map/ppermute | solution.py:396
  91.9 14.5 %collective-permute-start.30 = (bf16[128,2176]{1,0:T(8,128)(2,1)S(1)}, bf16[128,2176]{1,0:T(8,128)(2,1)S(1)}, u32[]{:S(2)}, u32[]{:S(2)}) collective-permute-start(bf16[128,2176]{1,0:T(8,128)(2,1)S(1)} %collective-permute-done.6.refs_0_), channel_id=1, source_target_pairs={{0,8},{8,0},{16,24},{24,16},{1,9},{9,1},{17,25},{25,17},{2,10},{10... | collective-permute-start | bytes 1671176 | tf_op jit(solution)/shard_map/ppermute | solution.py:396
  106.4 2.8 %collective-permute-start.36 = (bf16[128,2176]{1,0:T(8,128)(2,1)S(1)}, bf16[128,2176]{1,0:T(8,128)(2,1)S(1)}, u32[]{:S(2)}, u32[]{:S(2)}) collective-permute-start(bf16[128,2176]{1,0:T(8,128)(2,1)S(1)} %collective-permute-done.29.refs_2_), channel_id=1, source_target_pairs={{0,1},{1,0},{2,3},{3,2},{4,5},{5,4},{6,7},{7,6},{8,9},{9,8},{10,11... | collective-permute-start | bytes 1671176 | tf_op jit(solution)/shard_map/ppermute | solution.py:396
  106.9 3.0 %collective-permute-start.37 = (bf16[128,2176]{1,0:T(8,128)(2,1)S(1)}, bf16[128,2176]{1,0:T(8,128)(2,1)S(1)}, u32[]{:S(2)}, u32[]{:S(2)}) collective-permute-start(bf16[128,2176]{1,0:T(8,128)(2,1)S(1)} %collective-permute-done.28.refs_4_), channel_id=1, source_target_pairs={{0,1},{1,0},{2,3},{3,2},{4,5},{5,4},{6,7},{7,6},{8,9},{9,8},{10,11... | collective-permute-start | bytes 1671176 | tf_op jit(solution)/shard_map/ppermute | solution.py:396
  106.9 12.4 %collective-permute-start.34 = (bf16[128,1024]{1,0:T(8,128)(2,1)S(1)}, bf16[128,1024]{1,0:T(8,128)(2,1)S(1)}, u32[]{:S(2)}, u32[]{:S(2)}) collective-permute-start(bf16[128,1024]{1,0:T(8,128)(2,1)S(1)} %bitcast.10), channel_id=1, source_target_pairs={{0,6},{1,7},{2,4},{3,5},{4,2},{5,3},{6,0},{7,1},{8,14},{9,15},{10,... | collective-permute-start | bytes 786440 | tf_op jit(solution)/shard_map/ppermute | solution.py:396
  (9 other events, 45.8 us)

commit v5 on v4

--- a/solution.py
+++ b/solution.py
@@ -167,7 +167,7 @@
         return [refs.pop(0) for _ in range(count)]
 
     block_hbm = take(blocks)
-    gate_ref, up_ref, down_ref = take(3)
+    gate_ref, up_ref, across_ref = take(3)
     acc_refs = [] if first else take(3)
     out_refs = take(3)
     piece_hbm = take(2) if own else []
@@ -226,7 +226,7 @@
         d_out = d_rows[e]
         gate_pre = mul(rows_x, gate_ref[e])
         up_pre = mul(rows_x, up_ref[e])
-        d_hidden = contract_last(d_out, down_ref[e])
+        d_hidden = mul(d_out, across_ref[e])
         sig = 0.5 * jnp.tanh(0.5 * gate_pre) + 0.5
         act = gate_pre * sig
         hid[...] = (act * up_pre).astype(jnp.bfloat16)
@@ -338,54 +338,66 @@
     )(*args)
 
 
-def hold_kernel(*refs):
-    sem = refs[-1]
-    count = len(refs) // 2
-    copies = [
-        pltpu.make_async_copy(refs[m], refs[count + m], sem.at[m]) for m in range(count)
-    ]
+def hold_kernel(gate_hbm, up_hbm, down_hbm, gate_ref, up_ref, across_ref, down_buf, sem):
+    held, units, _ = down_buf.shape
+    refs = ((down_hbm, down_buf), (gate_hbm, gate_ref), (up_hbm, up_ref))
+    copies = [pltpu.make_async_copy(a, b, sem.at[m]) for m, (a, b) in enumerate(refs)]
     for copy in copies:
         copy.start()
-    for copy in copies:
+    copies[0].wait()
+
+    def turn(e, _):
+        for at in range(0, units, LANES):
+            cut = slice(at, at + LANES)
+            across_ref[e, :, cut] = down_buf[e, cut, :].T
+        return 0
+
+    lax.fori_loop(0, held, turn, 0)
+    for copy in copies[1:]:
         copy.wait()
 
 
-def hold(*arrays):
+def hold(w_gate, w_up, w_down):
+    held, units, width = w_down.shape
+    shapes = [w_gate.shape, w_up.shape, (held, width, units)]
     return pl.pallas_call(
         hold_kernel,
-        in_specs=[pl.BlockSpec(memory_space=pl.ANY)] * len(arrays),
-        out_specs=[pl.BlockSpec(memory_space=pltpu.VMEM)] * len(arrays),
-        out_shape=[pltpu.VMEM(a.shape, a.dtype) for a in arrays],
-        scratch_shapes=[pltpu.SemaphoreType.DMA((len(arrays),))],
+        in_specs=[pl.BlockSpec(memory_space=pl.ANY)] * 3,
+        out_specs=[pl.BlockSpec(memory_space=pltpu.VMEM)] * 3,
+        out_shape=[pltpu.VMEM(s, w_down.dtype) for s in shapes],
+        scratch_shapes=[pltpu.VMEM(w_down.shape, w_down.dtype), pltpu.SemaphoreType.DMA((3,))],
         compiler_params=pltpu.CompilerParams(vmem_limit_bytes=2 * VMEM_BYTES),
         cost_estimate=pl.CostEstimate(flops=0, bytes_accessed=2 * 10**6, transcendentals=0),
-    )(*arrays)
-
-
-def choose_kernel(inner_ref, outer_ref, out_ref, sem):
+    )(w_gate, w_up, w_down)
+
+
+def choose_kernel(inner_ref, outer_ref, out_ref, buf, sem):
     place = lax.axis_index("dp")
     inner = jnp.logical_and(place > 0, place < lax.axis_size("dp") - 1)
 
+    def move(source, target):
+        copy = pltpu.make_async_copy(source, target, sem)
+        copy.start()
+        copy.wait()
+
     @pl.when(inner)
     def _():
-        copy = pltpu.make_async_copy(inner_ref, out_ref, sem)
-        copy.start()
-        copy.wait()
+        move(inner_ref, buf)
 
     @pl.when(jnp.logical_not(inner))
     def _():
-        copy = pltpu.make_async_copy(outer_ref, out_ref, sem)
-        copy.start()
-        copy.wait()
+        move(outer_ref, buf)
+
+    move(buf, out_ref)
 
 
 def choose(inner, outer):
     return pl.pallas_call(
         choose_kernel,
-        in_specs=[pl.BlockSpec(memory_space=pltpu.HBM)] * 2,
+        in_specs=[pl.BlockSpec(memory_space=pl.ANY)] * 2,
         out_specs=pl.BlockSpec(memory_space=pltpu.HBM),
         out_shape=pltpu.HBM(inner.shape, inner.dtype),
-        scratch_shapes=[pltpu.SemaphoreType.DMA],
+        scratch_shapes=[pltpu.VMEM(inner.shape, inner.dtype), pltpu.SemaphoreType.DMA],
         compiler_params=pltpu.CompilerParams(vmem_limit_bytes=VMEM_BYTES),
         cost_estimate=pl.CostEstimate(flops=0, bytes_accessed=10**6, transcendentals=0),
     )(inner, outer)
@@ -422,30 +434,29 @@
     depth = depth_of(tok_dev, routes.shape[1], w_gate.shape[0] * lax.axis_size("expert"))
     tie = lax.optimization_barrier
     o0 = pack(tokens, grad_out, routes, combine)
-    x0, y0, o1, near = beside(o0), below(o0), swap(o0, "dp", 1), middle(o0)
+    near, o1, x0, y0 = middle(o0), swap(o0, "dp", 1), beside(o0), below(o0)
     group0 = pairs(o0)
     weights = hold(*tie((w_gate, w_up, w_down, o0))[:3])
-    x0, y0, o1, near, group0, weights = tie((x0, y0, o1, near, group0, weights))
     run = functools.partial(group, weights=weights, shards=shards, depth=depth)
-    x1, d0, near_end, far = beside(o1), below(x0), outward(near), middle(o1)
-    group0 += pairs(x0, y0, o1)
-    y0, near, group0 = tie((y0, near, group0))
-    *accs, even0, odd0 = run(group0, accs=None, own=6)
-    x1, d0, near_end, near, far, even0, odd0, y0 = tie(
-        (x1, d0, near_end, near, far, even0, odd0, y0)
-    )
+    *accs, mine, theirs = run(group0, accs=None, own=2)
+    near, o1, x0, y0, accs, theirs = tie((near, o1, x0, y0, accs, theirs))
+    near_end, far, d0, x1 = outward(near), middle(o1), below(x0), beside(o1)
+    group0 = pairs(x0, y0, o1)
+    y0, near, group0, accs = tie((y0, near, group0, accs))
+    *accs, even0, odd0 = run(group0, accs=accs, own=4)
+    near_end, near, even0, odd0 = tie((near_end, near, even0, odd0))
     o2 = choose(near, near_end)
+    far, d0, x1, o2, y0, odd0 = tie((far, d0, x1, o2, y0, odd0))
     x2, y2, far_end = beside(o2), below(o2), outward(far)
     crossed0 = swap(odd0, "expert", 1)
     group1 = pairs(d0, x1, o2)
     pair0 = (even0.astype(jnp.float32) + crossed0.astype(jnp.float32)).astype(jnp.bfloat16)
     group1, pair0, d0 = tie((group1, pair0, d0))
-    sent = [beside(pair0[1]), below(pair0[2])]
+    sent = [beside(pair0[0]), below(pair0[1])]
     *accs, even1, odd1 = run(group1, accs=accs, own=2)
-    x2, y2, far_end, y0, far, d0, even1, odd1, sent = tie(
-        (x2, y2, far_end, y0, far, d0, even1, odd1, sent)
-    )
+    far_end, far, even1, odd1 = tie((far_end, far, even1, odd1))
     o3 = choose(far, far_end)
+    x2, y2, y0, o3, d0, odd1, sent = tie((x2, y2, y0, o3, d0, odd1, sent))
     x3, y3, y1 = beside(o3), below(o3), swap(y0, "dp", 1)
     crossed1 = swap(odd1, "expert", 1)
     group2 = pairs(x2, y2, o3)
@@ -455,11 +466,11 @@
     x3, y3, y1, accs, pair1, d0, x2 = tie((x3, y3, y1, accs, pair1, d0, x2))
     d3, d2, d1 = beside(y3), below(x2), swap(d0, "dp", 1)
     accs = run(pairs(x3, y3, y1), accs=accs)
-    d3, d2, d1, accs, pair1 = tie((d3, d2, d1, accs, pair1))
-    sent.append(swap(pair1[0], "expert", 6))
+    d3, d2, d1, accs, pair1, theirs = tie((d3, d2, d1, accs, pair1, theirs))
+    sent += [swap(pair1[0], "expert", 6), swap(theirs[0], "expert", 1)]
     accs = run(pairs(d1, d2, d3), accs=accs, last=True)
     sent, accs = tie((sent, accs))
-    total = pair0[0].astype(jnp.float32)
+    total = mine[0].astype(jnp.float32)
     for piece in sent:
         total = total + piece.astype(jnp.float32)
     return (total.astype(jnp.bfloat16), *accs)

time: 121 us -> 120 us (level)
  waiting for transfers between devices: 24.2 us -> 19.4 us
  Pallas kernels: 61.2 us -> 64.1 us
    ppermute x34 -> x35, waiting for transfers between devices: 18.2 us -> 15.5 us  [swap(): return lax.ppermute(value, axis, [(i, i ^ bit) for i in range(size)])]
    pallas_call x5 -> x6, Pallas kernels: 53.8 us -> 56.3 us  [group(): pl.pallas_call(functools.partial(group_kernel, first, last, own, depth, b...]
    ppermute x2, waiting for transfers between devices: 5.94 us -> 3.96 us  [outward(): return lax.ppermute(value, 'dp', [(1, 0), (2, 3)])]
    ppermute x34 -> x35, starting transfers between devices: 27.5 us -> 28.2 us  [swap(): return lax.ppermute(value, axis, [(i, i ^ bit) for i in range(size)])]
  transfers between devices with their start and end apart: 38 -> 39, of which waited for: 15 -> 16; matrix products, arithmetic and copies ran while one was open for 0% -> 0% of each run, Pallas kernels for 49% -> 52%
where the time goes in v5:
time: 120 us
  Pallas kernels  64.1 us (53%)
  starting transfers between devices  32.9 us (27%)
  waiting for transfers between devices  19.4 us (16%)
    pallas_call x6, Pallas kernels, group(): pl.pallas_call(functools.partial(group_kernel, first, last, own, depth, b...  56.3 us
    ppermute x35, starting transfers between devices, swap(): return lax.ppermute(value, axis, [(i, i ^ bit) for i in range(size)])  28.2 us
    ppermute x35, waiting for transfers between devices, swap(): return lax.ppermute(value, axis, [(i, i ^ bit) for i in range(size)])  15.5 us
    ppermute x2, waiting for transfers between devices, outward(): return lax.ppermute(value, 'dp', [(1, 0), (2, 3)])  3.96 us
    pallas_call x1, Pallas kernels, hold(): pl.pallas_call(hold_kernel, in_specs=[pl.BlockSpec(memory_space=pl.ANY)]...  3.78 us
    ppermute x2, starting transfers between devices, outward(): return lax.ppermute(value, 'dp', [(1, 0), (2, 3)])  2.56 us
  transfers between devices with their start and end apart: 39, of which 16 were waited for; matrix products, arithmetic and copies ran while one was open for 0% of the time, Pallas kernels for 52%

profile of v5, /device:TPU:0, one launch (start us, length us, event | category | flops | bytes accessed | tf_op | source)
XLA Modules:
  0.0 119.7 jit_solution(6723741173906386491)
XLA Ops:
  0.6 2.0 %shard_map.102.refs_0_ = bf16[128,2176]{1,0:T(8,128)(2,1)} custom-call(bf16[128,1024]{1,0:T(8,128)(2,1)} %tok_ref.1, bf16[128,1024]{1,0:T(8,128)(2,1)} %dy_ref.1, s32[10,128]{1,0:T(8,128)} %bitcast.13, bf16[10,128]{1,0:T(8,128)(2,1)} %bitcast.14), custom_call_target="tpu_custom_call" | custom-call | flops 10000000 | bytes 2000000 | tf_op jit(solution)/shard_map/pallas_call | solution.py:155
  3.1 1.5 %collective-permute-start.1 = (bf16[128,2176]{1,0:T(8,128)(2,1)}, bf16[128,2176]{1,0:T(8,128)(2,1)}, u32[]{:S(2)}, u32[]{:S(2)}) collective-permute-start(bf16[128,2176]{1,0:T(8,128)(2,1)} %shard_map.102.refs_0_), channel_id=1, source_target_pairs={{8,16},{16,8},{9,17},{17,9},{10,18},{18,10},{11,19},{19,11},{12,20... | collective-permute-start | bytes 1671176 | tf_op jit(solution)/shard_map/ppermute | solution.py:424
  4.5 4.8 %collective-permute-start.2 = (bf16[128,2176]{1,0:T(8,128)(2,1)}, bf16[128,2176]{1,0:T(8,128)(2,1)S(1)}, u32[]{:S(2)}, u32[]{:S(2)}) collective-permute-start(bf16[128,2176]{1,0:T(8,128)(2,1)} %shard_map.102.refs_0_), channel_id=1, source_target_pairs={{0,8},{8,0},{16,24},{24,16},{1,9},{9,1},{17,25},{25,17},{2,10},{10... | collective-permute-start | bytes 1671176 | tf_op jit(solution)/shard_map/ppermute | solution.py:408
  9.4 1.5 %collective-permute-start.3 = (bf16[128,2176]{1,0:T(8,128)(2,1)}, bf16[128,2176]{1,0:T(8,128)(2,1)S(1)}, u32[]{:S(2)}, u32[]{:S(2)}) collective-permute-start(bf16[128,2176]{1,0:T(8,128)(2,1)} %shard_map.102.refs_0_), channel_id=1, source_target_pairs={{0,2},{1,3},{2,0},{3,1},{4,6},{5,7},{6,4},{7,5},{8,10},{9,11},{10,... | collective-permute-start | bytes 1671176 | tf_op jit(solution)/shard_map/ppermute | solution.py:408
  10.8 1.5 %collective-permute-start.4 = (bf16[128,2176]{1,0:T(8,128)(2,1)}, bf16[128,2176]{1,0:T(8,128)(2,1)S(1)}, u32[]{:S(2)}, u32[]{:S(2)}) collective-permute-start(bf16[128,2176]{1,0:T(8,128)(2,1)} %shard_map.102.refs_0_), channel_id=1, source_target_pairs={{0,4},{1,5},{2,6},{3,7},{4,0},{5,1},{6,2},{7,3},{8,12},{9,13},{10,... | collective-permute-start | bytes 1671176 | tf_op jit(solution)/shard_map/ppermute | solution.py:408
  12.4 3.8 %shard_map.103 = (bf16[3,1024,512]{2,1,0:T(8,128)(2,1)S(1)}, bf16[3,1024,512]{2,1,0:T(8,128)(2,1)S(1)}, bf16[3,1024,512]{2,1,0:T(8,128)(2,1)S(1)}) custom-call(bf16[3,1024,512]{2,1,0:T(8,128)(2,1)} %gate_hbm, bf16[3,1024,512]{2,1,0:T(8,128)(2,1)} %up_hbm, bf16[3,512,1024]{2,1,0:T(8,128)(2,1)} %down_hbm), custom_call_target="tpu_custom_call" | custom-call | bytes 2000000 | tf_op jit(solution)/shard_map/pallas_call | solution.py:363
  16.2 6.4 %shard_map.104 = (f32[3,256,512]{2,1,0:T(8,128)S(1)}, f32[3,256,512]{2,1,0:T(8,128)S(1)}, f32[3,128,1024]{2,1,0:T(8,128)S(1)}, bf16[1,128,1024]{2,1,0:T(8,128)(2,1)S(1)}, bf16[1,128,1024]{2,1,0:T(8,128)(2,1)S(1)}) custom-call(bf16[128,2176]{1,0:T(8,128)(2,1)S(1)} %copy-done.2, bf16[128,2176]{1,0:T(8,128)(2,1)S(1)} %collective-permute-done.refs_1_, ...), custom_call_target="tpu_custom_call" | custom-call | flops 50331648 | bytes 557056 | tf_op jit(solution)/shard_map/pallas_call | solution.py:325
  22.6 1.3 %collective-permute-done.3.refs_0_ = bf16[128,2176]{1,0:T(8,128)(2,1)S(1)} collective-permute-done((bf16[128,2176]{1,0:T(8,128)(2,1)}, bf16[128,2176]{1,0:T(8,128)(2,1)S(1)}, u32[]{:S(2)}, u32[]{:S(2)}) %collective-permute-start.3) | collective-permute-done | bytes 557088 | tf_op jit(solution)/shard_map/ppermute | solution.py:408
  23.9 1.2 %collective-permute-done.4.refs_2_ = bf16[128,2176]{1,0:T(8,128)(2,1)S(1)} collective-permute-done((bf16[128,2176]{1,0:T(8,128)(2,1)}, bf16[128,2176]{1,0:T(8,128)(2,1)S(1)}, u32[]{:S(2)}, u32[]{:S(2)}) %collective-permute-start.4) | collective-permute-done | bytes 557088 | tf_op jit(solution)/shard_map/ppermute | solution.py:408
  25.6 1.3 %collective-permute-start.8 = (bf16[128,2176]{1,0:T(8,128)(2,1)}, bf16[128,2176]{1,0:T(8,128)(2,1)S(1)}, u32[]{:S(2)}, u32[]{:S(2)}) collective-permute-start(bf16[128,2176]{1,0:T(8,128)(2,1)} %collective-permute-done.1.inner_ref), channel_id=1, source_target_pairs={{8,0},{16,24},{9,1},{17,25},{10,2},{18,26},{11,3},{19,27},{12,4},{... | collective-permute-start | bytes 1671176 | tf_op jit(solution)/shard_map/ppermute | solution.py:428
  27.6 1.6 %collective-permute-start.6 = (bf16[128,2176]{1,0:T(8,128)(2,1)S(1)}, bf16[128,2176]{1,0:T(8,128)(2,1)S(1)}, u32[]{:S(2)}, u32[]{:S(2)}) collective-permute-start(bf16[128,2176]{1,0:T(8,128)(2,1)S(1)} %collective-permute-done.3.refs_0_), channel_id=1, source_target_pairs={{0,4},{1,5},{2,6},{3,7},{4,0},{5,1},{6,2},{7,3},{8,12},{9,13},{10,... | collective-permute-start | bytes 1671176 | tf_op jit(solution)/shard_map/ppermute | solution.py:408
  29.8 11.8 %shard_map.105 = (f32[3,256,512]{2,1,0:T(8,128)S(1)}, f32[3,256,512]{2,1,0:T(8,128)S(1)}, f32[3,128,1024]{2,1,0:T(8,128)S(1)}, bf16[2,128,1024]{2,1,0:T(8,128)(2,1)S(1)}, bf16[2,128,1024]{2,1,0:T(8,128)(2,1)S(1)}) custom-call(bf16[128,2176]{1,0:T(8,128)(2,1)S(1)} %collective-permute-done.3.refs_0_, ...), custom_call_target="tpu_custom_call", output_to_operand_aliasing={{0}: (9, {}), {1}: (10, {}), {2}: (11, {})} | custom-call | flops 150994944 | bytes 557056 | tf_op jit(solution)/shard_map/pallas_call | solution.py:325
  41.6 1.2 collective-permute-done.8.outer_ref
  45.5 1.9 %collective-permute-done.18 = bf16[2,128,1024]{2,1,0:T(8,128)(2,1)S(1)} collective-permute-done((bf16[2,128,1024]{2,1,0:T(8,128)(2,1)S(1)}, bf16[2,128,1024]{2,1,0:T(8,128)(2,1)S(1)}, u32[]{:S(2)}, u32[]{:S(2)}) %collective-permute-start.18) | collective-permute-done | bytes 524320 | tf_op jit(solution)/shard_map/ppermute | solution.py:408
  47.4 1.3 %collective-permute-start.13 = (bf16[128,2176]{1,0:T(8,128)(2,1)}, bf16[128,2176]{1,0:T(8,128)(2,1)S(1)}, u32[]{:S(2)}, u32[]{:S(2)}) collective-permute-start(bf16[128,2176]{1,0:T(8,128)(2,1)} %shard_map.106.refs_4_), channel_id=1, source_target_pairs={{0,4},{1,5},{2,6},{3,7},{4,0},{5,1},{6,2},{7,3},{8,12},{9,13},{10,... | collective-permute-start | bytes 1671176 | tf_op jit(solution)/shard_map/ppermute | solution.py:408
  48.7 1.3 %collective-permute-start.14 = (bf16[128,2176]{1,0:T(8,128)(2,1)S(1)}, bf16[128,2176]{1,0:T(8,128)(2,1)S(1)}, u32[]{:S(2)}, u32[]{:S(2)}) collective-permute-start(bf16[128,2176]{1,0:T(8,128)(2,1)S(1)} %collective-permute-done.5.inner_ref), channel_id=1, source_target_pairs={{8,0},{16,24},{9,1},{17,25},{10,2},{18,26},{11,3},{19,27},{12,4},{... | collective-permute-start | bytes 1671176 | tf_op jit(solution)/shard_map/ppermute | solution.py:428
  51.6 11.4 %shard_map.107 = (f32[3,256,512]{2,1,0:T(8,128)S(1)}, f32[3,256,512]{2,1,0:T(8,128)S(1)}, f32[3,128,1024]{2,1,0:T(8,128)S(1)}, bf16[1,128,1024]{2,1,0:T(8,128)(2,1)S(1)}, bf16[1,128,1024]{2,1,0:T(8,128)(2,1)S(1)}) custom-call(bf16[128,2176]{1,0:T(8,128)(2,1)S(1)} %collective-permute-done.6.refs_0_, ...), custom_call_target="tpu_custom_call", output_to_operand_aliasing={{0}: (9, {}), {1}: (10, {}), {2}: (11, {})} | custom-call | flops 150994944 | bytes 557056 | tf_op jit(solution)/shard_map/pallas_call | solution.py:325
  63.0 2.8 %collective-permute-done.14.outer_ref = bf16[128,2176]{1,0:T(8,128)(2,1)S(1)} collective-permute-done((bf16[128,2176]{1,0:T(8,128)(2,1)S(1)}, bf16[128,2176]{1,0:T(8,128)(2,1)S(1)}, u32[]{:S(2)}, u32[]{:S(2)}) %collective-permute-start.14) | collective-permute-done | bytes 557088 | tf_op jit(solution)/shard_map/ppermute | solution.py:428
  65.8 1.1 shard_map.108.refs_4_
  69.5 1.1 collective-permute-done.27
  70.6 1.3 %collective-permute-start.22 = (bf16[128,2176]{1,0:T(8,128)(2,1)}, bf16[128,2176]{1,0:T(8,128)(2,1)S(1)}, u32[]{:S(2)}, u32[]{:S(2)}) collective-permute-start(bf16[128,2176]{1,0:T(8,128)(2,1)} %shard_map.108.refs_4_), channel_id=1, source_target_pairs={{0,4},{1,5},{2,6},{3,7},{4,0},{5,1},{6,2},{7,3},{8,12},{9,13},{10,... | collective-permute-start | bytes 1671176 | tf_op jit(solution)/shard_map/ppermute | solution.py:408
  71.9 3.2 %collective-permute-start.23 = (bf16[128,2176]{1,0:T(8,128)(2,1)S(1)}, bf16[128,2176]{1,0:T(8,128)(2,1)S(1)}, u32[]{:S(2)}, u32[]{:S(2)}) collective-permute-start(bf16[128,2176]{1,0:T(8,128)(2,1)S(1)} %collective-permute-done.4.refs_2_), channel_id=1, source_target_pairs={{0,8},{8,0},{16,24},{24,16},{1,9},{9,1},{17,25},{25,17},{2,10},{10... | collective-permute-start | bytes 1671176 | tf_op jit(solution)/shard_map/ppermute | solution.py:408
  76.2 8.7 %shard_map.109 = (f32[3,256,512]{2,1,0:T(8,128)S(1)}, f32[3,256,512]{2,1,0:T(8,128)S(1)}, f32[3,128,1024]{2,1,0:T(8,128)S(1)}) custom-call(bf16[128,2176]{1,0:T(8,128)(2,1)S(1)} %collective-permute-done.12.refs_0_, bf16[128,2176]{1,0:T(8,128)(2,1)S(1)} %collective-permute-done.24.refs_1_, ...), custom_call_target="tpu_custom_call", output_to_operand_aliasing={{0}: (9, {}), {1}: (10, {}), {2}: (11, {})} | custom-call | flops 150994944 | bytes 557056 | tf_op jit(solution)/shard_map/pallas_call | solution.py:325
  85.5 2.2 %collective-permute-done.23.refs_4_ = bf16[128,2176]{1,0:T(8,128)(2,1)S(1)} collective-permute-done((bf16[128,2176]{1,0:T(8,128)(2,1)S(1)}, bf16[128,2176]{1,0:T(8,128)(2,1)S(1)}, u32[]{:S(2)}, u32[]{:S(2)}) %collective-permute-start.23) | collective-permute-done | bytes 557088 | tf_op jit(solution)/shard_map/ppermute | solution.py:408
  88.3 1.5 %collective-permute-start.28 = (bf16[128,2176]{1,0:T(8,128)(2,1)S(1)}, bf16[128,2176]{1,0:T(8,128)(2,1)S(1)}, u32[]{:S(2)}, u32[]{:S(2)}) collective-permute-start(bf16[128,2176]{1,0:T(8,128)(2,1)S(1)} %collective-permute-done.22.refs_2_), channel_id=1, source_target_pairs={{0,2},{1,3},{2,0},{3,1},{4,6},{5,7},{6,4},{7,5},{8,10},{9,11},{10,... | collective-permute-start | bytes 1671176 | tf_op jit(solution)/shard_map/ppermute | solution.py:408
  89.8 1.5 %collective-permute-start.29 = (bf16[128,2176]{1,0:T(8,128)(2,1)S(1)}, bf16[128,2176]{1,0:T(8,128)(2,1)S(1)}, u32[]{:S(2)}, u32[]{:S(2)}) collective-permute-start(bf16[128,2176]{1,0:T(8,128)(2,1)S(1)} %collective-permute-done.12.refs_0_), channel_id=1, source_target_pairs={{0,4},{1,5},{2,6},{3,7},{4,0},{5,1},{6,2},{7,3},{8,12},{9,13},{10,... | collective-permute-start | bytes 1671176 | tf_op jit(solution)/shard_map/ppermute | solution.py:408
  91.3 1.7 %collective-permute-start.30 = (bf16[128,2176]{1,0:T(8,128)(2,1)S(1)}, bf16[128,2176]{1,0:T(8,128)(2,1)S(1)}, u32[]{:S(2)}, u32[]{:S(2)}) collective-permute-start(bf16[128,2176]{1,0:T(8,128)(2,1)S(1)} %collective-permute-done.6.refs_0_), channel_id=1, source_target_pairs={{0,8},{8,0},{16,24},{24,16},{1,9},{9,1},{17,25},{25,17},{2,10},{10... | collective-permute-start | bytes 1671176 | tf_op jit(solution)/shard_map/ppermute | solution.py:408
  93.0 8.7 %shard_map.110 = (f32[3,256,512]{2,1,0:T(8,128)S(1)}, f32[3,256,512]{2,1,0:T(8,128)S(1)}, f32[3,128,1024]{2,1,0:T(8,128)S(1)}) custom-call(bf16[128,2176]{1,0:T(8,128)(2,1)S(1)} %collective-permute-done.21.refs_0_, bf16[128,2176]{1,0:T(8,128)(2,1)S(1)} %collective-permute-done.31.refs_1_, ...), custom_call_target="tpu_custom_call", output_to_operand_aliasing={{0}: (9, {}), {1}: (10, {}), {2}: (11, {})} | custom-call | flops 150994944 | bytes 557056 | tf_op jit(solution)/shard_map/pallas_call | solution.py:325
  101.7 1.6 %collective-permute-done.28.refs_4_ = bf16[128,2176]{1,0:T(8,128)(2,1)S(1)} collective-permute-done((bf16[128,2176]{1,0:T(8,128)(2,1)S(1)}, bf16[128,2176]{1,0:T(8,128)(2,1)S(1)}, u32[]{:S(2)}, u32[]{:S(2)}) %collective-permute-start.28) | collective-permute-done | bytes 557088 | tf_op jit(solution)/shard_map/ppermute | solution.py:408
  103.3 1.2 %collective-permute-done.29.refs_2_ = bf16[128,2176]{1,0:T(8,128)(2,1)S(1)} collective-permute-done((bf16[128,2176]{1,0:T(8,128)(2,1)S(1)}, bf16[128,2176]{1,0:T(8,128)(2,1)S(1)}, u32[]{:S(2)}, u32[]{:S(2)}) %collective-permute-start.29) | collective-permute-done | bytes 557088 | tf_op jit(solution)/shard_map/ppermute | solution.py:408
  104.5 1.2 %collective-permute-done.30.refs_0_ = bf16[128,2176]{1,0:T(8,128)(2,1)S(1)} collective-permute-done((bf16[128,2176]{1,0:T(8,128)(2,1)S(1)}, bf16[128,2176]{1,0:T(8,128)(2,1)S(1)}, u32[]{:S(2)}, u32[]{:S(2)}) %collective-permute-start.30) | collective-permute-done | bytes 557088 | tf_op jit(solution)/shard_map/ppermute | solution.py:408
  109.3 9.4 %shard_map.111 = (bf16[3,256,512]{2,1,0:T(8,128)(2,1)}, bf16[3,256,512]{2,1,0:T(8,128)(2,1)}, bf16[3,128,1024]{2,1,0:T(8,128)(2,1)}) custom-call(bf16[128,2176]{1,0:T(8,128)(2,1)S(1)} %collective-permute-done.30.refs_0_, bf16[128,2176]{1,0:T(8,128)(2,1)S(1)} %collective-permute-done.36.refs_1_, bf16[128,2176]{1,0:T(8,128)(2,1)S(1)} %collective-permute-done.29.refs_2_, ...), custom_call_target="tpu_custom_call" | custom-call | flops 150994944 | bytes 557056 | tf_op jit(solution)/shard_map/pallas_call | solution.py:325
  (66 shorter events, 15.8 us)
Async XLA Ops:
  2.6 13.5 %collective-permute-start = (bf16[128,2176]{1,0:T(8,128)(2,1)}, bf16[128,2176]{1,0:T(8,128)(2,1)S(1)}, u32[]{:S(2)}, u32[]{:S(2)}) collective-permute-start(bf16[128,2176]{1,0:T(8,128)(2,1)} %shard_map.102.refs_0_), channel_id=1, source_target_pairs={{0,1},{1,0},{2,3},{3,2},{4,5},{5,4},{6,7},{7,6},{8,9},{9,8},{10,11... | collective-permute-start | bytes 1671176 | tf_op jit(solution)/shard_map/ppermute | solution.py:408
  3.1 19.5 %collective-permute-start.1 = (bf16[128,2176]{1,0:T(8,128)(2,1)}, bf16[128,2176]{1,0:T(8,128)(2,1)}, u32[]{:S(2)}, u32[]{:S(2)}) collective-permute-start(bf16[128,2176]{1,0:T(8,128)(2,1)} %shard_map.102.refs_0_), channel_id=1, source_target_pairs={{8,16},{16,8},{9,17},{17,9},{10,18},{18,10},{11,19},{19,11},{12,20... | collective-permute-start | bytes 1671176 | tf_op jit(solution)/shard_map/ppermute | solution.py:424
  4.5 18.0 %collective-permute-start.2 = (bf16[128,2176]{1,0:T(8,128)(2,1)}, bf16[128,2176]{1,0:T(8,128)(2,1)S(1)}, u32[]{:S(2)}, u32[]{:S(2)}) collective-permute-start(bf16[128,2176]{1,0:T(8,128)(2,1)} %shard_map.102.refs_0_), channel_id=1, source_target_pairs={{0,8},{8,0},{16,24},{24,16},{1,9},{9,1},{17,25},{25,17},{2,10},{10... | collective-permute-start | bytes 1671176 | tf_op jit(solution)/shard_map/ppermute | solution.py:408
  9.4 14.5 %collective-permute-start.3 = (bf16[128,2176]{1,0:T(8,128)(2,1)}, bf16[128,2176]{1,0:T(8,128)(2,1)S(1)}, u32[]{:S(2)}, u32[]{:S(2)}) collective-permute-start(bf16[128,2176]{1,0:T(8,128)(2,1)} %shard_map.102.refs_0_), channel_id=1, source_target_pairs={{0,2},{1,3},{2,0},{3,1},{4,6},{5,7},{6,4},{7,5},{8,10},{9,11},{10,... | collective-permute-start | bytes 1671176 | tf_op jit(solution)/shard_map/ppermute | solution.py:408
  10.8 14.3 %collective-permute-start.4 = (bf16[128,2176]{1,0:T(8,128)(2,1)}, bf16[128,2176]{1,0:T(8,128)(2,1)S(1)}, u32[]{:S(2)}, u32[]{:S(2)}) collective-permute-start(bf16[128,2176]{1,0:T(8,128)(2,1)} %shard_map.102.refs_0_), channel_id=1, source_target_pairs={{0,4},{1,5},{2,6},{3,7},{4,0},{5,1},{6,2},{7,3},{8,12},{9,13},{10,... | collective-permute-start | bytes 1671176 | tf_op jit(solution)/shard_map/ppermute | solution.py:408
  25.1 4.1 %collective-permute-start.11 = (bf16[128,2176]{1,0:T(8,128)(2,1)S(1)}, bf16[128,2176]{1,0:T(8,128)(2,1)S(1)}, u32[]{:S(2)}, u32[]{:S(2)}) collective-permute-start(bf16[128,2176]{1,0:T(8,128)(2,1)S(1)} %collective-permute-done.2.refs_4_), channel_id=1, source_target_pairs={{0,1},{1,0},{2,3},{3,2},{4,5},{5,4},{6,7},{7,6},{8,9},{9,8},{10,11... | collective-permute-start | bytes 1671176 | tf_op jit(solution)/shard_map/ppermute | solution.py:408
  25.6 4.1 %collective-permute-start.9 = (bf16[128,2176]{1,0:T(8,128)(2,1)S(1)}, bf16[128,2176]{1,0:T(8,128)(2,1)S(1)}, u32[]{:S(2)}, u32[]{:S(2)}) collective-permute-start(bf16[128,2176]{1,0:T(8,128)(2,1)S(1)} %collective-permute-done.3.refs_0_), channel_id=1, source_target_pairs={{0,1},{1,0},{2,3},{3,2},{4,5},{5,4},{6,7},{7,6},{8,9},{9,8},{10,11... | collective-permute-start | bytes 1671176 | tf_op jit(solution)/shard_map/ppermute | solution.py:408
  25.6 17.1 %collective-permute-start.8 = (bf16[128,2176]{1,0:T(8,128)(2,1)}, bf16[128,2176]{1,0:T(8,128)(2,1)S(1)}, u32[]{:S(2)}, u32[]{:S(2)}) collective-permute-start(bf16[128,2176]{1,0:T(8,128)(2,1)} %collective-permute-done.1.inner_ref), channel_id=1, source_target_pairs={{8,0},{16,24},{9,1},{17,25},{10,2},{18,26},{11,3},{19,27},{12,4},{... | collective-permute-start | bytes 1671176 | tf_op jit(solution)/shard_map/ppermute | solution.py:428
  26.9 16.8 %collective-permute-start.5 = (bf16[128,2176]{1,0:T(8,128)(2,1)S(1)}, bf16[128,2176]{1,0:T(8,128)(2,1)S(1)}, u32[]{:S(2)}, u32[]{:S(2)}) collective-permute-start(bf16[128,2176]{1,0:T(8,128)(2,1)S(1)} %collective-permute-done.2.refs_4_), channel_id=1, source_target_pairs={{8,16},{16,8},{9,17},{17,9},{10,18},{18,10},{11,19},{19,11},{12,20... | collective-permute-start | bytes 1671176 | tf_op jit(solution)/shard_map/ppermute | solution.py:424
  27.6 16.0 %collective-permute-start.6 = (bf16[128,2176]{1,0:T(8,128)(2,1)S(1)}, bf16[128,2176]{1,0:T(8,128)(2,1)S(1)}, u32[]{:S(2)}, u32[]{:S(2)}) collective-permute-start(bf16[128,2176]{1,0:T(8,128)(2,1)S(1)} %collective-permute-done.3.refs_0_), channel_id=1, source_target_pairs={{0,4},{1,5},{2,6},{3,7},{4,0},{5,1},{6,2},{7,3},{8,12},{9,13},{10,... | collective-permute-start | bytes 1671176 | tf_op jit(solution)/shard_map/ppermute | solution.py:408
  29.2 14.8 %collective-permute-start.7 = (bf16[128,2176]{1,0:T(8,128)(2,1)S(1)}, bf16[128,2176]{1,0:T(8,128)(2,1)S(1)}, u32[]{:S(2)}, u32[]{:S(2)}) collective-permute-start(bf16[128,2176]{1,0:T(8,128)(2,1)S(1)} %collective-permute-done.2.refs_4_), channel_id=1, source_target_pairs={{0,2},{1,3},{2,0},{3,1},{4,6},{5,7},{6,4},{7,5},{8,10},{9,11},{10,... | collective-permute-start | bytes 1671176 | tf_op jit(solution)/shard_map/ppermute | solution.py:408
  44.0 4.8 %collective-permute-start.15 = (bf16[128,2176]{1,0:T(8,128)(2,1)S(1)}, bf16[128,2176]{1,0:T(8,128)(2,1)S(1)}, u32[]{:S(2)}, u32[]{:S(2)}) collective-permute-start(bf16[128,2176]{1,0:T(8,128)(2,1)S(1)} %collective-permute-done.6.refs_0_), channel_id=1, source_target_pairs={{0,1},{1,0},{2,3},{3,2},{4,5},{5,4},{6,7},{7,6},{8,9},{9,8},{10,11... | collective-permute-start | bytes 1671176 | tf_op jit(solution)/shard_map/ppermute | solution.py:408
  44.5 5.7 %collective-permute-start.16 = (bf16[128,2176]{1,0:T(8,128)(2,1)S(1)}, bf16[128,2176]{1,0:T(8,128)(2,1)S(1)}, u32[]{:S(2)}, u32[]{:S(2)}) collective-permute-start(bf16[128,2176]{1,0:T(8,128)(2,1)S(1)} %collective-permute-done.7.refs_2_), channel_id=1, source_target_pairs={{0,1},{1,0},{2,3},{3,2},{4,5},{5,4},{6,7},{7,6},{8,9},{9,8},{10,11... | collective-permute-start | bytes 1671176 | tf_op jit(solution)/shard_map/ppermute | solution.py:408
  44.5 5.8 %collective-permute-start.17 = (bf16[128,2176]{1,0:T(8,128)(2,1)}, bf16[128,2176]{1,0:T(8,128)(2,1)S(1)}, u32[]{:S(2)}, u32[]{:S(2)}) collective-permute-start(bf16[128,2176]{1,0:T(8,128)(2,1)} %shard_map.106.refs_4_), channel_id=1, source_target_pairs={{0,1},{1,0},{2,3},{3,2},{4,5},{5,4},{6,7},{7,6},{8,9},{9,8},{10,11... | collective-permute-start | bytes 1671176 | tf_op jit(solution)/shard_map/ppermute | solution.py:408
  45.0 21.9 %collective-permute-start.12 = (bf16[128,2176]{1,0:T(8,128)(2,1)}, bf16[128,2176]{1,0:T(8,128)(2,1)S(1)}, u32[]{:S(2)}, u32[]{:S(2)}) collective-permute-start(bf16[128,2176]{1,0:T(8,128)(2,1)} %shard_map.106.refs_4_), channel_id=1, source_target_pairs={{0,2},{1,3},{2,0},{3,1},{4,6},{5,7},{6,4},{7,5},{8,10},{9,11},{10,... | collective-permute-start | bytes 1671176 | tf_op jit(solution)/shard_map/ppermute | solution.py:408
  47.4 19.5 %collective-permute-start.13 = (bf16[128,2176]{1,0:T(8,128)(2,1)}, bf16[128,2176]{1,0:T(8,128)(2,1)S(1)}, u32[]{:S(2)}, u32[]{:S(2)}) collective-permute-start(bf16[128,2176]{1,0:T(8,128)(2,1)} %shard_map.106.refs_4_), channel_id=1, source_target_pairs={{0,4},{1,5},{2,6},{3,7},{4,0},{5,1},{6,2},{7,3},{8,12},{9,13},{10,... | collective-permute-start | bytes 1671176 | tf_op jit(solution)/shard_map/ppermute | solution.py:408
  48.7 17.1 %collective-permute-start.14 = (bf16[128,2176]{1,0:T(8,128)(2,1)S(1)}, bf16[128,2176]{1,0:T(8,128)(2,1)S(1)}, u32[]{:S(2)}, u32[]{:S(2)}) collective-permute-start(bf16[128,2176]{1,0:T(8,128)(2,1)S(1)} %collective-permute-done.5.inner_ref), channel_id=1, source_target_pairs={{8,0},{16,24},{9,1},{17,25},{10,2},{18,26},{11,3},{19,27},{12,4},{... | collective-permute-start | bytes 1671176 | tf_op jit(solution)/shard_map/ppermute | solution.py:428
  50.3 16.6 %collective-permute-start.19 = (bf16[128,1024]{1,0:T(8,128)(2,1)S(1)}, bf16[128,1024]{1,0:T(8,128)(2,1)S(1)}, u32[]{:S(2)}, u32[]{:S(2)}) collective-permute-start(bf16[128,1024]{1,0:T(8,128)(2,1)S(1)} %get-tuple-element.225), channel_id=1, source_target_pairs={{0,2},{1,3},{2,0},{3,1},{4,6},{5,7},{6,4},{7,5},{8,10},{9,11},{10,... | collective-permute-start | bytes 786440 | tf_op jit(solution)/shard_map/ppermute | solution.py:408
  50.9 17.0 %collective-permute-start.20 = (bf16[128,1024]{1,0:T(8,128)(2,1)S(1)}, bf16[128,1024]{1,0:T(8,128)(2,1)S(1)}, u32[]{:S(2)}, u32[]{:S(2)}) collective-permute-start(bf16[128,1024]{1,0:T(8,128)(2,1)S(1)} %get-tuple-element.224), channel_id=1, source_target_pairs={{0,4},{1,5},{2,6},{3,7},{4,0},{5,1},{6,2},{7,3},{8,12},{9,13},{10,... | collective-permute-start | bytes 786440 | tf_op jit(solution)/shard_map/ppermute | solution.py:408
  67.9 4.0 %collective-permute-start.24 = (bf16[128,2176]{1,0:T(8,128)(2,1)S(1)}, bf16[128,2176]{1,0:T(8,128)(2,1)S(1)}, u32[]{:S(2)}, u32[]{:S(2)}) collective-permute-start(bf16[128,2176]{1,0:T(8,128)(2,1)S(1)} %collective-permute-done.12.refs_0_), channel_id=1, source_target_pairs={{0,1},{1,0},{2,3},{3,2},{4,5},{5,4},{6,7},{7,6},{8,9},{9,8},{10,11... | collective-permute-start | bytes 1671176 | tf_op jit(solution)/shard_map/ppermute | solution.py:408
  68.4 6.7 %collective-permute-start.25 = (bf16[128,2176]{1,0:T(8,128)(2,1)S(1)}, bf16[128,2176]{1,0:T(8,128)(2,1)S(1)}, u32[]{:S(2)}, u32[]{:S(2)}) collective-permute-start(bf16[128,2176]{1,0:T(8,128)(2,1)S(1)} %collective-permute-done.13.refs_2_), channel_id=1, source_target_pairs={{0,1},{1,0},{2,3},{3,2},{4,5},{5,4},{6,7},{7,6},{8,9},{9,8},{10,11... | collective-permute-start | bytes 1671176 | tf_op jit(solution)/shard_map/ppermute | solution.py:408
  68.4 6.7 %collective-permute-start.26 = (bf16[128,2176]{1,0:T(8,128)(2,1)}, bf16[128,2176]{1,0:T(8,128)(2,1)S(1)}, u32[]{:S(2)}, u32[]{:S(2)}) collective-permute-start(bf16[128,2176]{1,0:T(8,128)(2,1)} %shard_map.108.refs_4_), channel_id=1, source_target_pairs={{0,1},{1,0},{2,3},{3,2},{4,5},{5,4},{6,7},{7,6},{8,9},{9,8},{10,11... | collective-permute-start | bytes 1671176 | tf_op jit(solution)/shard_map/ppermute | solution.py:408
  68.9 16.0 %collective-permute-start.21 = (bf16[128,2176]{1,0:T(8,128)(2,1)}, bf16[128,2176]{1,0:T(8,128)(2,1)S(1)}, u32[]{:S(2)}, u32[]{:S(2)}) collective-permute-start(bf16[128,2176]{1,0:T(8,128)(2,1)} %shard_map.108.refs_4_), channel_id=1, source_target_pairs={{0,2},{1,3},{2,0},{3,1},{4,6},{5,7},{6,4},{7,5},{8,10},{9,11},{10,... | collective-permute-start | bytes 1671176 | tf_op jit(solution)/shard_map/ppermute | solution.py:408
  70.6 14.9 %collective-permute-start.22 = (bf16[128,2176]{1,0:T(8,128)(2,1)}, bf16[128,2176]{1,0:T(8,128)(2,1)S(1)}, u32[]{:S(2)}, u32[]{:S(2)}) collective-permute-start(bf16[128,2176]{1,0:T(8,128)(2,1)} %shard_map.108.refs_4_), channel_id=1, source_target_pairs={{0,4},{1,5},{2,6},{3,7},{4,0},{5,1},{6,2},{7,3},{8,12},{9,13},{10,... | collective-permute-start | bytes 1671176 | tf_op jit(solution)/shard_map/ppermute | solution.py:408
  71.9 15.8 %collective-permute-start.23 = (bf16[128,2176]{1,0:T(8,128)(2,1)S(1)}, bf16[128,2176]{1,0:T(8,128)(2,1)S(1)}, u32[]{:S(2)}, u32[]{:S(2)}) collective-permute-start(bf16[128,2176]{1,0:T(8,128)(2,1)S(1)} %collective-permute-done.4.refs_2_), channel_id=1, source_target_pairs={{0,8},{8,0},{16,24},{24,16},{1,9},{9,1},{17,25},{25,17},{2,10},{10... | collective-permute-start | bytes 1671176 | tf_op jit(solution)/shard_map/ppermute | solution.py:408
  87.8 5.3 %collective-permute-start.32 = (bf16[128,2176]{1,0:T(8,128)(2,1)S(1)}, bf16[128,2176]{1,0:T(8,128)(2,1)S(1)}, u32[]{:S(2)}, u32[]{:S(2)}) collective-permute-start(bf16[128,2176]{1,0:T(8,128)(2,1)S(1)} %collective-permute-done.22.refs_2_), channel_id=1, source_target_pairs={{0,1},{1,0},{2,3},{3,2},{4,5},{5,4},{6,7},{7,6},{8,9},{9,8},{10,11... | collective-permute-start | bytes 1671176 | tf_op jit(solution)/shard_map/ppermute | solution.py:408
  88.3 4.8 %collective-permute-start.33 = (bf16[128,2176]{1,0:T(8,128)(2,1)S(1)}, bf16[128,2176]{1,0:T(8,128)(2,1)S(1)}, u32[]{:S(2)}, u32[]{:S(2)}) collective-permute-start(bf16[128,2176]{1,0:T(8,128)(2,1)S(1)} %collective-permute-done.23.refs_4_), channel_id=1, source_target_pairs={{0,1},{1,0},{2,3},{3,2},{4,5},{5,4},{6,7},{7,6},{8,9},{9,8},{10,11... | collective-permute-start | bytes 1671176 | tf_op jit(solution)/shard_map/ppermute | solution.py:408
  88.3 15.0 %collective-permute-start.28 = (bf16[128,2176]{1,0:T(8,128)(2,1)S(1)}, bf16[128,2176]{1,0:T(8,128)(2,1)S(1)}, u32[]{:S(2)}, u32[]{:S(2)}) collective-permute-start(bf16[128,2176]{1,0:T(8,128)(2,1)S(1)} %collective-permute-done.22.refs_2_), channel_id=1, source_target_pairs={{0,2},{1,3},{2,0},{3,1},{4,6},{5,7},{6,4},{7,5},{8,10},{9,11},{10,... | collective-permute-start | bytes 1671176 | tf_op jit(solution)/shard_map/ppermute | solution.py:408
  89.8 14.8 %collective-permute-start.29 = (bf16[128,2176]{1,0:T(8,128)(2,1)S(1)}, bf16[128,2176]{1,0:T(8,128)(2,1)S(1)}, u32[]{:S(2)}, u32[]{:S(2)}) collective-permute-start(bf16[128,2176]{1,0:T(8,128)(2,1)S(1)} %collective-permute-done.12.refs_0_), channel_id=1, source_target_pairs={{0,4},{1,5},{2,6},{3,7},{4,0},{5,1},{6,2},{7,3},{8,12},{9,13},{10,... | collective-permute-start | bytes 1671176 | tf_op jit(solution)/shard_map/ppermute | solution.py:408
  91.3 14.5 %collective-permute-start.30 = (bf16[128,2176]{1,0:T(8,128)(2,1)S(1)}, bf16[128,2176]{1,0:T(8,128)(2,1)S(1)}, u32[]{:S(2)}, u32[]{:S(2)}) collective-permute-start(bf16[128,2176]{1,0:T(8,128)(2,1)S(1)} %collective-permute-done.6.refs_0_), channel_id=1, source_target_pairs={{0,8},{8,0},{16,24},{24,16},{1,9},{9,1},{17,25},{25,17},{2,10},{10... | collective-permute-start | bytes 1671176 | tf_op jit(solution)/shard_map/ppermute | solution.py:408
  106.3 12.4 %collective-permute-start.34 = (bf16[128,1024]{1,0:T(8,128)(2,1)S(1)}, bf16[128,1024]{1,0:T(8,128)(2,1)S(1)}, u32[]{:S(2)}, u32[]{:S(2)}) collective-permute-start(bf16[128,1024]{1,0:T(8,128)(2,1)S(1)} %bitcast.12), channel_id=1, source_target_pairs={{0,6},{1,7},{2,4},{3,5},{4,2},{5,3},{6,0},{7,1},{8,14},{9,15},{10,... | collective-permute-start | bytes 786440 | tf_op jit(solution)/shard_map/ppermute | solution.py:408
  107.4 11.4 %collective-permute-start.35 = (bf16[128,1024]{1,0:T(8,128)(2,1)S(1)}, bf16[128,1024]{1,0:T(8,128)(2,1)S(1)}, u32[]{:S(2)}, u32[]{:S(2)}) collective-permute-start(bf16[128,1024]{1,0:T(8,128)(2,1)S(1)} %bitcast.11), channel_id=1, source_target_pairs={{0,1},{1,0},{2,3},{3,2},{4,5},{5,4},{6,7},{7,6},{8,9},{9,8},{10,11... | collective-permute-start | bytes 786440 | tf_op jit(solution)/shard_map/ppermute | solution.py:408
  (10 other events, 42.5 us)

commit v6 on v5

--- a/solution.py
+++ b/solution.py
@@ -434,12 +434,12 @@
     depth = depth_of(tok_dev, routes.shape[1], w_gate.shape[0] * lax.axis_size("expert"))
     tie = lax.optimization_barrier
     o0 = pack(tokens, grad_out, routes, combine)
-    near, o1, x0, y0 = middle(o0), swap(o0, "dp", 1), beside(o0), below(o0)
+    x0, y0, o1, near = beside(o0), below(o0), swap(o0, "dp", 1), middle(o0)
     group0 = pairs(o0)
     weights = hold(*tie((w_gate, w_up, w_down, o0))[:3])
     run = functools.partial(group, weights=weights, shards=shards, depth=depth)
     *accs, mine, theirs = run(group0, accs=None, own=2)
-    near, o1, x0, y0, accs, theirs = tie((near, o1, x0, y0, accs, theirs))
+    x0, y0, o1, near, accs, theirs = tie((x0, y0, o1, near, accs, theirs))
     near_end, far, d0, x1 = outward(near), middle(o1), below(x0), beside(o1)
     group0 = pairs(x0, y0, o1)
     y0, near, group0, accs = tie((y0, near, group0, accs))
@@ -463,7 +463,7 @@
     group2, crossed1 = tie((group2, crossed1))
     pair1 = (even1.astype(jnp.float32) + crossed1.astype(jnp.float32)).astype(jnp.bfloat16)
     accs = run(group2, accs=accs)
-    x3, y3, y1, accs, pair1, d0, x2 = tie((x3, y3, y1, accs, pair1, d0, x2))
+    x3, y3, accs, pair1, d0, x2 = tie((x3, y3, accs, pair1, d0, x2))
     d3, d2, d1 = beside(y3), below(x2), swap(d0, "dp", 1)
     accs = run(pairs(x3, y3, y1), accs=accs)
     d3, d2, d1, accs, pair1, theirs = tie((d3, d2, d1, accs, pair1, theirs))

time: 120 us -> 118 us (0.983)
  starting transfers between devices: 32.9 us -> 30.9 us
    ppermute x35, waiting for transfers between devices: 15.5 us -> 10.6 us  [swap(): return lax.ppermute(value, axis, [(i, i ^ bit) for i in range(size)])]
    ppermute x2, waiting for transfers between devices: 3.96 us -> 8.69 us  [outward(): return lax.ppermute(value, 'dp', [(1, 0), (2, 3)])]
    ppermute x35, starting transfers between devices: 28.2 us -> 26.2 us  [swap(): return lax.ppermute(value, axis, [(i, i ^ bit) for i in range(size)])]
  transfers between devices with their start and end apart: 39 -> 39, of which waited for: 16 -> 11; matrix products, arithmetic and copies ran while one was open for 0% -> 0% of each run, Pallas kernels for 52% -> 53%
where the time goes in v6:
time: 118 us
  Pallas kernels  64.1 us (54%)
  starting transfers between devices  30.9 us (26%)
  waiting for transfers between devices  19.3 us (16%)
  other arithmetic  1.18 us (1%)
    pallas_call x6, Pallas kernels, group(): pl.pallas_call(functools.partial(group_kernel, first, last, own, depth, b...  56.4 us
    ppermute x35, starting transfers between devices, swap(): return lax.ppermute(value, axis, [(i, i ^ bit) for i in range(size)])  26.2 us
    ppermute x35, waiting for transfers between devices, swap(): return lax.ppermute(value, axis, [(i, i ^ bit) for i in range(size)])  10.6 us
    ppermute x2, waiting for transfers between devices, outward(): return lax.ppermute(value, 'dp', [(1, 0), (2, 3)])  8.69 us
    pallas_call x1, Pallas kernels, hold(): pl.pallas_call(hold_kernel, in_specs=[pl.BlockSpec(memory_space=pl.ANY)]...  3.78 us
    ppermute x2, starting transfers between devices, outward(): return lax.ppermute(value, 'dp', [(1, 0), (2, 3)])  2.56 us
  transfers between devices with their start and end apart: 39, of which 11 were waited for; matrix products, arithmetic and copies ran while one was open for 0% of the time, Pallas kernels for 53%

profile of v6, /device:TPU:0, one launch (start us, length us, event | category | flops | bytes accessed | tf_op | source)
XLA Modules:
  0.0 117.6 jit_solution(12329745350614708553)
XLA Ops:
  0.6 2.0 %shard_map.102.refs_0_ = bf16[128,2176]{1,0:T(8,128)(2,1)} custom-call(bf16[128,1024]{1,0:T(8,128)(2,1)} %tok_ref.1, bf16[128,1024]{1,0:T(8,128)(2,1)} %dy_ref.1, s32[10,128]{1,0:T(8,128)} %bitcast.13, bf16[10,128]{1,0:T(8,128)(2,1)} %bitcast.14), custom_call_target="tpu_custom_call" | custom-call | flops 10000000 | bytes 2000000 | tf_op jit(solution)/shard_map/pallas_call | solution.py:155
  3.1 2.5 %collective-permute-start.1 = (bf16[128,2176]{1,0:T(8,128)(2,1)}, bf16[128,2176]{1,0:T(8,128)(2,1)S(1)}, u32[]{:S(2)}, u32[]{:S(2)}) collective-permute-start(bf16[128,2176]{1,0:T(8,128)(2,1)} %shard_map.102.refs_0_), channel_id=1, source_target_pairs={{0,2},{1,3},{2,0},{3,1},{4,6},{5,7},{6,4},{7,5},{8,10},{9,11},{10,... | collective-permute-start | bytes 1671176 | tf_op jit(solution)/shard_map/ppermute | solution.py:408
  5.6 1.5 %collective-permute-start.2 = (bf16[128,2176]{1,0:T(8,128)(2,1)}, bf16[128,2176]{1,0:T(8,128)(2,1)S(1)}, u32[]{:S(2)}, u32[]{:S(2)}) collective-permute-start(bf16[128,2176]{1,0:T(8,128)(2,1)} %shard_map.102.refs_0_), channel_id=1, source_target_pairs={{0,4},{1,5},{2,6},{3,7},{4,0},{5,1},{6,2},{7,3},{8,12},{9,13},{10,... | collective-permute-start | bytes 1671176 | tf_op jit(solution)/shard_map/ppermute | solution.py:408
  7.1 1.6 %collective-permute-start.3 = (bf16[128,2176]{1,0:T(8,128)(2,1)}, bf16[128,2176]{1,0:T(8,128)(2,1)S(1)}, u32[]{:S(2)}, u32[]{:S(2)}) collective-permute-start(bf16[128,2176]{1,0:T(8,128)(2,1)} %shard_map.102.refs_0_), channel_id=1, source_target_pairs={{0,8},{8,0},{16,24},{24,16},{1,9},{9,1},{17,25},{25,17},{2,10},{10... | collective-permute-start | bytes 1671176 | tf_op jit(solution)/shard_map/ppermute | solution.py:408
  8.7 1.5 %collective-permute-start.4 = (bf16[128,2176]{1,0:T(8,128)(2,1)}, bf16[128,2176]{1,0:T(8,128)(2,1)}, u32[]{:S(2)}, u32[]{:S(2)}) collective-permute-start(bf16[128,2176]{1,0:T(8,128)(2,1)} %shard_map.102.refs_0_), channel_id=1, source_target_pairs={{8,16},{16,8},{9,17},{17,9},{10,18},{18,10},{11,19},{19,11},{12,20... | collective-permute-start | bytes 1671176 | tf_op jit(solution)/shard_map/ppermute | solution.py:424
  10.1 3.8 %shard_map.103 = (bf16[3,1024,512]{2,1,0:T(8,128)(2,1)S(1)}, bf16[3,1024,512]{2,1,0:T(8,128)(2,1)S(1)}, bf16[3,1024,512]{2,1,0:T(8,128)(2,1)S(1)}) custom-call(bf16[3,1024,512]{2,1,0:T(8,128)(2,1)} %gate_hbm, bf16[3,1024,512]{2,1,0:T(8,128)(2,1)} %up_hbm, bf16[3,512,1024]{2,1,0:T(8,128)(2,1)} %down_hbm), custom_call_target="tpu_custom_call" | custom-call | bytes 2000000 | tf_op jit(solution)/shard_map/pallas_call | solution.py:363
  13.9 6.4 %shard_map.104 = (f32[3,256,512]{2,1,0:T(8,128)S(1)}, f32[3,256,512]{2,1,0:T(8,128)S(1)}, f32[3,128,1024]{2,1,0:T(8,128)S(1)}, bf16[1,128,1024]{2,1,0:T(8,128)(2,1)S(1)}, bf16[1,128,1024]{2,1,0:T(8,128)(2,1)S(1)}) custom-call(bf16[128,2176]{1,0:T(8,128)(2,1)S(1)} %copy-done.2, bf16[128,2176]{1,0:T(8,128)(2,1)S(1)} %collective-permute-done.refs_1_, ...), custom_call_target="tpu_custom_call" | custom-call | flops 50331648 | bytes 557056 | tf_op jit(solution)/shard_map/pallas_call | solution.py:325
  20.5 1.2 %collective-permute-done.3.refs_4_ = bf16[128,2176]{1,0:T(8,128)(2,1)S(1)} collective-permute-done((bf16[128,2176]{1,0:T(8,128)(2,1)}, bf16[128,2176]{1,0:T(8,128)(2,1)S(1)}, u32[]{:S(2)}, u32[]{:S(2)}) %collective-permute-start.3) | collective-permute-done | bytes 557088 | tf_op jit(solution)/shard_map/ppermute | solution.py:408
  22.3 1.3 %collective-permute-start.8 = (bf16[128,2176]{1,0:T(8,128)(2,1)}, bf16[128,2176]{1,0:T(8,128)(2,1)S(1)}, u32[]{:S(2)}, u32[]{:S(2)}) collective-permute-start(bf16[128,2176]{1,0:T(8,128)(2,1)} %collective-permute-done.4.inner_ref), channel_id=1, source_target_pairs={{8,0},{16,24},{9,1},{17,25},{10,2},{18,26},{11,3},{19,27},{12,4},{... | collective-permute-start | bytes 1671176 | tf_op jit(solution)/shard_map/ppermute | solution.py:428
  25.3 11.8 %shard_map.105 = (f32[3,256,512]{2,1,0:T(8,128)S(1)}, f32[3,256,512]{2,1,0:T(8,128)S(1)}, f32[3,128,1024]{2,1,0:T(8,128)S(1)}, bf16[2,128,1024]{2,1,0:T(8,128)(2,1)S(1)}, bf16[2,128,1024]{2,1,0:T(8,128)(2,1)S(1)}) custom-call(bf16[128,2176]{1,0:T(8,128)(2,1)S(1)} %collective-permute-done.1.refs_0_, ...), custom_call_target="tpu_custom_call", output_to_operand_aliasing={{0}: (9, {}), {1}: (10, {}), {2}: (11, {})} | custom-call | flops 150994944 | bytes 557056 | tf_op jit(solution)/shard_map/pallas_call | solution.py:325
  37.2 4.6 %collective-permute-done.8.outer_ref = bf16[128,2176]{1,0:T(8,128)(2,1)S(1)} collective-permute-done((bf16[128,2176]{1,0:T(8,128)(2,1)}, bf16[128,2176]{1,0:T(8,128)(2,1)S(1)}, u32[]{:S(2)}, u32[]{:S(2)}) %collective-permute-start.8) | collective-permute-done | bytes 557088 | tf_op jit(solution)/shard_map/ppermute | solution.py:428
  41.8 0.9 shard_map.106.refs_4_
  44.3 1.9 %collective-permute-done.18 = bf16[2,128,1024]{2,1,0:T(8,128)(2,1)S(1)} collective-permute-done((bf16[2,128,1024]{2,1,0:T(8,128)(2,1)S(1)}, bf16[2,128,1024]{2,1,0:T(8,128)(2,1)S(1)}, u32[]{:S(2)}, u32[]{:S(2)}) %collective-permute-start.18) | collective-permute-done | bytes 524320 | tf_op jit(solution)/shard_map/ppermute | solution.py:408
  46.7 1.3 %collective-permute-start.14 = (bf16[128,2176]{1,0:T(8,128)(2,1)S(1)}, bf16[128,2176]{1,0:T(8,128)(2,1)S(1)}, u32[]{:S(2)}, u32[]{:S(2)}) collective-permute-start(bf16[128,2176]{1,0:T(8,128)(2,1)S(1)} %collective-permute-done.5.inner_ref), channel_id=1, source_target_pairs={{8,0},{16,24},{9,1},{17,25},{10,2},{18,26},{11,3},{19,27},{12,4},{... | collective-permute-start | bytes 1671176 | tf_op jit(solution)/shard_map/ppermute | solution.py:428
  48.9 1.5 %collective-permute-start.20 = (bf16[128,1024]{1,0:T(8,128)(2,1)S(1)}, bf16[128,1024]{1,0:T(8,128)(2,1)S(1)}, u32[]{:S(2)}, u32[]{:S(2)}) collective-permute-start(bf16[128,1024]{1,0:T(8,128)(2,1)S(1)} %get-tuple-element.222), channel_id=1, source_target_pairs={{0,4},{1,5},{2,6},{3,7},{4,0},{5,1},{6,2},{7,3},{8,12},{9,13},{10,... | collective-permute-start | bytes 786440 | tf_op jit(solution)/shard_map/ppermute | solution.py:408
  50.4 11.4 %shard_map.107 = (f32[3,256,512]{2,1,0:T(8,128)S(1)}, f32[3,256,512]{2,1,0:T(8,128)S(1)}, f32[3,128,1024]{2,1,0:T(8,128)S(1)}, bf16[1,128,1024]{2,1,0:T(8,128)(2,1)S(1)}, bf16[1,128,1024]{2,1,0:T(8,128)(2,1)S(1)}) custom-call(bf16[128,2176]{1,0:T(8,128)(2,1)S(1)} %collective-permute-done.6.refs_0_, ...), custom_call_target="tpu_custom_call", output_to_operand_aliasing={{0}: (9, {}), {1}: (10, {}), {2}: (11, {})} | custom-call | flops 150994944 | bytes 557056 | tf_op jit(solution)/shard_map/pallas_call | solution.py:325
  61.8 4.1 %collective-permute-done.14.outer_ref = bf16[128,2176]{1,0:T(8,128)(2,1)S(1)} collective-permute-done((bf16[128,2176]{1,0:T(8,128)(2,1)S(1)}, bf16[128,2176]{1,0:T(8,128)(2,1)S(1)}, u32[]{:S(2)}, u32[]{:S(2)}) %collective-permute-start.14) | collective-permute-done | bytes 557088 | tf_op jit(solution)/shard_map/ppermute | solution.py:428
  65.9 1.1 shard_map.108.refs_4_
  68.1 1.4 %collective-permute-start.21 = (bf16[128,2176]{1,0:T(8,128)(2,1)}, bf16[128,2176]{1,0:T(8,128)(2,1)S(1)}, u32[]{:S(2)}, u32[]{:S(2)}) collective-permute-start(bf16[128,2176]{1,0:T(8,128)(2,1)} %shard_map.108.refs_4_), channel_id=1, source_target_pairs={{0,2},{1,3},{2,0},{3,1},{4,6},{5,7},{6,4},{7,5},{8,10},{9,11},{10,... | collective-permute-start | bytes 1671176 | tf_op jit(solution)/shard_map/ppermute | solution.py:408
  70.0 4.9 %collective-permute-start.32 = (bf16[128,2176]{1,0:T(8,128)(2,1)S(1)}, bf16[128,2176]{1,0:T(8,128)(2,1)S(1)}, u32[]{:S(2)}, u32[]{:S(2)}) collective-permute-start(bf16[128,2176]{1,0:T(8,128)(2,1)S(1)} %collective-permute-done.2.refs_2_), channel_id=1, source_target_pairs={{0,8},{8,0},{16,24},{24,16},{1,9},{9,1},{17,25},{25,17},{2,10},{10... | collective-permute-start | bytes 1671176 | tf_op jit(solution)/shard_map/ppermute | solution.py:408
  75.0 1.0 copy-done.1
  76.1 8.7 %shard_map.109 = (f32[3,256,512]{2,1,0:T(8,128)S(1)}, f32[3,256,512]{2,1,0:T(8,128)S(1)}, f32[3,128,1024]{2,1,0:T(8,128)S(1)}) custom-call(bf16[128,2176]{1,0:T(8,128)(2,1)S(1)} %collective-permute-done.12.refs_0_, bf16[128,2176]{1,0:T(8,128)(2,1)S(1)} %collective-permute-done.23.refs_1_, ...), custom_call_target="tpu_custom_call", output_to_operand_aliasing={{0}: (9, {}), {1}: (10, {}), {2}: (11, {})} | custom-call | flops 150994944 | bytes 557056 | tf_op jit(solution)/shard_map/pallas_call | solution.py:325
  85.4 1.8 %collective-permute-done.32.refs_4_ = bf16[128,2176]{1,0:T(8,128)(2,1)S(1)} collective-permute-done((bf16[128,2176]{1,0:T(8,128)(2,1)S(1)}, bf16[128,2176]{1,0:T(8,128)(2,1)S(1)}, u32[]{:S(2)}, u32[]{:S(2)}) %collective-permute-start.32) | collective-permute-done | bytes 557088 | tf_op jit(solution)/shard_map/ppermute | solution.py:408
  87.2 0.9 collective-permute-start.27
  88.1 1.1 collective-permute-start.28
  89.2 1.7 %collective-permute-start.29 = (bf16[128,2176]{1,0:T(8,128)(2,1)S(1)}, bf16[128,2176]{1,0:T(8,128)(2,1)S(1)}, u32[]{:S(2)}, u32[]{:S(2)}) collective-permute-start(bf16[128,2176]{1,0:T(8,128)(2,1)S(1)} %collective-permute-done.6.refs_0_), channel_id=1, source_target_pairs={{0,8},{8,0},{16,24},{24,16},{1,9},{9,1},{17,25},{25,17},{2,10},{10... | collective-permute-start | bytes 1671176 | tf_op jit(solution)/shard_map/ppermute | solution.py:408
  90.9 8.7 %shard_map.110 = (f32[3,256,512]{2,1,0:T(8,128)S(1)}, f32[3,256,512]{2,1,0:T(8,128)S(1)}, f32[3,128,1024]{2,1,0:T(8,128)S(1)}) custom-call(bf16[128,2176]{1,0:T(8,128)(2,1)S(1)} %collective-permute-done.21.refs_0_, bf16[128,2176]{1,0:T(8,128)(2,1)S(1)} %collective-permute-done.30.refs_1_, ...), custom_call_target="tpu_custom_call", output_to_operand_aliasing={{0}: (9, {}), {1}: (10, {}), {2}: (11, {})} | custom-call | flops 150994944 | bytes 557056 | tf_op jit(solution)/shard_map/pallas_call | solution.py:325
  99.6 2.6 %collective-permute-done.27.refs_4_ = bf16[128,2176]{1,0:T(8,128)(2,1)S(1)} collective-permute-done((bf16[128,2176]{1,0:T(8,128)(2,1)S(1)}, bf16[128,2176]{1,0:T(8,128)(2,1)S(1)}, u32[]{:S(2)}, u32[]{:S(2)}) %collective-permute-start.27) | collective-permute-done | bytes 557088 | tf_op jit(solution)/shard_map/ppermute | solution.py:408
  102.9 0.8 collective-permute-done.29.refs_0_
  104.2 1.5 %collective-permute-start.34 = (bf16[128,1024]{1,0:T(8,128)(2,1)S(1)}, bf16[128,1024]{1,0:T(8,128)(2,1)S(1)}, u32[]{:S(2)}, u32[]{:S(2)}) collective-permute-start(bf16[128,1024]{1,0:T(8,128)(2,1)S(1)} %bitcast.12), channel_id=1, source_target_pairs={{0,6},{1,7},{2,4},{3,5},{4,2},{5,3},{6,0},{7,1},{8,14},{9,15},{10,... | collective-permute-start | bytes 786440 | tf_op jit(solution)/shard_map/ppermute | solution.py:408
  107.2 9.4 %shard_map.111 = (bf16[3,256,512]{2,1,0:T(8,128)(2,1)}, bf16[3,256,512]{2,1,0:T(8,128)(2,1)}, bf16[3,128,1024]{2,1,0:T(8,128)(2,1)}) custom-call(bf16[128,2176]{1,0:T(8,128)(2,1)S(1)} %collective-permute-done.29.refs_0_, bf16[128,2176]{1,0:T(8,128)(2,1)S(1)} %collective-permute-done.36.refs_1_, bf16[128,2176]{1,0:T(8,128)(2,1)S(1)} %collective-permute-done.28.refs_2_, ...), custom_call_target="tpu_custom_call" | custom-call | flops 150994944 | bytes 557056 | tf_op jit(solution)/shard_map/pallas_call | solution.py:325
  116.6 0.9 fusion.3
  (66 shorter events, 10.8 us)
Async XLA Ops:
  2.6 11.3 %collective-permute-start = (bf16[128,2176]{1,0:T(8,128)(2,1)}, bf16[128,2176]{1,0:T(8,128)(2,1)S(1)}, u32[]{:S(2)}, u32[]{:S(2)}) collective-permute-start(bf16[128,2176]{1,0:T(8,128)(2,1)} %shard_map.102.refs_0_), channel_id=1, source_target_pairs={{0,1},{1,0},{2,3},{3,2},{4,5},{5,4},{6,7},{7,6},{8,9},{9,8},{10,11... | collective-permute-start | bytes 1671176 | tf_op jit(solution)/shard_map/ppermute | solution.py:408
  3.1 17.3 %collective-permute-start.1 = (bf16[128,2176]{1,0:T(8,128)(2,1)}, bf16[128,2176]{1,0:T(8,128)(2,1)S(1)}, u32[]{:S(2)}, u32[]{:S(2)}) collective-permute-start(bf16[128,2176]{1,0:T(8,128)(2,1)} %shard_map.102.refs_0_), channel_id=1, source_target_pairs={{0,2},{1,3},{2,0},{3,1},{4,6},{5,7},{6,4},{7,5},{8,10},{9,11},{10,... | collective-permute-start | bytes 1671176 | tf_op jit(solution)/shard_map/ppermute | solution.py:408
  5.6 15.0 %collective-permute-start.2 = (bf16[128,2176]{1,0:T(8,128)(2,1)}, bf16[128,2176]{1,0:T(8,128)(2,1)S(1)}, u32[]{:S(2)}, u32[]{:S(2)}) collective-permute-start(bf16[128,2176]{1,0:T(8,128)(2,1)} %shard_map.102.refs_0_), channel_id=1, source_target_pairs={{0,4},{1,5},{2,6},{3,7},{4,0},{5,1},{6,2},{7,3},{8,12},{9,13},{10,... | collective-permute-start | bytes 1671176 | tf_op jit(solution)/shard_map/ppermute | solution.py:408
  7.1 14.7 %collective-permute-start.3 = (bf16[128,2176]{1,0:T(8,128)(2,1)}, bf16[128,2176]{1,0:T(8,128)(2,1)S(1)}, u32[]{:S(2)}, u32[]{:S(2)}) collective-permute-start(bf16[128,2176]{1,0:T(8,128)(2,1)} %shard_map.102.refs_0_), channel_id=1, source_target_pairs={{0,8},{8,0},{16,24},{24,16},{1,9},{9,1},{17,25},{25,17},{2,10},{10... | collective-permute-start | bytes 1671176 | tf_op jit(solution)/shard_map/ppermute | solution.py:408
  8.7 13.1 %collective-permute-start.4 = (bf16[128,2176]{1,0:T(8,128)(2,1)}, bf16[128,2176]{1,0:T(8,128)(2,1)}, u32[]{:S(2)}, u32[]{:S(2)}) collective-permute-start(bf16[128,2176]{1,0:T(8,128)(2,1)} %shard_map.102.refs_0_), channel_id=1, source_target_pairs={{8,16},{16,8},{9,17},{17,9},{10,18},{18,10},{11,19},{19,11},{12,20... | collective-permute-start | bytes 1671176 | tf_op jit(solution)/shard_map/ppermute | solution.py:424
  21.8 3.1 %collective-permute-start.11 = (bf16[128,2176]{1,0:T(8,128)(2,1)S(1)}, bf16[128,2176]{1,0:T(8,128)(2,1)S(1)}, u32[]{:S(2)}, u32[]{:S(2)}) collective-permute-start(bf16[128,2176]{1,0:T(8,128)(2,1)S(1)} %collective-permute-done.3.refs_4_), channel_id=1, source_target_pairs={{0,1},{1,0},{2,3},{3,2},{4,5},{5,4},{6,7},{7,6},{8,9},{9,8},{10,11... | collective-permute-start | bytes 1671176 | tf_op jit(solution)/shard_map/ppermute | solution.py:408
  22.3 19.5 %collective-permute-start.8 = (bf16[128,2176]{1,0:T(8,128)(2,1)}, bf16[128,2176]{1,0:T(8,128)(2,1)S(1)}, u32[]{:S(2)}, u32[]{:S(2)}) collective-permute-start(bf16[128,2176]{1,0:T(8,128)(2,1)} %collective-permute-done.4.inner_ref), channel_id=1, source_target_pairs={{8,0},{16,24},{9,1},{17,25},{10,2},{18,26},{11,3},{19,27},{12,4},{... | collective-permute-start | bytes 1671176 | tf_op jit(solution)/shard_map/ppermute | solution.py:428
  23.6 19.1 %collective-permute-start.5 = (bf16[128,2176]{1,0:T(8,128)(2,1)S(1)}, bf16[128,2176]{1,0:T(8,128)(2,1)S(1)}, u32[]{:S(2)}, u32[]{:S(2)}) collective-permute-start(bf16[128,2176]{1,0:T(8,128)(2,1)S(1)} %collective-permute-done.3.refs_4_), channel_id=1, source_target_pairs={{8,16},{16,8},{9,17},{17,9},{10,18},{18,10},{11,19},{19,11},{12,20... | collective-permute-start | bytes 1671176 | tf_op jit(solution)/shard_map/ppermute | solution.py:424
  24.3 18.4 %collective-permute-start.6 = (bf16[128,2176]{1,0:T(8,128)(2,1)S(1)}, bf16[128,2176]{1,0:T(8,128)(2,1)S(1)}, u32[]{:S(2)}, u32[]{:S(2)}) collective-permute-start(bf16[128,2176]{1,0:T(8,128)(2,1)S(1)} %collective-permute-done.1.refs_0_), channel_id=1, source_target_pairs={{0,4},{1,5},{2,6},{3,7},{4,0},{5,1},{6,2},{7,3},{8,12},{9,13},{10,... | collective-permute-start | bytes 1671176 | tf_op jit(solution)/shard_map/ppermute | solution.py:408
  24.9 17.8 %collective-permute-start.7 = (bf16[128,2176]{1,0:T(8,128)(2,1)S(1)}, bf16[128,2176]{1,0:T(8,128)(2,1)S(1)}, u32[]{:S(2)}, u32[]{:S(2)}) collective-permute-start(bf16[128,2176]{1,0:T(8,128)(2,1)S(1)} %collective-permute-done.3.refs_4_), channel_id=1, source_target_pairs={{0,2},{1,3},{2,0},{3,1},{4,6},{5,7},{6,4},{7,5},{8,10},{9,11},{10,... | collective-permute-start | bytes 1671176 | tf_op jit(solution)/shard_map/ppermute | solution.py:408
  42.7 4.0 %collective-permute-start.15 = (bf16[128,2176]{1,0:T(8,128)(2,1)S(1)}, bf16[128,2176]{1,0:T(8,128)(2,1)S(1)}, u32[]{:S(2)}, u32[]{:S(2)}) collective-permute-start(bf16[128,2176]{1,0:T(8,128)(2,1)S(1)} %collective-permute-done.6.refs_0_), channel_id=1, source_target_pairs={{0,1},{1,0},{2,3},{3,2},{4,5},{5,4},{6,7},{7,6},{8,9},{9,8},{10,11... | collective-permute-start | bytes 1671176 | tf_op jit(solution)/shard_map/ppermute | solution.py:408
  42.8 3.4 %collective-permute-start.18 = (bf16[2,128,1024]{2,1,0:T(8,128)(2,1)S(1)}, bf16[2,128,1024]{2,1,0:T(8,128)(2,1)S(1)}, u32[]{:S(2)}, u32[]{:S(2)}) collective-permute-start(bf16[2,128,1024]{2,1,0:T(8,128)(2,1)S(1)} %get-tuple-element.153), channel_id=1, source_target_pairs={{0,1},{1,0},{2,3},{3,2},{4,5},{5,4},{6,7},{7,6},{8,9},{9,8},{10,11... | collective-permute-start | bytes 1572872 | tf_op jit(solution)/shard_map/ppermute | solution.py:408
  43.3 4.9 %collective-permute-start.16 = (bf16[128,2176]{1,0:T(8,128)(2,1)S(1)}, bf16[128,2176]{1,0:T(8,128)(2,1)S(1)}, u32[]{:S(2)}, u32[]{:S(2)}) collective-permute-start(bf16[128,2176]{1,0:T(8,128)(2,1)S(1)} %collective-permute-done.7.refs_2_), channel_id=1, source_target_pairs={{0,1},{1,0},{2,3},{3,2},{4,5},{5,4},{6,7},{7,6},{8,9},{9,8},{10,11... | collective-permute-start | bytes 1671176 | tf_op jit(solution)/shard_map/ppermute | solution.py:408
  43.4 4.9 %collective-permute-start.17 = (bf16[128,2176]{1,0:T(8,128)(2,1)}, bf16[128,2176]{1,0:T(8,128)(2,1)S(1)}, u32[]{:S(2)}, u32[]{:S(2)}) collective-permute-start(bf16[128,2176]{1,0:T(8,128)(2,1)} %shard_map.106.refs_4_), channel_id=1, source_target_pairs={{0,1},{1,0},{2,3},{3,2},{4,5},{5,4},{6,7},{7,6},{8,9},{9,8},{10,11... | collective-permute-start | bytes 1671176 | tf_op jit(solution)/shard_map/ppermute | solution.py:408
  43.8 23.2 %collective-permute-start.12 = (bf16[128,2176]{1,0:T(8,128)(2,1)}, bf16[128,2176]{1,0:T(8,128)(2,1)S(1)}, u32[]{:S(2)}, u32[]{:S(2)}) collective-permute-start(bf16[128,2176]{1,0:T(8,128)(2,1)} %shard_map.106.refs_4_), channel_id=1, source_target_pairs={{0,2},{1,3},{2,0},{3,1},{4,6},{5,7},{6,4},{7,5},{8,10},{9,11},{10,... | collective-permute-start | bytes 1671176 | tf_op jit(solution)/shard_map/ppermute | solution.py:408
  46.2 20.8 %collective-permute-start.13 = (bf16[128,2176]{1,0:T(8,128)(2,1)}, bf16[128,2176]{1,0:T(8,128)(2,1)S(1)}, u32[]{:S(2)}, u32[]{:S(2)}) collective-permute-start(bf16[128,2176]{1,0:T(8,128)(2,1)} %shard_map.106.refs_4_), channel_id=1, source_target_pairs={{0,4},{1,5},{2,6},{3,7},{4,0},{5,1},{6,2},{7,3},{8,12},{9,13},{10,... | collective-permute-start | bytes 1671176 | tf_op jit(solution)/shard_map/ppermute | solution.py:408
  46.7 19.2 %collective-permute-start.14 = (bf16[128,2176]{1,0:T(8,128)(2,1)S(1)}, bf16[128,2176]{1,0:T(8,128)(2,1)S(1)}, u32[]{:S(2)}, u32[]{:S(2)}) collective-permute-start(bf16[128,2176]{1,0:T(8,128)(2,1)S(1)} %collective-permute-done.5.inner_ref), channel_id=1, source_target_pairs={{8,0},{16,24},{9,1},{17,25},{10,2},{18,26},{11,3},{19,27},{12,4},{... | collective-permute-start | bytes 1671176 | tf_op jit(solution)/shard_map/ppermute | solution.py:428
  48.3 18.7 %collective-permute-start.19 = (bf16[128,1024]{1,0:T(8,128)(2,1)S(1)}, bf16[128,1024]{1,0:T(8,128)(2,1)S(1)}, u32[]{:S(2)}, u32[]{:S(2)}) collective-permute-start(bf16[128,1024]{1,0:T(8,128)(2,1)S(1)} %get-tuple-element.223), channel_id=1, source_target_pairs={{0,2},{1,3},{2,0},{3,1},{4,6},{5,7},{6,4},{7,5},{8,10},{9,11},{10,... | collective-permute-start | bytes 786440 | tf_op jit(solution)/shard_map/ppermute | solution.py:408
  48.9 18.1 %collective-permute-start.20 = (bf16[128,1024]{1,0:T(8,128)(2,1)S(1)}, bf16[128,1024]{1,0:T(8,128)(2,1)S(1)}, u32[]{:S(2)}, u32[]{:S(2)}) collective-permute-start(bf16[128,1024]{1,0:T(8,128)(2,1)S(1)} %get-tuple-element.222), channel_id=1, source_target_pairs={{0,4},{1,5},{2,6},{3,7},{4,0},{5,1},{6,2},{7,3},{8,12},{9,13},{10,... | collective-permute-start | bytes 786440 | tf_op jit(solution)/shard_map/ppermute | solution.py:408
  67.6 7.3 %collective-permute-start.24 = (bf16[128,2176]{1,0:T(8,128)(2,1)S(1)}, bf16[128,2176]{1,0:T(8,128)(2,1)S(1)}, u32[]{:S(2)}, u32[]{:S(2)}) collective-permute-start(bf16[128,2176]{1,0:T(8,128)(2,1)S(1)} %collective-permute-done.13.refs_2_), channel_id=1, source_target_pairs={{0,1},{1,0},{2,3},{3,2},{4,5},{5,4},{6,7},{7,6},{8,9},{9,8},{10,11... | collective-permute-start | bytes 1671176 | tf_op jit(solution)/shard_map/ppermute | solution.py:408
  67.7 7.3 %collective-permute-start.25 = (bf16[128,2176]{1,0:T(8,128)(2,1)}, bf16[128,2176]{1,0:T(8,128)(2,1)S(1)}, u32[]{:S(2)}, u32[]{:S(2)}) collective-permute-start(bf16[128,2176]{1,0:T(8,128)(2,1)} %shard_map.108.refs_4_), channel_id=1, source_target_pairs={{0,1},{1,0},{2,3},{3,2},{4,5},{5,4},{6,7},{7,6},{8,9},{9,8},{10,11... | collective-permute-start | bytes 1671176 | tf_op jit(solution)/shard_map/ppermute | solution.py:408
  68.1 16.7 %collective-permute-start.21 = (bf16[128,2176]{1,0:T(8,128)(2,1)}, bf16[128,2176]{1,0:T(8,128)(2,1)S(1)}, u32[]{:S(2)}, u32[]{:S(2)}) collective-permute-start(bf16[128,2176]{1,0:T(8,128)(2,1)} %shard_map.108.refs_4_), channel_id=1, source_target_pairs={{0,2},{1,3},{2,0},{3,1},{4,6},{5,7},{6,4},{7,5},{8,10},{9,11},{10,... | collective-permute-start | bytes 1671176 | tf_op jit(solution)/shard_map/ppermute | solution.py:408
  69.5 15.2 %collective-permute-start.22 = (bf16[128,2176]{1,0:T(8,128)(2,1)}, bf16[128,2176]{1,0:T(8,128)(2,1)S(1)}, u32[]{:S(2)}, u32[]{:S(2)}) collective-permute-start(bf16[128,2176]{1,0:T(8,128)(2,1)} %shard_map.108.refs_4_), channel_id=1, source_target_pairs={{0,4},{1,5},{2,6},{3,7},{4,0},{5,1},{6,2},{7,3},{8,12},{9,13},{10,... | collective-permute-start | bytes 1671176 | tf_op jit(solution)/shard_map/ppermute | solution.py:408
  70.0 17.1 %collective-permute-start.32 = (bf16[128,2176]{1,0:T(8,128)(2,1)S(1)}, bf16[128,2176]{1,0:T(8,128)(2,1)S(1)}, u32[]{:S(2)}, u32[]{:S(2)}) collective-permute-start(bf16[128,2176]{1,0:T(8,128)(2,1)S(1)} %collective-permute-done.2.refs_2_), channel_id=1, source_target_pairs={{0,8},{8,0},{16,24},{24,16},{1,9},{9,1},{17,25},{25,17},{2,10},{10... | collective-permute-start | bytes 1671176 | tf_op jit(solution)/shard_map/ppermute | solution.py:408
  84.8 4.4 %collective-permute-start.30 = (bf16[128,2176]{1,0:T(8,128)(2,1)S(1)}, bf16[128,2176]{1,0:T(8,128)(2,1)S(1)}, u32[]{:S(2)}, u32[]{:S(2)}) collective-permute-start(bf16[128,2176]{1,0:T(8,128)(2,1)S(1)} %collective-permute-done.21.refs_0_), channel_id=1, source_target_pairs={{0,1},{1,0},{2,3},{3,2},{4,5},{5,4},{6,7},{7,6},{8,9},{9,8},{10,11... | collective-permute-start | bytes 1671176 | tf_op jit(solution)/shard_map/ppermute | solution.py:408
  84.9 6.1 %collective-permute-start.31 = (bf16[128,2176]{1,0:T(8,128)(2,1)S(1)}, bf16[128,2176]{1,0:T(8,128)(2,1)S(1)}, u32[]{:S(2)}, u32[]{:S(2)}) collective-permute-start(bf16[128,2176]{1,0:T(8,128)(2,1)S(1)} %collective-permute-done.22.refs_2_), channel_id=1, source_target_pairs={{0,1},{1,0},{2,3},{3,2},{4,5},{5,4},{6,7},{7,6},{8,9},{9,8},{10,11... | collective-permute-start | bytes 1671176 | tf_op jit(solution)/shard_map/ppermute | solution.py:408
  87.2 3.8 %collective-permute-start.33 = (bf16[128,2176]{1,0:T(8,128)(2,1)S(1)}, bf16[128,2176]{1,0:T(8,128)(2,1)S(1)}, u32[]{:S(2)}, u32[]{:S(2)}) collective-permute-start(bf16[128,2176]{1,0:T(8,128)(2,1)S(1)} %collective-permute-done.32.refs_4_), channel_id=1, source_target_pairs={{0,1},{1,0},{2,3},{3,2},{4,5},{5,4},{6,7},{7,6},{8,9},{9,8},{10,11... | collective-permute-start | bytes 1671176 | tf_op jit(solution)/shard_map/ppermute | solution.py:408
  87.2 15.0 %collective-permute-start.27 = (bf16[128,2176]{1,0:T(8,128)(2,1)S(1)}, bf16[128,2176]{1,0:T(8,128)(2,1)S(1)}, u32[]{:S(2)}, u32[]{:S(2)}) collective-permute-start(bf16[128,2176]{1,0:T(8,128)(2,1)S(1)} %collective-permute-done.22.refs_2_), channel_id=1, source_target_pairs={{0,2},{1,3},{2,0},{3,1},{4,6},{5,7},{6,4},{7,5},{8,10},{9,11},{10,... | collective-permute-start | bytes 1671176 | tf_op jit(solution)/shard_map/ppermute | solution.py:408
  88.1 14.8 %collective-permute-start.28 = (bf16[128,2176]{1,0:T(8,128)(2,1)S(1)}, bf16[128,2176]{1,0:T(8,128)(2,1)S(1)}, u32[]{:S(2)}, u32[]{:S(2)}) collective-permute-start(bf16[128,2176]{1,0:T(8,128)(2,1)S(1)} %collective-permute-done.12.refs_0_), channel_id=1, source_target_pairs={{0,4},{1,5},{2,6},{3,7},{4,0},{5,1},{6,2},{7,3},{8,12},{9,13},{10,... | collective-permute-start | bytes 1671176 | tf_op jit(solution)/shard_map/ppermute | solution.py:408
  89.2 14.5 %collective-permute-start.29 = (bf16[128,2176]{1,0:T(8,128)(2,1)S(1)}, bf16[128,2176]{1,0:T(8,128)(2,1)S(1)}, u32[]{:S(2)}, u32[]{:S(2)}) collective-permute-start(bf16[128,2176]{1,0:T(8,128)(2,1)S(1)} %collective-permute-done.6.refs_0_), channel_id=1, source_target_pairs={{0,8},{8,0},{16,24},{24,16},{1,9},{9,1},{17,25},{25,17},{2,10},{10... | collective-permute-start | bytes 1671176 | tf_op jit(solution)/shard_map/ppermute | solution.py:408
  104.2 12.4 %collective-permute-start.34 = (bf16[128,1024]{1,0:T(8,128)(2,1)S(1)}, bf16[128,1024]{1,0:T(8,128)(2,1)S(1)}, u32[]{:S(2)}, u32[]{:S(2)}) collective-permute-start(bf16[128,1024]{1,0:T(8,128)(2,1)S(1)} %bitcast.12), channel_id=1, source_target_pairs={{0,6},{1,7},{2,4},{3,5},{4,2},{5,3},{6,0},{7,1},{8,14},{9,15},{10,... | collective-permute-start | bytes 786440 | tf_op jit(solution)/shard_map/ppermute | solution.py:408
  105.7 11.0 %collective-permute-start.35 = (bf16[128,1024]{1,0:T(8,128)(2,1)S(1)}, bf16[128,1024]{1,0:T(8,128)(2,1)S(1)}, u32[]{:S(2)}, u32[]{:S(2)}) collective-permute-start(bf16[128,1024]{1,0:T(8,128)(2,1)S(1)} %bitcast.11), channel_id=1, source_target_pairs={{0,1},{1,0},{2,3},{3,2},{4,5},{5,4},{6,7},{7,6},{8,9},{9,8},{10,11... | collective-permute-start | bytes 786440 | tf_op jit(solution)/shard_map/ppermute | solution.py:408
  (10 other events, 39.1 us)

commit v7 on v6

--- a/solution.py
+++ b/solution.py
@@ -224,14 +224,17 @@
     def expert(e, _):
         rows_x = x_rows[e]
         d_out = d_rows[e]
-        gate_pre = mul(rows_x, gate_ref[e])
-        up_pre = mul(rows_x, up_ref[e])
-        d_hidden = mul(d_out, across_ref[e])
-        sig = 0.5 * jnp.tanh(0.5 * gate_pre) + 0.5
-        act = gate_pre * sig
-        hid[...] = (act * up_pre).astype(jnp.bfloat16)
-        both[:, :units] = (d_hidden * up_pre * (sig + act * (1.0 - sig))).astype(jnp.bfloat16)
-        both[:, units:] = (d_hidden * act).astype(jnp.bfloat16)
+        step = min(units, 256)
+        for at in range(0, units, step):
+            cut = slice(at, at + step)
+            gate_pre = mul(rows_x, gate_ref[e, :, cut])
+            up_pre = mul(rows_x, up_ref[e, :, cut])
+            d_hidden = mul(d_out, across_ref[e, :, cut])
+            sig = 0.5 * jnp.tanh(0.5 * gate_pre) + 0.5
+            act = gate_pre * sig
+            hid[:, cut] = (act * up_pre).astype(jnp.bfloat16)
+            both[:, cut] = (d_hidden * up_pre * (sig + act * (1.0 - sig))).astype(jnp.bfloat16)
+            both[:, units + at : units + at + step] = (d_hidden * act).astype(jnp.bfloat16)
         x_part = x_rows[e, :, pl.ds(pl.multiple_of(shard * x_cut, LANES), x_cut)]
         h_part = hid[:, pl.ds(pl.multiple_of(shard * h_cut, LANES), h_cut)]
         grad_both = contract_first(x_part, both[...])

time: 118 us -> 118 us (level)
  transfers between devices with their start and end apart: 39 -> 39, of which waited for: 11 -> 11; matrix products, arithmetic and copies ran while one was open for 0% -> 0% of each run, Pallas kernels for 53% -> 52%
where the time goes in v7:
time: 118 us
  Pallas kernels  63.7 us (54%)
  starting transfers between devices  31 us (26%)
  waiting for transfers between devices  19.6 us (17%)
  other arithmetic  1.18 us (1%)
    pallas_call x6, Pallas kernels, group(): pl.pallas_call(functools.partial(group_kernel, first, last, own, depth, b...  55.9 us
    ppermute x35, starting transfers between devices, swap(): return lax.ppermute(value, axis, [(i, i ^ bit) for i in range(size)])  26.3 us
    ppermute x35, waiting for transfers between devices, swap(): return lax.ppermute(value, axis, [(i, i ^ bit) for i in range(size)])  10.9 us
    ppermute x2, waiting for transfers between devices, outward(): return lax.ppermute(value, 'dp', [(1, 0), (2, 3)])  8.71 us
    pallas_call x1, Pallas kernels, hold(): pl.pallas_call(hold_kernel, in_specs=[pl.BlockSpec(memory_space=pl.ANY)]...  3.78 us
    ppermute x2, starting transfers between devices, outward(): return lax.ppermute(value, 'dp', [(1, 0), (2, 3)])  2.56 us
  transfers between devices with their start and end apart: 39, of which 11 were waited for; matrix products, arithmetic and copies ran while one was open for 0% of the time, Pallas kernels for 52%

profile of v7, /device:TPU:0, one launch (start us, length us, event | category | flops | bytes accessed | tf_op | source)
XLA Modules:
  0.0 117.5 jit_solution(18040483327618315701)
XLA Ops:
  0.6 2.0 %shard_map.102.refs_0_ = bf16[128,2176]{1,0:T(8,128)(2,1)} custom-call(bf16[128,1024]{1,0:T(8,128)(2,1)} %tok_ref.1, bf16[128,1024]{1,0:T(8,128)(2,1)} %dy_ref.1, s32[10,128]{1,0:T(8,128)} %bitcast.13, bf16[10,128]{1,0:T(8,128)(2,1)} %bitcast.14), custom_call_target="tpu_custom_call" | custom-call | flops 10000000 | bytes 2000000 | tf_op jit(solution)/shard_map/pallas_call | solution.py:155
  3.1 2.5 %collective-permute-start.1 = (bf16[128,2176]{1,0:T(8,128)(2,1)}, bf16[128,2176]{1,0:T(8,128)(2,1)S(1)}, u32[]{:S(2)}, u32[]{:S(2)}) collective-permute-start(bf16[128,2176]{1,0:T(8,128)(2,1)} %shard_map.102.refs_0_), channel_id=1, source_target_pairs={{0,2},{1,3},{2,0},{3,1},{4,6},{5,7},{6,4},{7,5},{8,10},{9,11},{10,... | collective-permute-start | bytes 1671176 | tf_op jit(solution)/shard_map/ppermute | solution.py:411
  5.6 1.5 %collective-permute-start.2 = (bf16[128,2176]{1,0:T(8,128)(2,1)}, bf16[128,2176]{1,0:T(8,128)(2,1)S(1)}, u32[]{:S(2)}, u32[]{:S(2)}) collective-permute-start(bf16[128,2176]{1,0:T(8,128)(2,1)} %shard_map.102.refs_0_), channel_id=1, source_target_pairs={{0,4},{1,5},{2,6},{3,7},{4,0},{5,1},{6,2},{7,3},{8,12},{9,13},{10,... | collective-permute-start | bytes 1671176 | tf_op jit(solution)/shard_map/ppermute | solution.py:411
  7.1 1.6 %collective-permute-start.3 = (bf16[128,2176]{1,0:T(8,128)(2,1)}, bf16[128,2176]{1,0:T(8,128)(2,1)S(1)}, u32[]{:S(2)}, u32[]{:S(2)}) collective-permute-start(bf16[128,2176]{1,0:T(8,128)(2,1)} %shard_map.102.refs_0_), channel_id=1, source_target_pairs={{0,8},{8,0},{16,24},{24,16},{1,9},{9,1},{17,25},{25,17},{2,10},{10... | collective-permute-start | bytes 1671176 | tf_op jit(solution)/shard_map/ppermute | solution.py:411
  8.7 1.5 %collective-permute-start.4 = (bf16[128,2176]{1,0:T(8,128)(2,1)}, bf16[128,2176]{1,0:T(8,128)(2,1)}, u32[]{:S(2)}, u32[]{:S(2)}) collective-permute-start(bf16[128,2176]{1,0:T(8,128)(2,1)} %shard_map.102.refs_0_), channel_id=1, source_target_pairs={{8,16},{16,8},{9,17},{17,9},{10,18},{18,10},{11,19},{19,11},{12,20... | collective-permute-start | bytes 1671176 | tf_op jit(solution)/shard_map/ppermute | solution.py:427
  10.1 3.8 %shard_map.103 = (bf16[3,1024,512]{2,1,0:T(8,128)(2,1)S(1)}, bf16[3,1024,512]{2,1,0:T(8,128)(2,1)S(1)}, bf16[3,1024,512]{2,1,0:T(8,128)(2,1)S(1)}) custom-call(bf16[3,1024,512]{2,1,0:T(8,128)(2,1)} %gate_hbm, bf16[3,1024,512]{2,1,0:T(8,128)(2,1)} %up_hbm, bf16[3,512,1024]{2,1,0:T(8,128)(2,1)} %down_hbm), custom_call_target="tpu_custom_call" | custom-call | bytes 2000000 | tf_op jit(solution)/shard_map/pallas_call | solution.py:366
  13.9 5.9 %shard_map.104 = (f32[3,256,512]{2,1,0:T(8,128)S(1)}, f32[3,256,512]{2,1,0:T(8,128)S(1)}, f32[3,128,1024]{2,1,0:T(8,128)S(1)}, bf16[1,128,1024]{2,1,0:T(8,128)(2,1)S(1)}, bf16[1,128,1024]{2,1,0:T(8,128)(2,1)S(1)}) custom-call(bf16[128,2176]{1,0:T(8,128)(2,1)S(1)} %copy-done.2, bf16[128,2176]{1,0:T(8,128)(2,1)S(1)} %collective-permute-done.refs_1_, ...), custom_call_target="tpu_custom_call" | custom-call | flops 50331648 | bytes 557056 | tf_op jit(solution)/shard_map/pallas_call | solution.py:328
  20.5 1.2 %collective-permute-done.3.refs_4_ = bf16[128,2176]{1,0:T(8,128)(2,1)S(1)} collective-permute-done((bf16[128,2176]{1,0:T(8,128)(2,1)}, bf16[128,2176]{1,0:T(8,128)(2,1)S(1)}, u32[]{:S(2)}, u32[]{:S(2)}) %collective-permute-start.3) | collective-permute-done | bytes 557088 | tf_op jit(solution)/shard_map/ppermute | solution.py:411
  22.3 1.3 %collective-permute-start.8 = (bf16[128,2176]{1,0:T(8,128)(2,1)}, bf16[128,2176]{1,0:T(8,128)(2,1)S(1)}, u32[]{:S(2)}, u32[]{:S(2)}) collective-permute-start(bf16[128,2176]{1,0:T(8,128)(2,1)} %collective-permute-done.4.inner_ref), channel_id=1, source_target_pairs={{8,0},{16,24},{9,1},{17,25},{10,2},{18,26},{11,3},{19,27},{12,4},{... | collective-permute-start | bytes 1671176 | tf_op jit(solution)/shard_map/ppermute | solution.py:431
  25.3 12.0 %shard_map.105 = (f32[3,256,512]{2,1,0:T(8,128)S(1)}, f32[3,256,512]{2,1,0:T(8,128)S(1)}, f32[3,128,1024]{2,1,0:T(8,128)S(1)}, bf16[2,128,1024]{2,1,0:T(8,128)(2,1)S(1)}, bf16[2,128,1024]{2,1,0:T(8,128)(2,1)S(1)}) custom-call(bf16[128,2176]{1,0:T(8,128)(2,1)S(1)} %collective-permute-done.1.refs_0_, ...), custom_call_target="tpu_custom_call", output_to_operand_aliasing={{0}: (9, {}), {1}: (10, {}), {2}: (11, {})} | custom-call | flops 150994944 | bytes 557056 | tf_op jit(solution)/shard_map/pallas_call | solution.py:328
  37.3 4.4 %collective-permute-done.8.outer_ref = bf16[128,2176]{1,0:T(8,128)(2,1)S(1)} collective-permute-done((bf16[128,2176]{1,0:T(8,128)(2,1)}, bf16[128,2176]{1,0:T(8,128)(2,1)S(1)}, u32[]{:S(2)}, u32[]{:S(2)}) %collective-permute-start.8) | collective-permute-done | bytes 557088 | tf_op jit(solution)/shard_map/ppermute | solution.py:431
  41.8 0.9 shard_map.106.refs_4_
  44.3 1.9 %collective-permute-done.18 = bf16[2,128,1024]{2,1,0:T(8,128)(2,1)S(1)} collective-permute-done((bf16[2,128,1024]{2,1,0:T(8,128)(2,1)S(1)}, bf16[2,128,1024]{2,1,0:T(8,128)(2,1)S(1)}, u32[]{:S(2)}, u32[]{:S(2)}) %collective-permute-start.18) | collective-permute-done | bytes 524320 | tf_op jit(solution)/shard_map/ppermute | solution.py:411
  46.7 1.3 %collective-permute-start.14 = (bf16[128,2176]{1,0:T(8,128)(2,1)S(1)}, bf16[128,2176]{1,0:T(8,128)(2,1)S(1)}, u32[]{:S(2)}, u32[]{:S(2)}) collective-permute-start(bf16[128,2176]{1,0:T(8,128)(2,1)S(1)} %collective-permute-done.5.inner_ref), channel_id=1, source_target_pairs={{8,0},{16,24},{9,1},{17,25},{10,2},{18,26},{11,3},{19,27},{12,4},{... | collective-permute-start | bytes 1671176 | tf_op jit(solution)/shard_map/ppermute | solution.py:431
  48.9 1.5 %collective-permute-start.20 = (bf16[128,1024]{1,0:T(8,128)(2,1)S(1)}, bf16[128,1024]{1,0:T(8,128)(2,1)S(1)}, u32[]{:S(2)}, u32[]{:S(2)}) collective-permute-start(bf16[128,1024]{1,0:T(8,128)(2,1)S(1)} %get-tuple-element.222), channel_id=1, source_target_pairs={{0,4},{1,5},{2,6},{3,7},{4,0},{5,1},{6,2},{7,3},{8,12},{9,13},{10,... | collective-permute-start | bytes 786440 | tf_op jit(solution)/shard_map/ppermute | solution.py:411
  50.4 11.3 %shard_map.107 = (f32[3,256,512]{2,1,0:T(8,128)S(1)}, f32[3,256,512]{2,1,0:T(8,128)S(1)}, f32[3,128,1024]{2,1,0:T(8,128)S(1)}, bf16[1,128,1024]{2,1,0:T(8,128)(2,1)S(1)}, bf16[1,128,1024]{2,1,0:T(8,128)(2,1)S(1)}) custom-call(bf16[128,2176]{1,0:T(8,128)(2,1)S(1)} %collective-permute-done.6.refs_0_, ...), custom_call_target="tpu_custom_call", output_to_operand_aliasing={{0}: (9, {}), {1}: (10, {}), {2}: (11, {})} | custom-call | flops 150994944 | bytes 557056 | tf_op jit(solution)/shard_map/pallas_call | solution.py:328
  61.7 4.3 %collective-permute-done.14.outer_ref = bf16[128,2176]{1,0:T(8,128)(2,1)S(1)} collective-permute-done((bf16[128,2176]{1,0:T(8,128)(2,1)S(1)}, bf16[128,2176]{1,0:T(8,128)(2,1)S(1)}, u32[]{:S(2)}, u32[]{:S(2)}) %collective-permute-start.14) | collective-permute-done | bytes 557088 | tf_op jit(solution)/shard_map/ppermute | solution.py:431
  66.0 1.1 shard_map.108.refs_4_
  68.2 1.5 %collective-permute-start.21 = (bf16[128,2176]{1,0:T(8,128)(2,1)}, bf16[128,2176]{1,0:T(8,128)(2,1)S(1)}, u32[]{:S(2)}, u32[]{:S(2)}) collective-permute-start(bf16[128,2176]{1,0:T(8,128)(2,1)} %shard_map.108.refs_4_), channel_id=1, source_target_pairs={{0,2},{1,3},{2,0},{3,1},{4,6},{5,7},{6,4},{7,5},{8,10},{9,11},{10,... | collective-permute-start | bytes 1671176 | tf_op jit(solution)/shard_map/ppermute | solution.py:411
  70.2 4.9 %collective-permute-start.32 = (bf16[128,2176]{1,0:T(8,128)(2,1)S(1)}, bf16[128,2176]{1,0:T(8,128)(2,1)S(1)}, u32[]{:S(2)}, u32[]{:S(2)}) collective-permute-start(bf16[128,2176]{1,0:T(8,128)(2,1)S(1)} %collective-permute-done.2.refs_2_), channel_id=1, source_target_pairs={{0,8},{8,0},{16,24},{24,16},{1,9},{9,1},{17,25},{25,17},{2,10},{10... | collective-permute-start | bytes 1671176 | tf_op jit(solution)/shard_map/ppermute | solution.py:411
  75.2 1.0 copy-done.1
  76.2 8.8 %shard_map.109 = (f32[3,256,512]{2,1,0:T(8,128)S(1)}, f32[3,256,512]{2,1,0:T(8,128)S(1)}, f32[3,128,1024]{2,1,0:T(8,128)S(1)}) custom-call(bf16[128,2176]{1,0:T(8,128)(2,1)S(1)} %collective-permute-done.12.refs_0_, bf16[128,2176]{1,0:T(8,128)(2,1)S(1)} %collective-permute-done.23.refs_1_, ...), custom_call_target="tpu_custom_call", output_to_operand_aliasing={{0}: (9, {}), {1}: (10, {}), {2}: (11, {})} | custom-call | flops 150994944 | bytes 557056 | tf_op jit(solution)/shard_map/pallas_call | solution.py:328
  85.6 1.7 %collective-permute-done.32.refs_4_ = bf16[128,2176]{1,0:T(8,128)(2,1)S(1)} collective-permute-done((bf16[128,2176]{1,0:T(8,128)(2,1)S(1)}, bf16[128,2176]{1,0:T(8,128)(2,1)S(1)}, u32[]{:S(2)}, u32[]{:S(2)}) %collective-permute-start.32) | collective-permute-done | bytes 557088 | tf_op jit(solution)/shard_map/ppermute | solution.py:411
  87.3 0.9 collective-permute-start.27
  88.3 1.1 collective-permute-start.28
  89.3 1.7 %collective-permute-start.29 = (bf16[128,2176]{1,0:T(8,128)(2,1)S(1)}, bf16[128,2176]{1,0:T(8,128)(2,1)S(1)}, u32[]{:S(2)}, u32[]{:S(2)}) collective-permute-start(bf16[128,2176]{1,0:T(8,128)(2,1)S(1)} %collective-permute-done.6.refs_0_), channel_id=1, source_target_pairs={{0,8},{8,0},{16,24},{24,16},{1,9},{9,1},{17,25},{25,17},{2,10},{10... | collective-permute-start | bytes 1671176 | tf_op jit(solution)/shard_map/ppermute | solution.py:411
  91.1 8.8 %shard_map.110 = (f32[3,256,512]{2,1,0:T(8,128)S(1)}, f32[3,256,512]{2,1,0:T(8,128)S(1)}, f32[3,128,1024]{2,1,0:T(8,128)S(1)}) custom-call(bf16[128,2176]{1,0:T(8,128)(2,1)S(1)} %collective-permute-done.21.refs_0_, bf16[128,2176]{1,0:T(8,128)(2,1)S(1)} %collective-permute-done.30.refs_1_, ...), custom_call_target="tpu_custom_call", output_to_operand_aliasing={{0}: (9, {}), {1}: (10, {}), {2}: (11, {})} | custom-call | flops 150994944 | bytes 557056 | tf_op jit(solution)/shard_map/pallas_call | solution.py:328
  99.9 2.5 %collective-permute-done.27.refs_4_ = bf16[128,2176]{1,0:T(8,128)(2,1)S(1)} collective-permute-done((bf16[128,2176]{1,0:T(8,128)(2,1)S(1)}, bf16[128,2176]{1,0:T(8,128)(2,1)S(1)}, u32[]{:S(2)}, u32[]{:S(2)}) %collective-permute-start.27) | collective-permute-done | bytes 557088 | tf_op jit(solution)/shard_map/ppermute | solution.py:411
  103.0 0.8 collective-permute-done.29.refs_0_
  104.3 1.5 %collective-permute-start.34 = (bf16[128,1024]{1,0:T(8,128)(2,1)S(1)}, bf16[128,1024]{1,0:T(8,128)(2,1)S(1)}, u32[]{:S(2)}, u32[]{:S(2)}) collective-permute-start(bf16[128,1024]{1,0:T(8,128)(2,1)S(1)} %bitcast.12), channel_id=1, source_target_pairs={{0,6},{1,7},{2,4},{3,5},{4,2},{5,3},{6,0},{7,1},{8,14},{9,15},{10,... | collective-permute-start | bytes 786440 | tf_op jit(solution)/shard_map/ppermute | solution.py:411
  107.4 9.2 %shard_map.111 = (bf16[3,256,512]{2,1,0:T(8,128)(2,1)}, bf16[3,256,512]{2,1,0:T(8,128)(2,1)}, bf16[3,128,1024]{2,1,0:T(8,128)(2,1)}) custom-call(bf16[128,2176]{1,0:T(8,128)(2,1)S(1)} %collective-permute-done.29.refs_0_, bf16[128,2176]{1,0:T(8,128)(2,1)S(1)} %collective-permute-done.36.refs_1_, bf16[128,2176]{1,0:T(8,128)(2,1)S(1)} %collective-permute-done.28.refs_2_, ...), custom_call_target="tpu_custom_call" | custom-call | flops 150994944 | bytes 557056 | tf_op jit(solution)/shard_map/pallas_call | solution.py:328
  116.6 0.9 fusion.3
  (66 shorter events, 11.3 us)
Async XLA Ops:
  2.6 11.3 %collective-permute-start = (bf16[128,2176]{1,0:T(8,128)(2,1)}, bf16[128,2176]{1,0:T(8,128)(2,1)S(1)}, u32[]{:S(2)}, u32[]{:S(2)}) collective-permute-start(bf16[128,2176]{1,0:T(8,128)(2,1)} %shard_map.102.refs_0_), channel_id=1, source_target_pairs={{0,1},{1,0},{2,3},{3,2},{4,5},{5,4},{6,7},{7,6},{8,9},{9,8},{10,11... | collective-permute-start | bytes 1671176 | tf_op jit(solution)/shard_map/ppermute | solution.py:411
  3.1 16.8 %collective-permute-start.1 = (bf16[128,2176]{1,0:T(8,128)(2,1)}, bf16[128,2176]{1,0:T(8,128)(2,1)S(1)}, u32[]{:S(2)}, u32[]{:S(2)}) collective-permute-start(bf16[128,2176]{1,0:T(8,128)(2,1)} %shard_map.102.refs_0_), channel_id=1, source_target_pairs={{0,2},{1,3},{2,0},{3,1},{4,6},{5,7},{6,4},{7,5},{8,10},{9,11},{10,... | collective-permute-start | bytes 1671176 | tf_op jit(solution)/shard_map/ppermute | solution.py:411
  5.6 15.0 %collective-permute-start.2 = (bf16[128,2176]{1,0:T(8,128)(2,1)}, bf16[128,2176]{1,0:T(8,128)(2,1)S(1)}, u32[]{:S(2)}, u32[]{:S(2)}) collective-permute-start(bf16[128,2176]{1,0:T(8,128)(2,1)} %shard_map.102.refs_0_), channel_id=1, source_target_pairs={{0,4},{1,5},{2,6},{3,7},{4,0},{5,1},{6,2},{7,3},{8,12},{9,13},{10,... | collective-permute-start | bytes 1671176 | tf_op jit(solution)/shard_map/ppermute | solution.py:411
  7.1 14.7 %collective-permute-start.3 = (bf16[128,2176]{1,0:T(8,128)(2,1)}, bf16[128,2176]{1,0:T(8,128)(2,1)S(1)}, u32[]{:S(2)}, u32[]{:S(2)}) collective-permute-start(bf16[128,2176]{1,0:T(8,128)(2,1)} %shard_map.102.refs_0_), channel_id=1, source_target_pairs={{0,8},{8,0},{16,24},{24,16},{1,9},{9,1},{17,25},{25,17},{2,10},{10... | collective-permute-start | bytes 1671176 | tf_op jit(solution)/shard_map/ppermute | solution.py:411
  8.7 13.1 %collective-permute-start.4 = (bf16[128,2176]{1,0:T(8,128)(2,1)}, bf16[128,2176]{1,0:T(8,128)(2,1)}, u32[]{:S(2)}, u32[]{:S(2)}) collective-permute-start(bf16[128,2176]{1,0:T(8,128)(2,1)} %shard_map.102.refs_0_), channel_id=1, source_target_pairs={{8,16},{16,8},{9,17},{17,9},{10,18},{18,10},{11,19},{19,11},{12,20... | collective-permute-start | bytes 1671176 | tf_op jit(solution)/shard_map/ppermute | solution.py:427
  21.8 3.1 %collective-permute-start.11 = (bf16[128,2176]{1,0:T(8,128)(2,1)S(1)}, bf16[128,2176]{1,0:T(8,128)(2,1)S(1)}, u32[]{:S(2)}, u32[]{:S(2)}) collective-permute-start(bf16[128,2176]{1,0:T(8,128)(2,1)S(1)} %collective-permute-done.3.refs_4_), channel_id=1, source_target_pairs={{0,1},{1,0},{2,3},{3,2},{4,5},{5,4},{6,7},{7,6},{8,9},{9,8},{10,11... | collective-permute-start | bytes 1671176 | tf_op jit(solution)/shard_map/ppermute | solution.py:411
  22.3 19.5 %collective-permute-start.8 = (bf16[128,2176]{1,0:T(8,128)(2,1)}, bf16[128,2176]{1,0:T(8,128)(2,1)S(1)}, u32[]{:S(2)}, u32[]{:S(2)}) collective-permute-start(bf16[128,2176]{1,0:T(8,128)(2,1)} %collective-permute-done.4.inner_ref), channel_id=1, source_target_pairs={{8,0},{16,24},{9,1},{17,25},{10,2},{18,26},{11,3},{19,27},{12,4},{... | collective-permute-start | bytes 1671176 | tf_op jit(solution)/shard_map/ppermute | solution.py:431
  23.6 19.1 %collective-permute-start.5 = (bf16[128,2176]{1,0:T(8,128)(2,1)S(1)}, bf16[128,2176]{1,0:T(8,128)(2,1)S(1)}, u32[]{:S(2)}, u32[]{:S(2)}) collective-permute-start(bf16[128,2176]{1,0:T(8,128)(2,1)S(1)} %collective-permute-done.3.refs_4_), channel_id=1, source_target_pairs={{8,16},{16,8},{9,17},{17,9},{10,18},{18,10},{11,19},{19,11},{12,20... | collective-permute-start | bytes 1671176 | tf_op jit(solution)/shard_map/ppermute | solution.py:427
  24.3 18.4 %collective-permute-start.6 = (bf16[128,2176]{1,0:T(8,128)(2,1)S(1)}, bf16[128,2176]{1,0:T(8,128)(2,1)S(1)}, u32[]{:S(2)}, u32[]{:S(2)}) collective-permute-start(bf16[128,2176]{1,0:T(8,128)(2,1)S(1)} %collective-permute-done.1.refs_0_), channel_id=1, source_target_pairs={{0,4},{1,5},{2,6},{3,7},{4,0},{5,1},{6,2},{7,3},{8,12},{9,13},{10,... | collective-permute-start | bytes 1671176 | tf_op jit(solution)/shard_map/ppermute | solution.py:411
  24.9 17.8 %collective-permute-start.7 = (bf16[128,2176]{1,0:T(8,128)(2,1)S(1)}, bf16[128,2176]{1,0:T(8,128)(2,1)S(1)}, u32[]{:S(2)}, u32[]{:S(2)}) collective-permute-start(bf16[128,2176]{1,0:T(8,128)(2,1)S(1)} %collective-permute-done.3.refs_4_), channel_id=1, source_target_pairs={{0,2},{1,3},{2,0},{3,1},{4,6},{5,7},{6,4},{7,5},{8,10},{9,11},{10,... | collective-permute-start | bytes 1671176 | tf_op jit(solution)/shard_map/ppermute | solution.py:411
  42.7 4.0 %collective-permute-start.15 = (bf16[128,2176]{1,0:T(8,128)(2,1)S(1)}, bf16[128,2176]{1,0:T(8,128)(2,1)S(1)}, u32[]{:S(2)}, u32[]{:S(2)}) collective-permute-start(bf16[128,2176]{1,0:T(8,128)(2,1)S(1)} %collective-permute-done.6.refs_0_), channel_id=1, source_target_pairs={{0,1},{1,0},{2,3},{3,2},{4,5},{5,4},{6,7},{7,6},{8,9},{9,8},{10,11... | collective-permute-start | bytes 1671176 | tf_op jit(solution)/shard_map/ppermute | solution.py:411
  42.8 3.4 %collective-permute-start.18 = (bf16[2,128,1024]{2,1,0:T(8,128)(2,1)S(1)}, bf16[2,128,1024]{2,1,0:T(8,128)(2,1)S(1)}, u32[]{:S(2)}, u32[]{:S(2)}) collective-permute-start(bf16[2,128,1024]{2,1,0:T(8,128)(2,1)S(1)} %get-tuple-element.153), channel_id=1, source_target_pairs={{0,1},{1,0},{2,3},{3,2},{4,5},{5,4},{6,7},{7,6},{8,9},{9,8},{10,11... | collective-permute-start | bytes 1572872 | tf_op jit(solution)/shard_map/ppermute | solution.py:411
  43.3 4.9 %collective-permute-start.16 = (bf16[128,2176]{1,0:T(8,128)(2,1)S(1)}, bf16[128,2176]{1,0:T(8,128)(2,1)S(1)}, u32[]{:S(2)}, u32[]{:S(2)}) collective-permute-start(bf16[128,2176]{1,0:T(8,128)(2,1)S(1)} %collective-permute-done.7.refs_2_), channel_id=1, source_target_pairs={{0,1},{1,0},{2,3},{3,2},{4,5},{5,4},{6,7},{7,6},{8,9},{9,8},{10,11... | collective-permute-start | bytes 1671176 | tf_op jit(solution)/shard_map/ppermute | solution.py:411
  43.4 4.9 %collective-permute-start.17 = (bf16[128,2176]{1,0:T(8,128)(2,1)}, bf16[128,2176]{1,0:T(8,128)(2,1)S(1)}, u32[]{:S(2)}, u32[]{:S(2)}) collective-permute-start(bf16[128,2176]{1,0:T(8,128)(2,1)} %shard_map.106.refs_4_), channel_id=1, source_target_pairs={{0,1},{1,0},{2,3},{3,2},{4,5},{5,4},{6,7},{7,6},{8,9},{9,8},{10,11... | collective-permute-start | bytes 1671176 | tf_op jit(solution)/shard_map/ppermute | solution.py:411
  43.8 23.3 %collective-permute-start.12 = (bf16[128,2176]{1,0:T(8,128)(2,1)}, bf16[128,2176]{1,0:T(8,128)(2,1)S(1)}, u32[]{:S(2)}, u32[]{:S(2)}) collective-permute-start(bf16[128,2176]{1,0:T(8,128)(2,1)} %shard_map.106.refs_4_), channel_id=1, source_target_pairs={{0,2},{1,3},{2,0},{3,1},{4,6},{5,7},{6,4},{7,5},{8,10},{9,11},{10,... | collective-permute-start | bytes 1671176 | tf_op jit(solution)/shard_map/ppermute | solution.py:411
  46.2 20.8 %collective-permute-start.13 = (bf16[128,2176]{1,0:T(8,128)(2,1)}, bf16[128,2176]{1,0:T(8,128)(2,1)S(1)}, u32[]{:S(2)}, u32[]{:S(2)}) collective-permute-start(bf16[128,2176]{1,0:T(8,128)(2,1)} %shard_map.106.refs_4_), channel_id=1, source_target_pairs={{0,4},{1,5},{2,6},{3,7},{4,0},{5,1},{6,2},{7,3},{8,12},{9,13},{10,... | collective-permute-start | bytes 1671176 | tf_op jit(solution)/shard_map/ppermute | solution.py:411
  46.7 19.2 %collective-permute-start.14 = (bf16[128,2176]{1,0:T(8,128)(2,1)S(1)}, bf16[128,2176]{1,0:T(8,128)(2,1)S(1)}, u32[]{:S(2)}, u32[]{:S(2)}) collective-permute-start(bf16[128,2176]{1,0:T(8,128)(2,1)S(1)} %collective-permute-done.5.inner_ref), channel_id=1, source_target_pairs={{8,0},{16,24},{9,1},{17,25},{10,2},{18,26},{11,3},{19,27},{12,4},{... | collective-permute-start | bytes 1671176 | tf_op jit(solution)/shard_map/ppermute | solution.py:431
  48.3 18.8 %collective-permute-start.19 = (bf16[128,1024]{1,0:T(8,128)(2,1)S(1)}, bf16[128,1024]{1,0:T(8,128)(2,1)S(1)}, u32[]{:S(2)}, u32[]{:S(2)}) collective-permute-start(bf16[128,1024]{1,0:T(8,128)(2,1)S(1)} %get-tuple-element.223), channel_id=1, source_target_pairs={{0,2},{1,3},{2,0},{3,1},{4,6},{5,7},{6,4},{7,5},{8,10},{9,11},{10,... | collective-permute-start | bytes 786440 | tf_op jit(solution)/shard_map/ppermute | solution.py:411
  48.9 18.2 %collective-permute-start.20 = (bf16[128,1024]{1,0:T(8,128)(2,1)S(1)}, bf16[128,1024]{1,0:T(8,128)(2,1)S(1)}, u32[]{:S(2)}, u32[]{:S(2)}) collective-permute-start(bf16[128,1024]{1,0:T(8,128)(2,1)S(1)} %get-tuple-element.222), channel_id=1, source_target_pairs={{0,4},{1,5},{2,6},{3,7},{4,0},{5,1},{6,2},{7,3},{8,12},{9,13},{10,... | collective-permute-start | bytes 786440 | tf_op jit(solution)/shard_map/ppermute | solution.py:411
  67.7 7.4 %collective-permute-start.24 = (bf16[128,2176]{1,0:T(8,128)(2,1)S(1)}, bf16[128,2176]{1,0:T(8,128)(2,1)S(1)}, u32[]{:S(2)}, u32[]{:S(2)}) collective-permute-start(bf16[128,2176]{1,0:T(8,128)(2,1)S(1)} %collective-permute-done.13.refs_2_), channel_id=1, source_target_pairs={{0,1},{1,0},{2,3},{3,2},{4,5},{5,4},{6,7},{7,6},{8,9},{9,8},{10,11... | collective-permute-start | bytes 1671176 | tf_op jit(solution)/shard_map/ppermute | solution.py:411
  67.8 7.4 %collective-permute-start.25 = (bf16[128,2176]{1,0:T(8,128)(2,1)}, bf16[128,2176]{1,0:T(8,128)(2,1)S(1)}, u32[]{:S(2)}, u32[]{:S(2)}) collective-permute-start(bf16[128,2176]{1,0:T(8,128)(2,1)} %shard_map.108.refs_4_), channel_id=1, source_target_pairs={{0,1},{1,0},{2,3},{3,2},{4,5},{5,4},{6,7},{7,6},{8,9},{9,8},{10,11... | collective-permute-start | bytes 1671176 | tf_op jit(solution)/shard_map/ppermute | solution.py:411
  68.2 16.8 %collective-permute-start.21 = (bf16[128,2176]{1,0:T(8,128)(2,1)}, bf16[128,2176]{1,0:T(8,128)(2,1)S(1)}, u32[]{:S(2)}, u32[]{:S(2)}) collective-permute-start(bf16[128,2176]{1,0:T(8,128)(2,1)} %shard_map.108.refs_4_), channel_id=1, source_target_pairs={{0,2},{1,3},{2,0},{3,1},{4,6},{5,7},{6,4},{7,5},{8,10},{9,11},{10,... | collective-permute-start | bytes 1671176 | tf_op jit(solution)/shard_map/ppermute | solution.py:411
  69.7 15.3 %collective-permute-start.22 = (bf16[128,2176]{1,0:T(8,128)(2,1)}, bf16[128,2176]{1,0:T(8,128)(2,1)S(1)}, u32[]{:S(2)}, u32[]{:S(2)}) collective-permute-start(bf16[128,2176]{1,0:T(8,128)(2,1)} %shard_map.108.refs_4_), channel_id=1, source_target_pairs={{0,4},{1,5},{2,6},{3,7},{4,0},{5,1},{6,2},{7,3},{8,12},{9,13},{10,... | collective-permute-start | bytes 1671176 | tf_op jit(solution)/shard_map/ppermute | solution.py:411
  70.2 17.1 %collective-permute-start.32 = (bf16[128,2176]{1,0:T(8,128)(2,1)S(1)}, bf16[128,2176]{1,0:T(8,128)(2,1)S(1)}, u32[]{:S(2)}, u32[]{:S(2)}) collective-permute-start(bf16[128,2176]{1,0:T(8,128)(2,1)S(1)} %collective-permute-done.2.refs_2_), channel_id=1, source_target_pairs={{0,8},{8,0},{16,24},{24,16},{1,9},{9,1},{17,25},{25,17},{2,10},{10... | collective-permute-start | bytes 1671176 | tf_op jit(solution)/shard_map/ppermute | solution.py:411
  85.0 4.3 %collective-permute-start.30 = (bf16[128,2176]{1,0:T(8,128)(2,1)S(1)}, bf16[128,2176]{1,0:T(8,128)(2,1)S(1)}, u32[]{:S(2)}, u32[]{:S(2)}) collective-permute-start(bf16[128,2176]{1,0:T(8,128)(2,1)S(1)} %collective-permute-done.21.refs_0_), channel_id=1, source_target_pairs={{0,1},{1,0},{2,3},{3,2},{4,5},{5,4},{6,7},{7,6},{8,9},{9,8},{10,11... | collective-permute-start | bytes 1671176 | tf_op jit(solution)/shard_map/ppermute | solution.py:411
  85.1 6.0 %collective-permute-start.31 = (bf16[128,2176]{1,0:T(8,128)(2,1)S(1)}, bf16[128,2176]{1,0:T(8,128)(2,1)S(1)}, u32[]{:S(2)}, u32[]{:S(2)}) collective-permute-start(bf16[128,2176]{1,0:T(8,128)(2,1)S(1)} %collective-permute-done.22.refs_2_), channel_id=1, source_target_pairs={{0,1},{1,0},{2,3},{3,2},{4,5},{5,4},{6,7},{7,6},{8,9},{9,8},{10,11... | collective-permute-start | bytes 1671176 | tf_op jit(solution)/shard_map/ppermute | solution.py:411
  87.3 3.8 %collective-permute-start.33 = (bf16[128,2176]{1,0:T(8,128)(2,1)S(1)}, bf16[128,2176]{1,0:T(8,128)(2,1)S(1)}, u32[]{:S(2)}, u32[]{:S(2)}) collective-permute-start(bf16[128,2176]{1,0:T(8,128)(2,1)S(1)} %collective-permute-done.32.refs_4_), channel_id=1, source_target_pairs={{0,1},{1,0},{2,3},{3,2},{4,5},{5,4},{6,7},{7,6},{8,9},{9,8},{10,11... | collective-permute-start | bytes 1671176 | tf_op jit(solution)/shard_map/ppermute | solution.py:411
  87.3 15.0 %collective-permute-start.27 = (bf16[128,2176]{1,0:T(8,128)(2,1)S(1)}, bf16[128,2176]{1,0:T(8,128)(2,1)S(1)}, u32[]{:S(2)}, u32[]{:S(2)}) collective-permute-start(bf16[128,2176]{1,0:T(8,128)(2,1)S(1)} %collective-permute-done.22.refs_2_), channel_id=1, source_target_pairs={{0,2},{1,3},{2,0},{3,1},{4,6},{5,7},{6,4},{7,5},{8,10},{9,11},{10,... | collective-permute-start | bytes 1671176 | tf_op jit(solution)/shard_map/ppermute | solution.py:411
  88.3 14.8 %collective-permute-start.28 = (bf16[128,2176]{1,0:T(8,128)(2,1)S(1)}, bf16[128,2176]{1,0:T(8,128)(2,1)S(1)}, u32[]{:S(2)}, u32[]{:S(2)}) collective-permute-start(bf16[128,2176]{1,0:T(8,128)(2,1)S(1)} %collective-permute-done.12.refs_0_), channel_id=1, source_target_pairs={{0,4},{1,5},{2,6},{3,7},{4,0},{5,1},{6,2},{7,3},{8,12},{9,13},{10,... | collective-permute-start | bytes 1671176 | tf_op jit(solution)/shard_map/ppermute | solution.py:411
  89.3 14.5 %collective-permute-start.29 = (bf16[128,2176]{1,0:T(8,128)(2,1)S(1)}, bf16[128,2176]{1,0:T(8,128)(2,1)S(1)}, u32[]{:S(2)}, u32[]{:S(2)}) collective-permute-start(bf16[128,2176]{1,0:T(8,128)(2,1)S(1)} %collective-permute-done.6.refs_0_), channel_id=1, source_target_pairs={{0,8},{8,0},{16,24},{24,16},{1,9},{9,1},{17,25},{25,17},{2,10},{10... | collective-permute-start | bytes 1671176 | tf_op jit(solution)/shard_map/ppermute | solution.py:411
  104.3 12.2 %collective-permute-start.34 = (bf16[128,1024]{1,0:T(8,128)(2,1)S(1)}, bf16[128,1024]{1,0:T(8,128)(2,1)S(1)}, u32[]{:S(2)}, u32[]{:S(2)}) collective-permute-start(bf16[128,1024]{1,0:T(8,128)(2,1)S(1)} %bitcast.12), channel_id=1, source_target_pairs={{0,6},{1,7},{2,4},{3,5},{4,2},{5,3},{6,0},{7,1},{8,14},{9,15},{10,... | collective-permute-start | bytes 786440 | tf_op jit(solution)/shard_map/ppermute | solution.py:411
  105.8 10.8 %collective-permute-start.35 = (bf16[128,1024]{1,0:T(8,128)(2,1)S(1)}, bf16[128,1024]{1,0:T(8,128)(2,1)S(1)}, u32[]{:S(2)}, u32[]{:S(2)}) collective-permute-start(bf16[128,1024]{1,0:T(8,128)(2,1)S(1)} %bitcast.11), channel_id=1, source_target_pairs={{0,1},{1,0},{2,3},{3,2},{4,5},{5,4},{6,7},{7,6},{8,9},{9,8},{10,11... | collective-permute-start | bytes 786440 | tf_op jit(solution)/shard_map/ppermute | solution.py:411
  (10 other events, 39.3 us)
